TPU v7x, 32 devices: a whole 2x2x4 slice. The times are simulated.
32 devices in a mesh: prow: 4 (over y, core), pcol: 8 (over z, x).
Axes of the slice: x: 2, y: 2, z: 4, core: 2. Of those that a mesh axis runs over, the one named last changes fastest.
Arguments:
- cross_cov: float32 [2, 512, 16384], P(None, 'prow', 'pcol'), may hold values from -6 to 6
- prev_rows: bfloat16 [2, 512, 16384], P(None, 'pcol', 'prow'), may hold values from -0.0625 to 0.0625
- prev_solved: bfloat16 [16384, 16384], P('prow', 'pcol'), may hold values from -6 to 6
- sub_block: float32 [512, 512], replicated, may hold values from -0.25 to 0.25
- inv_first: float32 [512, 512], replicated, as said below
- inv_second: float32 [512, 512], replicated, as said below
Outputs:
- solved: float32 [2, 512, 16384], P(None, 'prow', 'pcol')
Inputs may be any that keep to these rules, and one draw needn't show every extreme that they name: inv_first is lower triangular with a positive diagonal. inv_second is lower triangular with a positive diagonal.
All inputs are finite; a program needn't handle non-finite values.
Results may differ from a plain program's by a relative error of at most 0.0003.
Values may be sent and summed in bfloat16 or wider, within the bound.
No kernel may reach another device: no remote copies, remote signals or barrier semaphores. Data moves between devices by JAX's collectives and lax.ppermute only.
A program may use at most 128 MiB of HBM per device.

v0:
```python
import jax
import jax.numpy as jnp
from jax import lax
from jax.sharding import PartitionSpec as P


def mult(left, right):
    return jnp.dot(left, right, preferred_element_type=jnp.float32, precision=lax.Precision.HIGHEST)


def local(cross_cov, prev_rows, prev_solved, sub_block, inv_first, inv_second):
    terms = jnp.einsum(
        "kra,ac->krc",
        lax.all_gather(prev_rows, "pcol", axis=1, tiled=True),
        prev_solved,
        preferred_element_type=jnp.float32,
    )
    update = lax.psum_scatter(terms, "prow", scatter_dimension=1, tiled=True)
    first_part = cross_cov[0] - update[0]
    second_part = cross_cov[1] - update[1]
    local_rows = first_part.shape[0]
    offset = lax.axis_index("prow") * local_rows

    def own_rows(matrix):
        return lax.dynamic_slice_in_dim(matrix, offset, local_rows, 0)

    first_full, second_full = (
        lax.all_gather(first_part, "prow", axis=0, tiled=True),
        lax.all_gather(second_part, "prow", axis=0, tiled=True),
    )
    whole_first = mult(inv_first, first_full)
    whole_second = mult(inv_second, second_full - mult(sub_block, whole_first))
    solved_first = own_rows(whole_first)
    solved_second = own_rows(whole_second)
    return jnp.stack([solved_first, solved_second])


def solution(mesh):
    return jax.shard_map(
        local,
        mesh=mesh,
        in_specs=(
            P(None, "prow", "pcol"),
            P(None, "pcol", "prow"),
            P("prow", "pcol"),
            P(),
            P(),
            P(),
        ),
        out_specs=P(None, "prow", "pcol"),
        check_vma=False,
    )
```

profile of v0, /device:TPU:0, one launch (start us, length us, event | category | flops | bytes accessed | tf_op | source)
XLA Modules:
  0.0 329.5 jit_solution(14952545638319132880)
XLA Ops:
  6.5 0.0 copy-start
  6.5 0.0 all-gather.6.cloned.1.call-start
  6.5 0.7 all-gather.6.cloned.1.call-update
  7.3 0.0 reduce-scatter.2.cloned.1.call-start
  7.3 129.9 %all-gather.6.cloned.1.call-done = bf16[2,512,4096]{2,1,0:T(8,128)(2,1)} async-done(((bf16[2,64,4096]{2,1,0:T(8,128)(2,1)}), bf16[2,512,4096]{2,1,0:T(8,128)(2,1)}) %all-gather.6.cloned.1.call-update) | async-done | bytes 8388624 | tf_op jit(solution)/shard_map/all_gather | solution.py:14
  137.2 24.0 %fusion = f32[2,512,2048]{2,1,0:T(8,128)} fusion(bf16[2,512,4096]{2,1,0:T(8,128)(2,1)} %all-gather.6.cloned.1.call-done, bf16[4096,2048]{1,0:T(8,128)(2,1)} %param.8), kind=kOutput, calls=%fused_computation | convolution fusion | flops 17179869184 | bytes 33554432 | tf_op jit(solution)/shard_map/kra,ac->krc/dot_general | solution.py:12
  161.2 0.0 copy-start.2
  161.2 0.0 reduce-scatter.2.cloned.1.call-update
  161.2 0.0 all-gather.8.cloned.1.call-start
  161.3 70.1 %reduce-scatter.2.cloned.1.call-done = f32[2,128,2048]{2,1,0:T(8,128)} async-done(((f32[2,512,2048]{2,1,0:T(8,128)}), f32[2,128,2048]{2,1,0:T(8,128)}) %reduce-scatter.2.cloned.1.call-update) | async-done | bytes 2097168 | tf_op jit(solution)/shard_map/reduce_scatter | solution.py:18
  231.4 0.0 copy-done.2
  231.4 3.1 slice_subtract_fusion
  234.5 0.0 all-gather.8.cloned.1.call-update
  234.5 0.2 all-gather.10.cloned.1.call-start
  234.7 0.3 all-gather.10.cloned.1.call-update
  235.1 0.0 copy-start.4
  235.1 34.0 %all-gather.8.cloned.1.call-done = f32[1,512,2048]{2,1,0:T(8,128)} async-done(((f32[1,128,2048]{2,1,0:T(8,128)}), f32[1,512,2048]{2,1,0:T(8,128)}) %all-gather.8.cloned.1.call-update) | async-done | bytes 4194320 | tf_op jit(solution)/shard_map/all_gather | solution.py:28
  269.1 0.0 copy-done
  269.1 15.0 %fusion.4 = f32[2048,512]{1,0:T(8,128)S(1)} fusion(f32[512,512]{1,0:T(8,128)S(1)} %copy-done, f32[1,512,2048]{2,1,0:T(8,128)} %all-gather.8.cloned.1.call-done), kind=kOutput, calls=%fused_computation.5 | convolution fusion | flops 6442450944 | bytes 9437184 | tf_op jit(solution)/shard_map/dot_general | solution.py:8
  284.1 1.2 dynamic-slice_bitcast_fusion.1
  285.3 0.0 copy-done.4
  285.3 0.0 copy-start.3
  285.3 8.4 %fusion.6 = f32[2048,512]{0,1:T(8,128)} fusion(f32[2048,512]{1,0:T(8,128)S(1)} %fusion.4, f32[512,512]{1,0:T(8,128)S(1)} %copy-done.4), kind=kOutput, calls=%fused_computation.12 | convolution fusion | flops 6442450944 | bytes 9437184 | tf_op jit(solution)/shard_map/dot_general | solution.py:8
  293.7 11.4 %all-gather.10.cloned.1.call-done = f32[1,512,2048]{2,1,0:T(8,128)} async-done(((f32[1,128,2048]{2,1,0:T(8,128)}), f32[1,512,2048]{2,1,0:T(8,128)}) %all-gather.10.cloned.1.call-update) | async-done | bytes 4194320 | tf_op jit(solution)/shard_map/all_gather | solution.py:29
  305.1 0.0 copy-done.3
  305.1 0.0 copy-start.1
  305.1 15.7 %fusion.2 = f32[2048,512]{1,0:T(8,128)S(1)} fusion(f32[512,512]{1,0:T(8,128)S(1)} %copy-done.3, f32[2048,512]{0,1:T(8,128)} %fusion.6, f32[1,512,2048]{2,1,0:T(8,128)} %all-gather.10.cloned.1.call-done), kind=kOutput, calls=%fused_computation.3 | convolution fusion | flops 6443499520 | bytes 13631488 | tf_op jit(solution)/shard_map/dot_general | solution.py:8
  320.8 0.1 dynamic-slice_bitcast_fusion
  321.0 0.0 copy-done.1
  321.0 0.1 pad_maximum_fusion
  321.1 1.8 copy.7
Async XLA Ops:
  6.5 262.6 %copy-start = (f32[512,512]{1,0:T(8,128)S(1)}, f32[512,512]{1,0:T(8,128)}, u32[]{:S(2)}) copy-start(f32[512,512]{1,0:T(8,128)} %param.10) | copy-start | bytes 3145732
  6.5 130.7 %all-gather.6.cloned.1.call-start = ((), (), s32[]{:S(2)}) async-start(), calls=%async_computation.1 | async-start | bytes 9437184 | tf_op jit(solution)/shard_map/all_gather | solution.py:14
  7.3 224.1 %reduce-scatter.2.cloned.1.call-start = ((), (), s32[]{:S(2)}) async-start(), calls=%async_computation.2 | async-start | bytes 10485760 | tf_op jit(solution)/shard_map/reduce_scatter | solution.py:18
  161.2 70.1 %copy-start.2 = (f32[2,128,2048]{2,1,0:T(8,128)S(1)}, f32[2,128,2048]{2,1,0:T(8,128)}, u32[]{:S(2)}) copy-start(f32[2,128,2048]{2,1,0:T(8,128)} %param.6) | copy-start | bytes 6291460
  161.2 107.9 %all-gather.8.cloned.1.call-start = ((), (), s32[]{:S(2)}) async-start(), calls=%async_computation.3 | async-start | bytes 5242880 | tf_op jit(solution)/shard_map/all_gather | solution.py:28
  234.5 70.6 %all-gather.10.cloned.1.call-start = ((), (), s32[]{:S(2)}) async-start(), calls=%async_computation.4 | async-start | bytes 5242880 | tf_op jit(solution)/shard_map/all_gather | solution.py:29
  235.1 50.2 %copy-start.4 = (f32[512,512]{1,0:T(8,128)S(1)}, f32[512,512]{1,0:T(8,128)}, u32[]{:S(2)}) copy-start(f32[512,512]{1,0:T(8,128)} %param.9) | copy-start | bytes 3145732
  285.3 19.8 %copy-start.3 = (f32[512,512]{1,0:T(8,128)S(1)}, f32[512,512]{1,0:T(8,128)}, u32[]{:S(2)}) copy-start(f32[512,512]{1,0:T(8,128)} %param.11) | copy-start | bytes 3145732
  305.1 15.8 %copy-start.1 = (f32[1,128,2048]{1,2,0:T(8,128)S(1)}, f32[1,128,2048]{1,2,0:T(8,128)}, u32[]{:S(2)}) copy-start(f32[1,128,2048]{1,2,0:T(8,128)} %dynamic-slice_bitcast_fusion.1) | copy-start | bytes 3145732
Sparse Core Ops, SparseCore 0:
  9.5 127.5 all-gather.5
  161.4 69.9 reduce-scatter.1
  234.6 34.4 all-gather.7
  270.6 34.4 all-gather.9
where the time goes:
time: 330 us; the launch traced here: 329 us
  waiting for transfers between devices  246 us (75%)
  matrix products  63.1 us (19%)
  between operations  13.2 us (4%)
    all_gather x1, waiting for transfers between devices, local(): lax.all_gather(prev_rows, 'pcol', axis=1, tiled=True)  130 us
    reduce_scatter x1, waiting for transfers between devices, local(): update = lax.psum_scatter(terms, 'prow', scatter_dimension=1, tiled=True)  70.1 us
    dot_general x3, matrix products, mult(): jnp.dot(left, right, preferred_element_type=jnp.float32, precision=lax.Pr...  39 us
    all_gather x1, waiting for transfers between devices, local(): lax.all_gather(first_part, 'prow', axis=0, tiled=True)  34 us
    dot_general x1, matrix products, local(): jnp.einsum('kra,ac->krc', lax.all_gather(prev_rows, 'pcol', axis=1, tiled...  24 us
    all_gather x1, waiting for transfers between devices, local(): lax.all_gather(second_part, 'prow', axis=0, tiled=True)  11.4 us
  transfers between devices with their start and end apart: 4, of which 4 were waited for; matrix products, arithmetic and copies ran while one was open for 7% of the time, Pallas kernels for 0%

commit v1 on v0

v1 whole, which is shorter than its diff:
```python
import functools

import jax
import jax.numpy as jnp
from jax import lax
from jax.experimental import pallas as pl
from jax.experimental.pallas import tpu as pltpu
from jax.sharding import PartitionSpec as P

F32, BF16 = jnp.float32, jnp.bfloat16
COLS = 512
KERNEL_BYTES = 12 * 2**20
OCTAVES, LOWEST = 248.0, -124.0


def split(value):
    high = value.astype(BF16)
    return high, (value - high.astype(F32)).astype(BF16)


def dot(left, right):
    return jnp.dot(left, right, preferred_element_type=F32)


def products(starts_ref, piece_refs, rows_ref, solved_ref, columns):
    terms = dot(rows_ref[...], solved_ref[:, columns])
    top = 0
    for i, ref in enumerate(piece_refs):
        count = ref.shape[0]
        yield pl.ds(pl.multiple_of(starts_ref[i], 16), count), terms[top : top + count]
        top += count


def gather_rows(piece_refs, rows_ref):
    top = 0
    for ref in piece_refs:
        rows_ref[top : top + ref.shape[0]] = ref[...]
        top += ref.shape[0]


def chunks(ref, body):
    def step(j, carry):
        body(pl.ds(pl.multiple_of(j * COLS, COLS), COLS))
        return carry

    lax.fori_loop(0, ref.shape[1] // COLS, step, 0)


def early_kernel(starts_ref, *refs):
    *piece_refs, solved_ref, cov_ref, rhs_ref, rows_ref = refs
    n = len(piece_refs)
    gather_rows(piece_refs, rows_ref)

    def body(columns):
        rhs_ref[:, columns] = jnp.zeros((rhs_ref.shape[0], COLS), F32)
        rhs_ref[pl.ds(pl.multiple_of(starts_ref[n], 16), cov_ref.shape[0]), columns] = cov_ref[:, columns]
        for place, term in products(starts_ref, piece_refs, rows_ref, solved_ref, columns):
            rhs_ref[place, columns] = rhs_ref[place, columns] - term

    chunks(solved_ref, body)


def solve(pair_ref, high, low, top, count, end):
    size = high.shape[0]
    wide, fine = pair_ref[top : top + count, :end], pair_ref[size + top : size + top + count, :end]
    return dot(wide, high[:end]) + dot(wide, low[:end]) + dot(fine, high[:end])


def late_kernel(has_base, has_cross, devices, starts_ref, *refs):
    refs = list(refs)
    rows_ref, rhs_ref, out_ref = refs[-3:]
    n = len(refs) - 3 - 3 - 2 - has_base - 2 * has_cross
    piece_refs, refs = refs[:n], refs[n:-3]
    solved_ref, early_ref, pair_ref, *refs = refs
    keep_ref, send_ref = refs[-2:]
    size = early_ref.shape[0]
    block, count = size // 2, size // devices
    gather_rows(piece_refs, rows_ref)

    def body(columns):
        rhs_ref[...] = early_ref[:, columns]
        for place, term in products(starts_ref, piece_refs, rows_ref, solved_ref, columns):
            rhs_ref[place] = rhs_ref[place] - term
        high, low = split(rhs_ref[...])
        for top in (0, block):
            value = solve(pair_ref, high, low, top, block, top + block)
            if has_base:
                value = value + refs[0][top : top + block, columns]
            for at in range(0, block, count):
                place = pl.ds(pl.multiple_of(starts_ref[n + (top + at) // count], 16), count)
                out_ref[place] = value[at : at + count]
            if has_cross:
                refs[1][top : top + block, columns] = solve(refs[0], high, low, top, block, size)
        keep_ref[:, columns] = out_ref[:block]
        send_ref[:, columns] = out_ref[block:]

    chunks(solved_ref, body)


def call(kernel, starts, pieces, solved, full, outs, scratch, flops):
    depth, width = solved.shape
    rows = sum(piece.shape[0] for piece in pieces)
    vmem = pl.BlockSpec(memory_space=pltpu.VMEM)
    return pl.pallas_call(
        kernel,
        in_specs=[pl.BlockSpec(memory_space=pltpu.SMEM)] + [vmem] * (len(pieces) + 1 + len(full)),
        out_specs=[vmem] * len(outs),
        out_shape=[pltpu.VMEM((count, width), F32) for count in outs],
        scratch_shapes=[pltpu.VMEM((rows, depth), BF16)] + [pltpu.VMEM((count, COLS), F32) for count in scratch],
        compiler_params=pltpu.CompilerParams(vmem_limit_bytes=KERNEL_BYTES),
        cost_estimate=pl.CostEstimate(
            flops=2 * rows * depth * width + flops, bytes_accessed=2 * rows * depth, transcendentals=0
        ),
    )(starts, *pieces, solved, *full)


def hold_kernel(from_ref, to_ref, sems):
    copies = [
        pltpu.make_async_copy(from_ref.at[rows], to_ref.at[rows], sems.at[i])
        for i in range(sems.shape[0])
        for rows in [pl.ds(i * (from_ref.shape[0] // sems.shape[0]), from_ref.shape[0] // sems.shape[0])]
    ]
    for copy in copies:
        copy.start()
    for copy in copies:
        copy.wait()


def hold(array):
    return pl.pallas_call(
        hold_kernel,
        in_specs=[pl.BlockSpec(memory_space=pltpu.HBM)],
        out_specs=pl.BlockSpec(memory_space=pltpu.VMEM),
        out_shape=pltpu.VMEM(array.shape, array.dtype),
        scratch_shapes=[pltpu.SemaphoreType.DMA((4,))],
        compiler_params=pltpu.CompilerParams(vmem_limit_bytes=KERNEL_BYTES),
        cost_estimate=pl.CostEstimate(flops=0, bytes_accessed=2 * array.size, transcendentals=0),
    )(pltpu.with_memory_space_constraint(array, pltpu.HBM))


def pack_kernel(keep_ref, got_ref, own_ref, coded_ref):
    count = own_ref.shape[0]

    def body(columns):
        own_ref[:, columns] = keep_ref[:count, columns] + got_ref[:count, columns]
        value = keep_ref[count:, columns] + got_ref[count:, columns]
        size = jnp.abs(value)
        top = jnp.maximum(jnp.max(size, axis=0, keepdims=True) * 1.01, 1e-30).astype(BF16)
        level = jnp.minimum(size / top.astype(F32), 1.0) * OCTAVES + LOWEST
        coded = jnp.exp2(level)
        coded_ref[:count, columns] = jnp.where(value < 0, -coded, coded).astype(BF16)
        coded_ref[count:, columns] = jnp.broadcast_to(top, (coded_ref.shape[0] - count, COLS))

    chunks(keep_ref, body)


def pack(keep, got):
    width, count = keep.shape[1], keep.shape[0] // 2
    vmem = pl.BlockSpec(memory_space=pltpu.VMEM)
    return pl.pallas_call(
        pack_kernel,
        in_specs=[vmem] * 2,
        out_specs=[vmem] * 2,
        out_shape=[pltpu.VMEM((count, width), F32), pltpu.VMEM((count + 16, width), BF16)],
        compiler_params=pltpu.CompilerParams(vmem_limit_bytes=KERNEL_BYTES),
        cost_estimate=pl.CostEstimate(flops=10 * count * width, bytes_accessed=24 * count * width, transcendentals=count * width),
    )(keep, got)


def unpack_kernel(own0_ref, got0_ref, own1_ref, got1_ref, out_ref):
    cols = out_ref.shape[2]
    columns = pl.ds(pl.multiple_of(pl.program_id(0) * cols, cols), cols)
    for k, (own_ref, got_ref) in enumerate(((own0_ref, got0_ref), (own1_ref, got1_ref))):
        count = own_ref.shape[0]
        coded = got_ref[:count, columns].astype(F32)
        size = jnp.maximum(jnp.log2(jnp.abs(coded)) - LOWEST, 0.0) * (1.0 / OCTAVES)
        size = size * got_ref[count:, columns].astype(F32)[:1]
        out_ref[k] = own_ref[:, columns] + jnp.where(coded < 0, -size, size)


def unpack(own0, got0, own1, got1):
    count, width = own0.shape
    return pl.pallas_call(
        unpack_kernel,
        grid=(width // COLS,),
        in_specs=[pl.BlockSpec(memory_space=pltpu.VMEM)] * 4,
        out_specs=pl.BlockSpec((2, count, COLS), lambda j: (0, 0, j)),
        out_shape=jax.ShapeDtypeStruct((2, count, width), F32),
        compiler_params=pltpu.CompilerParams(vmem_limit_bytes=KERNEL_BYTES),
        cost_estimate=pl.CostEstimate(flops=20 * count * width, bytes_accessed=20 * count * width, transcendentals=2 * count * width),
    )(own0, got0, own1, got1)


def mult(left, right):
    return jnp.dot(left, right, preferred_element_type=F32, precision=lax.Precision.HIGHEST)


def general(cross_cov, prev_rows, prev_solved, sub_block, inv_first, inv_second):
    terms = jnp.einsum(
        "kra,ac->krc",
        lax.all_gather(prev_rows, "pcol", axis=1, tiled=True),
        prev_solved,
        preferred_element_type=F32,
    )
    update = lax.psum_scatter(terms, "prow", scatter_dimension=1, tiled=True)
    reduced = lax.all_gather(cross_cov - update, "prow", axis=1, tiled=True)
    first = mult(inv_first, reduced[0])
    second = mult(inv_second, reduced[1] - mult(sub_block, first))
    rows = cross_cov.shape[1]
    return lax.dynamic_slice_in_dim(jnp.stack([first, second]), lax.axis_index("prow") * rows, rows, 1)


RING = (0, 2, 4, 6, 7, 5, 3, 1)
N = len(RING)
AHEAD = [(RING[i], RING[(i + 1) % N]) for i in range(N)]
BACK = [(RING[(i + 1) % N], RING[i]) for i in range(N)]
DEVICES = 4
SWAP_CORE = [(p, p ^ 1) for p in range(DEVICES)]
SWAP_Y = [(p, p ^ 2) for p in range(DEVICES)]


def halves(matrix):
    high = lax.reduce_precision(matrix, 8, 7)
    return jnp.concatenate([high, matrix - high]).astype(BF16)


def after(value, *others):
    return lax.optimization_barrier((value, *others))[0]


def fast(cross_cov, prev_rows, prev_solved, sub_block, inv_first, inv_second):
    p, q = lax.axis_index("prow"), lax.axis_index("pcol")
    rows, block = cross_cov.shape[1], prev_rows.shape[1]
    half = block // 2
    spot = jnp.where(q % 2 == 0, q // 2, N - 1 - q // 2)

    def rows_of(steps, part=0):
        there = (spot + steps) % N
        return jnp.where(there < N // 2, 2 * there, 2 * (N - 1 - there) + 1) * block + part * half

    def ahead(x):
        return lax.ppermute(x, "pcol", AHEAD)

    def back(x):
        return lax.ppermute(x, "pcol", BACK)

    own_a, own_b = prev_rows[0], prev_rows[1]
    fa, ba, fb, bb = [own_a], [own_a], [own_b], [own_b]
    held = hold(prev_solved)
    for i in range(3):
        for f, b in ((fa, ba), (fb, bb)):
            f.append(ahead(after(f[-1], held) if i == 1 else f[-1]))
            b.append(back(b[-1]))
    for f, b in ((fa, ba), (fb, bb)):
        f.append(ahead(f[3][:half]))
        b.append(back(b[3][half:]))

    cross = -mult(inv_second, mult(sub_block, inv_first))

    slots = [((d % 2 != p % 2) * 2 + (d // 2 != p // 2)) * rows for d in range(DEVICES)]

    def starts(*values):
        return jnp.stack([jnp.asarray(v, jnp.int32) for v in values])

    own_cov = p * rows
    early_a = [own_a, fa[1], ba[1], fa[2], ba[2]]
    early_b = [own_b, fb[1], bb[1], fb[2], bb[2]]
    late_a = [fa[3], ba[3], fa[4], ba[4]]
    late_b = [fb[3], bb[3], fb[4], bb[4]]
    early_starts = starts(*[rows_of(s) for s in (0, -1, 1, -2, 2)], own_cov)
    late_starts = starts(rows_of(-3), rows_of(3), rows_of(4, 0), rows_of(4, 1), *slots)
    size = N * block

    solve_flops = 6 * size * size * cross_cov.shape[2]
    rhs_a, = call(early_kernel, early_starts, early_a, held, [cross_cov[0]], [size], [], 0)
    rhs_b, = call(early_kernel, early_starts, early_b, held, [cross_cov[1]], [size], [], 0)
    base, keep_a, send_a = call(
        functools.partial(late_kernel, 0, 1, DEVICES), late_starts, late_a, held,
        [rhs_a, halves(inv_first), halves(cross)], [size, size // 2, size // 2], [size, size], 2 * solve_flops)
    own0, coded = pack(keep_a, lax.ppermute(send_a, "prow", SWAP_CORE))
    got0 = lax.ppermute(coded, "prow", SWAP_Y)
    keep_b, send_b = call(
        functools.partial(late_kernel, 1, 0, DEVICES), late_starts, late_b, held,
        [rhs_b, halves(inv_second), base], [size // 2, size // 2], [size, size], solve_flops)
    own1, coded = pack(keep_b, lax.ppermute(send_b, "prow", SWAP_CORE))
    got1 = lax.ppermute(coded, "prow", SWAP_Y)
    return unpack(own0, got0, own1, got1)


def solution(mesh):
    sizes = dict(mesh.shape)
    return jax.shard_map(
        fast if (sizes["prow"], sizes["pcol"]) == (DEVICES, N) else general,
        mesh=mesh,
        in_specs=(
            P(None, "prow", "pcol"),
            P(None, "pcol", "prow"),
            P("prow", "pcol"),
            P(),
            P(),
            P(),
        ),
        out_specs=P(None, "prow", "pcol"),
        check_vma=False,
    )
```

time: 330 us -> 137 us (0.42)
  waiting for transfers between devices: 246 us -> 42.5 us
  matrix products: 63.1 us -> 3.8 us
  Pallas kernels: 0 us -> 45.2 us
  starting transfers between devices: 0.31 us -> 22.7 us
  local copies, waits for them, and re-layouts: 3.19 us -> 19.4 us
  between operations: 13.2 us -> 0.53 us
    all_gather x3 -> x0, waiting for transfers between devices: 175 us -> none  [the longest x1 130 us: local(): lax.all_gather(prev_rows, 'pcol', axis=1, tiled=True)]
    reduce_scatter x1 -> x0, waiting for transfers between devices: 70.1 us -> none  [local(): update = lax.psum_scatter(terms, 'prow', scatter_dimension=1, tiled=True)]
    dot_general x4 -> x2, matrix products: 63.1 us -> 3.8 us  [mult(): jnp.dot(left, right, preferred_element_type=F32, precision=lax.Precision....]
    pallas_call x0 -> x8, Pallas kernels: none -> 45.2 us  [the longest x4 35.8 us: call(): pl.pallas_call(kernel, in_specs=[pl.BlockSpec(memory_space=pltpu.SMEM)] +...]
    ppermute x0 -> x20, waiting for transfers between devices: none -> 42.5 us  [the longest x8 18.9 us: ahead(): return lax.ppermute(x, 'pcol', AHEAD)]
    ppermute x0 -> x20, starting transfers between devices: none -> 22.7 us  [the longest x8 17.7 us: ahead(): return lax.ppermute(x, 'pcol', AHEAD)]
    unnamed x10 -> x34, local copies, waits for them, and re-layouts: 0.02 us -> 15.8 us
  transfers between devices with their start and end apart: 4 -> 20, of which waited for: 4 -> 6; matrix products, arithmetic and copies ran while one was open for 7% -> 6% of each run, Pallas kernels for 0% -> 32%
where the time goes in v1:
time: 137 us; the launch traced here: 136 us
  Pallas kernels  45.2 us (33%)
  waiting for transfers between devices  42.5 us (31%)
  starting transfers between devices  22.7 us (17%)
  local copies, waits for them, and re-layouts  19.4 us (14%)
  matrix products  3.8 us (3%)
  other arithmetic  1.9 us (1%)
    pallas_call x4, Pallas kernels, call(): pl.pallas_call(kernel, in_specs=[pl.BlockSpec(memory_space=pltpu.SMEM)] +...  35.8 us
    ppermute x8, waiting for transfers between devices, ahead(): return lax.ppermute(x, 'pcol', AHEAD)  18.9 us
    ppermute x8, starting transfers between devices, ahead(): return lax.ppermute(x, 'pcol', AHEAD)  17.7 us
    unnamed x34, local copies, waits for them, and re-layouts  15.8 us
    ppermute x1, waiting for transfers between devices, fast(): got1 = lax.ppermute(coded, 'prow', SWAP_Y)  11.9 us
    ppermute x1, waiting for transfers between devices, fast(): got0 = lax.ppermute(coded, 'prow', SWAP_Y)  10.4 us
    pallas_call x1, Pallas kernels, hold(): pl.pallas_call(hold_kernel, in_specs=[pl.BlockSpec(memory_space=pltpu.HBM...  5.89 us
    dot_general x2, matrix products, mult(): jnp.dot(left, right, preferred_element_type=F32, precision=lax.Precision....  3.8 us
  transfers between devices with their start and end apart: 20, of which 6 were waited for; matrix products, arithmetic and copies ran while one was open for 6% of the time, Pallas kernels for 32%

profile of v1, /device:TPU:0, one launch (start us, length us, event | category | flops | bytes accessed | tf_op | source)
XLA Modules:
  0.0 136.1 jit_solution(2115158883201520968)
XLA Ops:
  0.0 1.4 %slice_bitcast_fusion.2 = (bf16[64,4096]{1,0:T(8,128)(2,1)S(1)}, bf16[64,4096]{1,0:T(8,128)(2,1)S(1)}) fusion(bf16[2,64,4096]{2,1,0:T(8,128)(2,1)} %param.7), kind=kLoop, calls=%fused_computation.16 | loop fusion | bytes 2097152 | tf_op jit(solution)/shard_map/squeeze | solution.py:247
  1.4 3.1 %collective-permute-start = (bf16[64,4096]{1,0:T(8,128)(2,1)S(1)}, bf16[64,4096]{1,0:T(8,128)(2,1)S(1)}, u32[]{:S(2)}, u32[]{:S(2)}) collective-permute-start(bf16[64,4096]{1,0:T(8,128)(2,1)S(1)} %get-tuple-element.32.refs_0_), channel_id=1, source_target_pairs={{0,2},{2,4},{4,6},{6,7},{7,5},{5,3},{3,1},{1,0},{8,10},{10,12},{12... | collective-permute-start | bytes 1572872 | tf_op jit(solution)/shard_map/ppermute | solution.py:242
  4.5 2.0 %collective-permute-start.10 = (bf16[64,4096]{1,0:T(8,128)(2,1)S(1)}, bf16[64,4096]{1,0:T(8,128)(2,1)}, u32[]{:S(2)}, u32[]{:S(2)}) collective-permute-start(bf16[64,4096]{1,0:T(8,128)(2,1)S(1)} %get-tuple-element.31.refs_0_), channel_id=1, source_target_pairs={{0,2},{2,4},{4,6},{6,7},{7,5},{5,3},{3,1},{1,0},{8,10},{10,12},{12... | collective-permute-start | bytes 1572872 | tf_op jit(solution)/shard_map/ppermute | solution.py:242
  6.5 5.9 %shard_map.64.refs_5_.refs_4_ = bf16[4096,2048]{1,0:T(8,128)(2,1)S(1)} custom-call(bf16[4096,2048]{1,0:T(8,128)(2,1)} %from_ref.1), custom_call_target="tpu_custom_call" | custom-call | bytes 16777216 | tf_op jit(solution)/shard_map/pallas_call | solution.py:130
  12.4 5.7 %copy-done.2 = bf16[4096,2048]{1,0:T(8,128)(2,1)} copy-done((bf16[4096,2048]{1,0:T(8,128)(2,1)}, bf16[4096,2048]{1,0:T(8,128)(2,1)S(1)}, u32[]{:S(2)}) %copy-start.2) | copy-done | bytes 16777240
  18.3 1.1 copy-done.14
  19.4 1.9 %fusion.4 = f32[512,512]{1,0:T(8,128)S(1)} fusion(f32[512,512]{1,0:T(8,128)S(1)} %copy-done, f32[512,512]{1,0:T(8,128)S(1)} %copy-done.14), kind=kOutput, calls=%fused_computation.18 | convolution fusion | flops 1610612736 | bytes 3145728 | tf_op jit(solution)/shard_map/dot_general | solution.py:195
  21.3 2.0 %reduce-precision_convert_fusion.1 = (bf16[512,512]{1,0:T(8,128)(2,1)S(1)}, bf16[512,512]{1,0:T(8,128)(2,1)S(1)}) fusion(f32[512,512]{1,0:T(8,128)S(1)} %fusion.4, f32[512,512]{1,0:T(8,128)S(1)} %copy-done.15), kind=kOutput, calls=%fused_computation.3 | convolution fusion | flops 1611923456 | bytes 3145728 | tf_op jit(solution)/shard_map/dot_general | solution.py:195
  23.3 2.1 %collective-permute-start.1 = (bf16[64,4096]{1,0:T(8,128)(2,1)S(1)}, bf16[64,4096]{1,0:T(8,128)(2,1)}, u32[]{:S(2)}, u32[]{:S(2)}) collective-permute-start(bf16[64,4096]{1,0:T(8,128)(2,1)S(1)} %collective-permute-done.refs_1_), channel_id=1, source_target_pairs={{0,2},{2,4},{4,6},{6,7},{7,5},{5,3},{3,1},{1,0},{8,10},{10,12},{12... | collective-permute-start | bytes 1572872 | tf_op jit(solution)/shard_map/ppermute | solution.py:242
  25.5 3.0 %collective-permute-done.10.refs_1_ = bf16[64,4096]{1,0:T(8,128)(2,1)} collective-permute-done((bf16[64,4096]{1,0:T(8,128)(2,1)S(1)}, bf16[64,4096]{1,0:T(8,128)(2,1)}, u32[]{:S(2)}, u32[]{:S(2)}) %collective-permute-start.10) | collective-permute-done | bytes 524320 | tf_op jit(solution)/shard_map/ppermute | solution.py:242
  28.5 2.1 %collective-permute-start.11 = (bf16[64,4096]{1,0:T(8,128)(2,1)}, bf16[64,4096]{1,0:T(8,128)(2,1)}, u32[]{:S(2)}, u32[]{:S(2)}) collective-permute-start(bf16[64,4096]{1,0:T(8,128)(2,1)} %collective-permute-done.10.refs_1_), channel_id=1, source_target_pairs={{0,2},{2,4},{4,6},{6,7},{7,5},{5,3},{3,1},{1,0},{8,10},{10,12},{12... | collective-permute-start | bytes 1572872 | tf_op jit(solution)/shard_map/ppermute | solution.py:242
  30.7 1.5 %pad_maximum_fusion = (bf16[1024,512]{1,0:T(8,128)(2,1)}, bf16[1024,512]{1,0:T(8,128)(2,1)}) fusion(bf16[512,512]{1,0:T(8,128)(2,1)S(1)} %get-tuple-element.36, bf16[512,512]{1,0:T(8,128)(2,1)S(1)} %get-tuple-element.35, bf16[512,512]{1,0:T(8,128)(2,1)S(1)} %get-tuple-element.34, bf16[512,512]{1,0:T(8,128)(2,1)S(1)} %get-tuple-element.33), kind=kLoop, calls=%fused_computation.11 | loop fusion | flops 4194304 | bytes 4194304 | tf_op jit(solution)/shard_map/concatenate | solution.py:224
  32.3 7.4 %collective-permute-done.1.refs_3_ = bf16[64,4096]{1,0:T(8,128)(2,1)} collective-permute-done((bf16[64,4096]{1,0:T(8,128)(2,1)S(1)}, bf16[64,4096]{1,0:T(8,128)(2,1)}, u32[]{:S(2)}, u32[]{:S(2)}) %collective-permute-start.1) | collective-permute-done | bytes 524320 | tf_op jit(solution)/shard_map/ppermute | solution.py:242
  39.7 2.1 %collective-permute-start.2 = (bf16[64,4096]{1,0:T(8,128)(2,1)}, bf16[64,4096]{1,0:T(8,128)(2,1)}, u32[]{:S(2)}, u32[]{:S(2)}) collective-permute-start(bf16[64,4096]{1,0:T(8,128)(2,1)} %collective-permute-done.1.refs_3_), channel_id=1, source_target_pairs={{0,2},{2,4},{4,6},{6,7},{7,5},{5,3},{3,1},{1,0},{8,10},{10,12},{12... | collective-permute-start | bytes 1572872 | tf_op jit(solution)/shard_map/ppermute | solution.py:242
  42.4 8.6 %collective-permute-done.11.refs_3_ = bf16[64,4096]{1,0:T(8,128)(2,1)} collective-permute-done((bf16[64,4096]{1,0:T(8,128)(2,1)}, bf16[64,4096]{1,0:T(8,128)(2,1)}, u32[]{:S(2)}, u32[]{:S(2)}) %collective-permute-start.11) | collective-permute-done | bytes 524320 | tf_op jit(solution)/shard_map/ppermute | solution.py:242
  51.0 2.1 %collective-permute-start.12 = (bf16[64,4096]{1,0:T(8,128)(2,1)}, bf16[64,4096]{1,0:T(8,128)(2,1)S(1)}, u32[]{:S(2)}, u32[]{:S(2)}) collective-permute-start(bf16[64,4096]{1,0:T(8,128)(2,1)} %collective-permute-done.11.refs_3_), channel_id=1, source_target_pairs={{0,2},{2,4},{4,6},{6,7},{7,5},{5,3},{3,1},{1,0},{8,10},{10,12},{12... | collective-permute-start | bytes 1572872 | tf_op jit(solution)/shard_map/ppermute | solution.py:242
  53.1 5.8 %copy-done.3 = bf16[4096,2048]{1,0:T(8,128)(2,1)S(1)} copy-done((bf16[4096,2048]{1,0:T(8,128)(2,1)S(1)}, bf16[4096,2048]{1,0:T(8,128)(2,1)}, u32[]{:S(2)}) %copy-start.3) | copy-done | bytes 16777240
  58.9 1.0 copy-done.7
  60.0 1.0 copy-done.11
  61.0 1.0 copy-done.13
  62.0 7.6 %shard_map.65.refs_5_ = f32[512,2048]{1,0:T(8,128)S(1)} custom-call(s32[6]{0:T(128)S(1)} %stack.63.starts_ref, bf16[64,4096]{1,0:T(8,128)(2,1)S(1)} %copy-done.7, bf16[64,4096]{1,0:T(8,128)(2,1)S(1)} %copy-done.11, bf16[64,4096]{1,0:T(8,128)(2,1)S(1)} %copy-done.13, bf16[64,4096]{1,0:T(8,128)(2,1)} %collective-permute-done.1.refs_3_, ...), custom_call_target="tpu_custom_call" | custom-call | flops 5368709120 | bytes 2621440 | tf_op jit(solution)/shard_map/pallas_call | solution.py:104
  70.6 2.1 %collective-permute-start.6 = (bf16[32,4096]{1,0:T(8,128)(2,1)S(1)}, bf16[32,4096]{1,0:T(8,128)(2,1)S(1)}, u32[]{:S(2)}, u32[]{:S(2)}) collective-permute-start(bf16[32,4096]{1,0:T(8,128)(2,1)S(1)} %slice.32), channel_id=1, source_target_pairs={{0,2},{2,4},{4,6},{6,7},{7,5},{5,3},{3,1},{1,0},{8,10},{10,12},{12... | collective-permute-start | bytes 786440 | tf_op jit(solution)/shard_map/ppermute | solution.py:242
  73.8 8.0 %shard_map.68.refs_5_ = f32[512,2048]{1,0:T(8,128)S(1)} custom-call(s32[6]{0:T(128)S(1)} %stack.63.starts_ref, bf16[64,4096]{1,0:T(8,128)(2,1)S(1)} %copy-done.5, bf16[64,4096]{1,0:T(8,128)(2,1)} %collective-permute-done.10.refs_1_, bf16[64,4096]{1,0:T(8,128)(2,1)} %collective-permute-done.13.refs_2_, bf16[64,4096]{1,0:T(8,128)(2,1)} %collective-permute-done.11.refs_3_, ...), custom_call_target="tpu_custom_call" | custom-call | flops 5368709120 | bytes 2621440 | tf_op jit(solution)/shard_map/pallas_call | solution.py:104
  81.8 2.0 %collective-permute-start.16 = (bf16[32,4096]{1,0:T(8,128)(2,1)S(1)}, bf16[32,4096]{1,0:T(8,128)(2,1)S(1)}, u32[]{:S(2)}, u32[]{:S(2)}) collective-permute-start(bf16[32,4096]{1,0:T(8,128)(2,1)S(1)} %slice.34), channel_id=1, source_target_pairs={{0,2},{2,4},{4,6},{6,7},{7,5},{5,3},{3,1},{1,0},{8,10},{10,12},{12... | collective-permute-start | bytes 786440 | tf_op jit(solution)/shard_map/ppermute | solution.py:242
  84.1 12.1 %shard_map.66 = (f32[512,2048]{1,0:T(8,128)S(1)}, f32[256,2048]{1,0:T(8,128)S(1)}, f32[256,2048]{1,0:T(8,128)S(1)}) custom-call(s32[8]{0:T(128)S(1)} %stack.56.starts_ref, bf16[64,4096]{1,0:T(8,128)(2,1)} %collective-permute-done.2.refs_0_, bf16[64,4096]{1,0:T(8,128)(2,1)} %collective-permute-done.5.refs_1_, ...), custom_call_target="tpu_custom_call" | custom-call | flops 9663676416 | bytes 1572864 | tf_op jit(solution)/shard_map/pallas_call | solution.py:104
  96.3 8.2 %shard_map.69 = (f32[256,2048]{1,0:T(8,128)S(1)}, f32[256,2048]{1,0:T(8,128)S(1)}) custom-call(s32[8]{0:T(128)S(1)} %stack.56.starts_ref, bf16[64,4096]{1,0:T(8,128)(2,1)S(1)} %collective-permute-done.12.refs_0_, bf16[64,4096]{1,0:T(8,128)(2,1)S(1)} %collective-permute-done.15.refs_1_, bf16[32,4096]{1,0:T(8,128)(2,1)S(1)} %collective-permute-done.16.refs_2_, ...), custom_call_target="tpu_custom_call" | custom-call | flops 6442450944 | bytes 1572864 | tf_op jit(solution)/shard_map/pallas_call | solution.py:104
  105.7 2.0 %collective-permute-start.9 = (bf16[144,2048]{1,0:T(8,128)(2,1)S(1)}, bf16[144,2048]{1,0:T(8,128)(2,1)S(1)}, u32[]{:S(2)}, u32[]{:S(2)}) collective-permute-start(bf16[144,2048]{1,0:T(8,128)(2,1)S(1)} %get-tuple-element.20), channel_id=1, source_target_pairs={{0,16},{8,24},{16,0},{24,8},{1,17},{9,25},{17,1},{25,9},{2,18},{10... | collective-permute-start | bytes 1769480 | tf_op jit(solution)/shard_map/ppermute | solution.py:281
  107.7 1.1 collective-permute-done.18.got_ref
  109.5 2.0 %collective-permute-start.19 = (bf16[144,2048]{1,0:T(8,128)(2,1)S(1)}, bf16[144,2048]{1,0:T(8,128)(2,1)S(1)}, u32[]{:S(2)}, u32[]{:S(2)}) collective-permute-start(bf16[144,2048]{1,0:T(8,128)(2,1)S(1)} %get-tuple-element.26), channel_id=1, source_target_pairs={{0,16},{8,24},{16,0},{24,8},{1,17},{9,25},{17,1},{25,9},{2,18},{10... | collective-permute-start | bytes 1769480 | tf_op jit(solution)/shard_map/ppermute | solution.py:286
  111.5 10.4 %collective-permute-done.9.got0_ref = bf16[144,2048]{1,0:T(8,128)(2,1)S(1)} collective-permute-done((bf16[144,2048]{1,0:T(8,128)(2,1)S(1)}, bf16[144,2048]{1,0:T(8,128)(2,1)S(1)}, u32[]{:S(2)}, u32[]{:S(2)}) %collective-permute-start.9) | collective-permute-done | bytes 589856 | tf_op jit(solution)/shard_map/ppermute | solution.py:281
  121.9 11.9 %collective-permute-done.19.got1_ref = bf16[144,2048]{1,0:T(8,128)(2,1)S(1)} collective-permute-done((bf16[144,2048]{1,0:T(8,128)(2,1)S(1)}, bf16[144,2048]{1,0:T(8,128)(2,1)S(1)}, u32[]{:S(2)}, u32[]{:S(2)}) %collective-permute-start.19) | collective-permute-done | bytes 589856 | tf_op jit(solution)/shard_map/ppermute | solution.py:286
  133.9 2.2 %shard_map.71 = f32[2,128,2048]{2,1,0:T(8,128)} custom-call(f32[128,2048]{1,0:T(8,128)S(1)} %get-tuple-element.19.own0_ref, bf16[144,2048]{1,0:T(8,128)(2,1)S(1)} %collective-permute-done.9.got0_ref, f32[128,2048]{1,0:T(8,128)S(1)} %get-tuple-element.25.own1_ref, bf16[144,2048]{1,0:T(8,128)(2,1)S(1)} %collective-permute-done.19.got1_ref), custom_call_target="tpu_custom_call" | custom-call | flops 5242880 | bytes 5242880 | tf_op jit(solution)/shard_map/pallas_call | solution.py:183
  (64 shorter events, 5.2 us)
Async XLA Ops:
  0.0 18.3 %copy-start = (f32[512,512]{1,0:T(8,128)S(1)}, f32[512,512]{1,0:T(8,128)}, u32[]{:S(2)}) copy-start(f32[512,512]{1,0:T(8,128)} %param.9) | copy-start | bytes 3145732
  1.4 11.0 %copy-start.4 = (bf16[64,4096]{1,0:T(8,128)(2,1)}, bf16[64,4096]{1,0:T(8,128)(2,1)S(1)}, u32[]{:S(2)}) copy-start(bf16[64,4096]{1,0:T(8,128)(2,1)S(1)} %get-tuple-element.31.refs_0_) | copy-start | bytes 1572868
  1.4 11.0 %copy-start.6 = (bf16[64,4096]{1,0:T(8,128)(2,1)}, bf16[64,4096]{1,0:T(8,128)(2,1)S(1)}, u32[]{:S(2)}) copy-start(bf16[64,4096]{1,0:T(8,128)(2,1)S(1)} %get-tuple-element.32.refs_0_) | copy-start | bytes 1572868
  1.4 21.8 %collective-permute-start = (bf16[64,4096]{1,0:T(8,128)(2,1)S(1)}, bf16[64,4096]{1,0:T(8,128)(2,1)S(1)}, u32[]{:S(2)}, u32[]{:S(2)}) collective-permute-start(bf16[64,4096]{1,0:T(8,128)(2,1)S(1)} %get-tuple-element.32.refs_0_), channel_id=1, source_target_pairs={{0,2},{2,4},{4,6},{6,7},{7,5},{5,3},{3,1},{1,0},{8,10},{10,12},{12... | collective-permute-start | bytes 1572872 | tf_op jit(solution)/shard_map/ppermute | solution.py:242
  4.5 20.9 %collective-permute-start.3 = (bf16[64,4096]{1,0:T(8,128)(2,1)S(1)}, bf16[64,4096]{1,0:T(8,128)(2,1)S(1)}, u32[]{:S(2)}, u32[]{:S(2)}) collective-permute-start(bf16[64,4096]{1,0:T(8,128)(2,1)S(1)} %get-tuple-element.32.refs_0_), channel_id=1, source_target_pairs={{2,0},{4,2},{6,4},{7,6},{5,7},{3,5},{1,3},{0,1},{10,8},{12,10},{14... | collective-permute-start | bytes 1572872 | tf_op jit(solution)/shard_map/ppermute | solution.py:245
  4.5 13.7 %copy-start.16 = (f32[2,128,2048]{2,1,0:T(8,128)S(1)}, f32[2,128,2048]{2,1,0:T(8,128)}, u32[]{:S(2)}) copy-start(f32[2,128,2048]{2,1,0:T(8,128)} %param.6) | copy-start | bytes 6291460
  4.5 24.0 %collective-permute-start.10 = (bf16[64,4096]{1,0:T(8,128)(2,1)S(1)}, bf16[64,4096]{1,0:T(8,128)(2,1)}, u32[]{:S(2)}, u32[]{:S(2)}) collective-permute-start(bf16[64,4096]{1,0:T(8,128)(2,1)S(1)} %get-tuple-element.31.refs_0_), channel_id=1, source_target_pairs={{0,2},{2,4},{4,6},{6,7},{7,5},{5,3},{3,1},{1,0},{8,10},{10,12},{12... | collective-permute-start | bytes 1572872 | tf_op jit(solution)/shard_map/ppermute | solution.py:242
  6.5 24.2 %collective-permute-start.13 = (bf16[64,4096]{1,0:T(8,128)(2,1)S(1)}, bf16[64,4096]{1,0:T(8,128)(2,1)}, u32[]{:S(2)}, u32[]{:S(2)}) collective-permute-start(bf16[64,4096]{1,0:T(8,128)(2,1)S(1)} %get-tuple-element.31.refs_0_), channel_id=1, source_target_pairs={{2,0},{4,2},{6,4},{7,6},{5,7},{3,5},{1,3},{0,1},{10,8},{12,10},{14... | collective-permute-start | bytes 1572872 | tf_op jit(solution)/shard_map/ppermute | solution.py:245
  12.4 5.8 %copy-start.2 = (bf16[4096,2048]{1,0:T(8,128)(2,1)}, bf16[4096,2048]{1,0:T(8,128)(2,1)S(1)}, u32[]{:S(2)}) copy-start(bf16[4096,2048]{1,0:T(8,128)(2,1)S(1)} %shard_map.64.refs_5_.refs_4_) | copy-start | bytes 50331652
  23.3 8.9 %copy-start.10 = (bf16[64,4096]{1,0:T(8,128)(2,1)}, bf16[64,4096]{1,0:T(8,128)(2,1)S(1)}, u32[]{:S(2)}) copy-start(bf16[64,4096]{1,0:T(8,128)(2,1)S(1)} %collective-permute-done.refs_1_) | copy-start | bytes 1572868
  23.3 16.5 %collective-permute-start.1 = (bf16[64,4096]{1,0:T(8,128)(2,1)S(1)}, bf16[64,4096]{1,0:T(8,128)(2,1)}, u32[]{:S(2)}, u32[]{:S(2)}) collective-permute-start(bf16[64,4096]{1,0:T(8,128)(2,1)S(1)} %collective-permute-done.refs_1_), channel_id=1, source_target_pairs={{0,2},{2,4},{4,6},{6,7},{7,5},{5,3},{3,1},{1,0},{8,10},{10,12},{12... | collective-permute-start | bytes 1572872 | tf_op jit(solution)/shard_map/ppermute | solution.py:242
  25.3 6.8 %copy-start.12 = (bf16[64,4096]{1,0:T(8,128)(2,1)}, bf16[64,4096]{1,0:T(8,128)(2,1)S(1)}, u32[]{:S(2)}) copy-start(bf16[64,4096]{1,0:T(8,128)(2,1)S(1)} %collective-permute-done.3.refs_2_) | copy-start | bytes 1572868
  25.3 16.6 %collective-permute-start.4 = (bf16[64,4096]{1,0:T(8,128)(2,1)S(1)}, bf16[64,4096]{1,0:T(8,128)(2,1)}, u32[]{:S(2)}, u32[]{:S(2)}) collective-permute-start(bf16[64,4096]{1,0:T(8,128)(2,1)S(1)} %collective-permute-done.3.refs_2_), channel_id=1, source_target_pairs={{2,0},{4,2},{6,4},{7,6},{5,7},{3,5},{1,3},{0,1},{10,8},{12,10},{14... | collective-permute-start | bytes 1572872 | tf_op jit(solution)/shard_map/ppermute | solution.py:245
  28.5 22.5 %collective-permute-start.11 = (bf16[64,4096]{1,0:T(8,128)(2,1)}, bf16[64,4096]{1,0:T(8,128)(2,1)}, u32[]{:S(2)}, u32[]{:S(2)}) collective-permute-start(bf16[64,4096]{1,0:T(8,128)(2,1)} %collective-permute-done.10.refs_1_), channel_id=1, source_target_pairs={{0,2},{2,4},{4,6},{6,7},{7,5},{5,3},{3,1},{1,0},{8,10},{10,12},{12... | collective-permute-start | bytes 1572872 | tf_op jit(solution)/shard_map/ppermute | solution.py:242
  30.7 22.5 %collective-permute-start.14 = (bf16[64,4096]{1,0:T(8,128)(2,1)}, bf16[64,4096]{1,0:T(8,128)(2,1)}, u32[]{:S(2)}, u32[]{:S(2)}) collective-permute-start(bf16[64,4096]{1,0:T(8,128)(2,1)} %collective-permute-done.13.refs_2_), channel_id=1, source_target_pairs={{2,0},{4,2},{6,4},{7,6},{5,7},{3,5},{1,3},{0,1},{10,8},{12,10},{14... | collective-permute-start | bytes 1572872 | tf_op jit(solution)/shard_map/ppermute | solution.py:245
  39.7 29.9 %collective-permute-start.2 = (bf16[64,4096]{1,0:T(8,128)(2,1)}, bf16[64,4096]{1,0:T(8,128)(2,1)}, u32[]{:S(2)}, u32[]{:S(2)}) collective-permute-start(bf16[64,4096]{1,0:T(8,128)(2,1)} %collective-permute-done.1.refs_3_), channel_id=1, source_target_pairs={{0,2},{2,4},{4,6},{6,7},{7,5},{5,3},{3,1},{1,0},{8,10},{10,12},{12... | collective-permute-start | bytes 1572872 | tf_op jit(solution)/shard_map/ppermute | solution.py:242
  41.9 30.8 %collective-permute-start.5 = (bf16[64,4096]{1,0:T(8,128)(2,1)}, bf16[64,4096]{1,0:T(8,128)(2,1)}, u32[]{:S(2)}, u32[]{:S(2)}) collective-permute-start(bf16[64,4096]{1,0:T(8,128)(2,1)} %collective-permute-done.4.refs_4_), channel_id=1, source_target_pairs={{2,0},{4,2},{6,4},{7,6},{5,7},{3,5},{1,3},{0,1},{10,8},{12,10},{14... | collective-permute-start | bytes 1572872 | tf_op jit(solution)/shard_map/ppermute | solution.py:245
  51.0 30.8 %collective-permute-start.12 = (bf16[64,4096]{1,0:T(8,128)(2,1)}, bf16[64,4096]{1,0:T(8,128)(2,1)S(1)}, u32[]{:S(2)}, u32[]{:S(2)}) collective-permute-start(bf16[64,4096]{1,0:T(8,128)(2,1)} %collective-permute-done.11.refs_3_), channel_id=1, source_target_pairs={{0,2},{2,4},{4,6},{6,7},{7,5},{5,3},{3,1},{1,0},{8,10},{10,12},{12... | collective-permute-start | bytes 1572872 | tf_op jit(solution)/shard_map/ppermute | solution.py:242
  53.1 30.7 %collective-permute-start.15 = (bf16[64,4096]{1,0:T(8,128)(2,1)}, bf16[64,4096]{1,0:T(8,128)(2,1)S(1)}, u32[]{:S(2)}, u32[]{:S(2)}) collective-permute-start(bf16[64,4096]{1,0:T(8,128)(2,1)} %collective-permute-done.14.refs_4_), channel_id=1, source_target_pairs={{2,0},{4,2},{6,4},{7,6},{5,7},{3,5},{1,3},{0,1},{10,8},{12,10},{14... | collective-permute-start | bytes 1572872 | tf_op jit(solution)/shard_map/ppermute | solution.py:245
  53.1 5.8 %copy-start.3 = (bf16[4096,2048]{1,0:T(8,128)(2,1)S(1)}, bf16[4096,2048]{1,0:T(8,128)(2,1)}, u32[]{:S(2)}) copy-start(bf16[4096,2048]{1,0:T(8,128)(2,1)} %copy-done.2) | copy-start | bytes 50331652
  62.0 11.7 %copy-start.5 = (bf16[64,4096]{1,0:T(8,128)(2,1)S(1)}, bf16[64,4096]{1,0:T(8,128)(2,1)}, u32[]{:S(2)}) copy-start(bf16[64,4096]{1,0:T(8,128)(2,1)} %copy-done.4) | copy-start | bytes 1572868
  70.6 13.5 %collective-permute-start.6 = (bf16[32,4096]{1,0:T(8,128)(2,1)S(1)}, bf16[32,4096]{1,0:T(8,128)(2,1)S(1)}, u32[]{:S(2)}, u32[]{:S(2)}) collective-permute-start(bf16[32,4096]{1,0:T(8,128)(2,1)S(1)} %slice.32), channel_id=1, source_target_pairs={{0,2},{2,4},{4,6},{6,7},{7,5},{5,3},{3,1},{1,0},{8,10},{10,12},{12... | collective-permute-start | bytes 786440 | tf_op jit(solution)/shard_map/ppermute | solution.py:242
  73.7 10.5 %collective-permute-start.7 = (bf16[32,4096]{1,0:T(8,128)(2,1)S(1)}, bf16[32,4096]{1,0:T(8,128)(2,1)S(1)}, u32[]{:S(2)}, u32[]{:S(2)}) collective-permute-start(bf16[32,4096]{1,0:T(8,128)(2,1)S(1)} %slice.33), channel_id=1, source_target_pairs={{2,0},{4,2},{6,4},{7,6},{5,7},{3,5},{1,3},{0,1},{10,8},{12,10},{14... | collective-permute-start | bytes 786440 | tf_op jit(solution)/shard_map/ppermute | solution.py:245
  73.7 10.4 %copy-start.8 = (bf16[1024,512]{1,0:T(8,128)(2,1)S(1)}, bf16[1024,512]{1,0:T(8,128)(2,1)}, u32[]{:S(2)}) copy-start(bf16[1024,512]{1,0:T(8,128)(2,1)} %get-tuple-element.37.refs_6_) | copy-start | bytes 3145732
  73.7 10.4 %copy-start.9 = (bf16[1024,512]{1,0:T(8,128)(2,1)S(1)}, bf16[1024,512]{1,0:T(8,128)(2,1)}, u32[]{:S(2)}) copy-start(bf16[1024,512]{1,0:T(8,128)(2,1)} %get-tuple-element.38.refs_7_) | copy-start | bytes 3145732
  81.8 14.5 %collective-permute-start.16 = (bf16[32,4096]{1,0:T(8,128)(2,1)S(1)}, bf16[32,4096]{1,0:T(8,128)(2,1)S(1)}, u32[]{:S(2)}, u32[]{:S(2)}) collective-permute-start(bf16[32,4096]{1,0:T(8,128)(2,1)S(1)} %slice.34), channel_id=1, source_target_pairs={{0,2},{2,4},{4,6},{6,7},{7,5},{5,3},{3,1},{1,0},{8,10},{10,12},{12... | collective-permute-start | bytes 786440 | tf_op jit(solution)/shard_map/ppermute | solution.py:242
  83.8 12.5 %collective-permute-start.17 = (bf16[32,4096]{1,0:T(8,128)(2,1)S(1)}, bf16[32,4096]{1,0:T(8,128)(2,1)S(1)}, u32[]{:S(2)}, u32[]{:S(2)}) collective-permute-start(bf16[32,4096]{1,0:T(8,128)(2,1)S(1)} %slice.35), channel_id=1, source_target_pairs={{2,0},{4,2},{6,4},{7,6},{5,7},{3,5},{1,3},{0,1},{10,8},{12,10},{14... | collective-permute-start | bytes 786440 | tf_op jit(solution)/shard_map/ppermute | solution.py:245
  96.2 8.9 %collective-permute-start.8 = (f32[256,2048]{1,0:T(8,128)S(1)}, f32[256,2048]{1,0:T(8,128)S(1)}, u32[]{:S(2)}, u32[]{:S(2)}) collective-permute-start(f32[256,2048]{1,0:T(8,128)S(1)} %get-tuple-element.18), channel_id=1, source_target_pairs={{0,8},{8,0},{16,24},{24,16},{1,9},{9,1},{17,25},{25,17},{2,10},{10... | collective-permute-start | bytes 6291464 | tf_op jit(solution)/shard_map/ppermute | solution.py:280
  104.5 4.3 %collective-permute-start.18 = (f32[256,2048]{1,0:T(8,128)S(1)}, f32[256,2048]{1,0:T(8,128)S(1)}, u32[]{:S(2)}, u32[]{:S(2)}) collective-permute-start(f32[256,2048]{1,0:T(8,128)S(1)} %get-tuple-element.24), channel_id=1, source_target_pairs={{0,8},{8,0},{16,24},{24,16},{1,9},{9,1},{17,25},{25,17},{2,10},{10... | collective-permute-start | bytes 6291464 | tf_op jit(solution)/shard_map/ppermute | solution.py:285
  105.7 16.2 %collective-permute-start.9 = (bf16[144,2048]{1,0:T(8,128)(2,1)S(1)}, bf16[144,2048]{1,0:T(8,128)(2,1)S(1)}, u32[]{:S(2)}, u32[]{:S(2)}) collective-permute-start(bf16[144,2048]{1,0:T(8,128)(2,1)S(1)} %get-tuple-element.20), channel_id=1, source_target_pairs={{0,16},{8,24},{16,0},{24,8},{1,17},{9,25},{17,1},{25,9},{2,18},{10... | collective-permute-start | bytes 1769480 | tf_op jit(solution)/shard_map/ppermute | solution.py:281
  109.5 24.4 %collective-permute-start.19 = (bf16[144,2048]{1,0:T(8,128)(2,1)S(1)}, bf16[144,2048]{1,0:T(8,128)(2,1)S(1)}, u32[]{:S(2)}, u32[]{:S(2)}) collective-permute-start(bf16[144,2048]{1,0:T(8,128)(2,1)S(1)} %get-tuple-element.26), channel_id=1, source_target_pairs={{0,16},{8,24},{16,0},{24,8},{1,17},{9,25},{17,1},{25,9},{2,18},{10... | collective-permute-start | bytes 1769480 | tf_op jit(solution)/shard_map/ppermute | solution.py:286
  133.9 2.2 %copy-start.1 = (f32[512,512]{1,0:T(8,128)S(1)}, f32[512,512]{1,0:T(8,128)}, u32[]{:S(2)}) copy-start(f32[512,512]{1,0:T(8,128)} %param.9) | copy-start | bytes 3145732
  (5 other events, 6.2 us)

commit v2 on v0

v2 whole, which is shorter than its diff:
```python
import functools

import jax
import jax.numpy as jnp
from jax import lax
from jax.experimental import pallas as pl
from jax.experimental.pallas import tpu as pltpu
from jax.sharding import PartitionSpec as P

F32, BF16 = jnp.float32, jnp.bfloat16
COLS, LANES = 512, 128
PIECES, SPLITS = 8, 2
COST = pl.CostEstimate(flops=0, bytes_accessed=0, transcendentals=0)
KERNEL_BYTES = 12 * 2**20
OCTAVES, LOWEST = 248.0, -124.0


VMEM = pl.BlockSpec(memory_space=pltpu.VMEM)


def params():
    return pltpu.CompilerParams(vmem_limit_bytes=KERNEL_BYTES)


def split(value):
    high = value.astype(BF16)
    return high, (value - high.astype(F32)).astype(BF16)


def dot(left, right):
    return jnp.dot(left, right, preferred_element_type=F32)


def products(starts_ref, piece_refs, rows_ref, solved_ref, columns):
    terms = dot(rows_ref[...], solved_ref[:, columns])
    top = 0
    for i, ref in enumerate(piece_refs):
        count = ref.shape[0]
        yield pl.ds(pl.multiple_of(starts_ref[i], 16), count), terms[top : top + count]
        top += count


def gather_rows(piece_refs, rows_ref):
    top = 0
    for ref in piece_refs:
        rows_ref[top : top + ref.shape[0]] = ref[...]
        top += ref.shape[0]


def early_kernel(streams, starts_ref, *refs):
    refs = list(refs)
    n = len(refs) - 4 - 2 * streams
    piece_refs, refs = refs[:n], refs[n:]
    if streams:
        solved_ref, cov_ref, rhs_ref, held_ref, rows_ref, sems = refs
    else:
        held_ref, cov_ref, rhs_ref, rows_ref = refs
    steps = held_ref.shape[1] // COLS
    spans = [slice(j * COLS, (j + 1) * COLS) for j in range(steps)]
    if streams:
        copies = [pltpu.make_async_copy(solved_ref.at[:, c], held_ref.at[:, c], sems.at[j]) for j, c in enumerate(spans)]
        copies[0].start()
        copies[1].start()
    gather_rows(piece_refs, rows_ref)
    for j, columns in enumerate(spans):
        if streams:
            copies[j].wait()
            if j + 2 < steps:
                copies[j + 2].start()
        rhs_ref[:, columns] = jnp.zeros((rhs_ref.shape[0], COLS), F32)
        rhs_ref[pl.ds(pl.multiple_of(starts_ref[n], 16), cov_ref.shape[0]), columns] = cov_ref[:, columns]
        for place, term in products(starts_ref, piece_refs, rows_ref, held_ref, columns):
            rhs_ref[place, columns] = rhs_ref[place, columns] - term


def early(starts, pieces, solved, cov, size, streams):
    depth, width = solved.shape
    rows = sum(piece.shape[0] for piece in pieces)
    scratch = [pltpu.VMEM((rows, depth), BF16)]
    outs = [pltpu.VMEM((size, width), F32)]
    if streams:
        solved = pltpu.with_memory_space_constraint(solved, pltpu.HBM)
        outs.append(pltpu.VMEM((depth, width), BF16))
        scratch.append(pltpu.SemaphoreType.DMA((width // COLS,)))
    return pl.pallas_call(
        functools.partial(early_kernel, streams),
        in_specs=[pl.BlockSpec(memory_space=pltpu.SMEM)]
        + [VMEM] * len(pieces)
        + [pl.BlockSpec(memory_space=pltpu.HBM) if streams else VMEM, VMEM],
        out_specs=[VMEM] * len(outs),
        out_shape=outs,
        scratch_shapes=scratch,
        compiler_params=params(),
        cost_estimate=COST,
    )(starts, *pieces, solved, cov)


def solve(pair_ref, high, low, top, count, end):
    size = high.shape[0]
    wide, fine = pair_ref[top : top + count, :end], pair_ref[size + top : size + top + count, :end]
    return dot(wide, high[:end]) + dot(wide, low[:end]) + dot(fine, high[:end])


def late_kernel(has_base, first, devices, starts_ref, *refs):
    refs = list(refs)
    n = len(refs) - 8 - PIECES
    piece_refs, refs = refs[:n], refs[n:]
    held_ref, early_ref, pair_ref = refs[:3]
    rows_ref, rhs_ref, out_ref = refs[-3:]
    if has_base:
        base_ref, keep_ref, *send_refs = refs[3:-3]
    else:
        keep_ref, *send_refs, whole_ref = refs[3:-3]
    size = early_ref.shape[0]
    block, count = size // 2, size // devices
    gather_rows(piece_refs, rows_ref)
    for j in range(keep_ref.shape[1] // COLS):
        here = slice(j * COLS, (j + 1) * COLS)
        columns = slice(first + j * COLS, first + (j + 1) * COLS)
        rhs_ref[...] = early_ref[:, columns]
        for place, term in products(starts_ref, piece_refs, rows_ref, held_ref, columns):
            rhs_ref[place] = rhs_ref[place] - term
        high, low = split(rhs_ref[...])
        if not has_base:
            whole_ref[:size, here] = high
            whole_ref[size:, here] = low
        for top in (0, block):
            value = solve(pair_ref, high, low, top, block, top + block)
            if has_base:
                value = value + base_ref[top : top + block, columns]
            for at in range(0, block, count):
                place = pl.ds(pl.multiple_of(starts_ref[n + (top + at) // count], 16), count)
                out_ref[place] = value[at : at + count]
        keep_ref[:, here] = out_ref[:block]
        for i, send_ref in enumerate(send_refs):
            few = block // PIECES
            send_ref[:, here] = out_ref[block + i * few : block + (i + 1) * few]


def late(starts, pieces, held, rhs, pair, base, first, width):
    depth = held.shape[0]
    rows, size = sum(piece.shape[0] for piece in pieces), rhs.shape[0]
    given = [held, rhs, pair] + ([] if base is None else [base])
    outs = [pltpu.VMEM((size // 2, width), F32)] + [pltpu.VMEM((size // 2 // PIECES, width), F32)] * PIECES
    if base is None:
        outs.append(pltpu.VMEM((2 * size, width), BF16))
    return pl.pallas_call(
        functools.partial(late_kernel, base is not None, first, DEVICES),
        in_specs=[pl.BlockSpec(memory_space=pltpu.SMEM)] + [VMEM] * (len(pieces) + len(given)),
        out_specs=[VMEM] * len(outs),
        out_shape=outs,
        scratch_shapes=[pltpu.VMEM((rows, depth), BF16)] + [pltpu.VMEM((size, COLS), F32)] * 2,
        compiler_params=params(),
        cost_estimate=COST,
    )(starts, *pieces, *given)


def times_kernel(pair_ref, whole_ref, out_ref):
    size = out_ref.shape[0]
    block = size // 2
    for j in range(out_ref.shape[1] // COLS):
        columns = slice(j * COLS, (j + 1) * COLS)
        for top in (0, block):
            out_ref[top : top + block, columns] = solve(
                pair_ref, whole_ref[:size, columns], whole_ref[size:, columns], top, block, size
            )


def times(pair, whole):
    size, width = whole.shape[0] // 2, whole.shape[1]
    return pl.pallas_call(
        times_kernel,
        in_specs=[VMEM] * 2,
        out_specs=VMEM,
        out_shape=pltpu.VMEM((size, width), F32),
        compiler_params=params(),
        cost_estimate=COST,
    )(pair, whole)


def pack_kernel(keep_ref, *refs):
    *got_refs, own_ref, coded_ref = refs
    count = own_ref.shape[0]
    near, far = got_refs[: PIECES // 2], got_refs[PIECES // 2 :]
    few = near[0].shape[0]
    for i, ref in enumerate(near):
        own_ref[i * few : (i + 1) * few] = keep_ref[i * few : (i + 1) * few] + ref[...]
    blocks = own_ref.shape[1] // LANES
    tops = []
    for i in range(blocks):
        columns = slice(i * LANES, (i + 1) * LANES)
        value = keep_ref[count:, columns] + jnp.concatenate([ref[:, columns] for ref in far])
        size = jnp.abs(value)
        top = jnp.maximum(jnp.max(size, axis=0, keepdims=True) * 1.01, 1e-30).astype(BF16)
        level = jnp.minimum(size / top.astype(F32), 1.0) * OCTAVES + LOWEST
        coded = jnp.exp2(level)
        coded_ref[i * count : (i + 1) * count] = jnp.where(value < 0, -coded, coded).astype(BF16)
        tops.append(top)
    tops.append(jnp.ones((coded_ref.shape[0] - blocks * (count + 1), LANES), BF16))
    coded_ref[blocks * count :] = jnp.concatenate([top for top in tops if top.shape[0]])


def pack(keep, got):
    width, count = keep.shape[1], keep.shape[0] // 2
    blocks = width // LANES
    return pl.pallas_call(
        pack_kernel,
        in_specs=[VMEM] * (1 + len(got)),
        out_specs=[VMEM] * 2,
        out_shape=[pltpu.VMEM((count, width), F32), pltpu.VMEM((blocks * count + -(-blocks // 16) * 16, LANES), BF16)],
        compiler_params=params(),
        cost_estimate=COST,
    )(keep, *got)


def unpack_kernel(*refs):
    *refs, out_ref = refs
    count = out_ref.shape[1]
    at = 0
    for own_ref, got_ref in zip(refs[::2], refs[1::2]):
        blocks = own_ref.shape[1] // LANES
        tops = got_ref[blocks * count :].astype(F32) * (1.0 / OCTAVES)
        for i in range(blocks):
            coded = got_ref[i * count : (i + 1) * count].astype(F32)
            size = jnp.maximum(jnp.log2(jnp.abs(coded)) - LOWEST, 0.0) * tops[i : i + 1]
            value = own_ref[:, i * LANES : (i + 1) * LANES] + jnp.where(coded < 0, -size, size)
            out_ref[at // out_ref.shape[2], :, at % out_ref.shape[2] : at % out_ref.shape[2] + LANES] = value
            at += LANES


def unpack(sums):
    count, width = sums[0][0].shape[0], sum(own.shape[1] for own, _ in sums) // 2
    return pl.pallas_call(
        unpack_kernel,
        in_specs=[VMEM] * (2 * len(sums)),
        out_specs=VMEM,
        out_shape=jax.ShapeDtypeStruct((2, count, width), F32),
        compiler_params=params(),
        cost_estimate=COST,
    )(*[array for pair in sums for array in pair])


def mult(left, right):
    return jnp.dot(left, right, preferred_element_type=F32, precision=lax.Precision.HIGHEST)


def general(cross_cov, prev_rows, prev_solved, sub_block, inv_first, inv_second):
    terms = jnp.einsum(
        "kra,ac->krc",
        lax.all_gather(prev_rows, "pcol", axis=1, tiled=True),
        prev_solved,
        preferred_element_type=F32,
    )
    update = lax.psum_scatter(terms, "prow", scatter_dimension=1, tiled=True)
    reduced = lax.all_gather(cross_cov - update, "prow", axis=1, tiled=True)
    first = mult(inv_first, reduced[0])
    second = mult(inv_second, reduced[1] - mult(sub_block, first))
    rows = cross_cov.shape[1]
    return lax.dynamic_slice_in_dim(jnp.stack([first, second]), lax.axis_index("prow") * rows, rows, 1)


RING = (0, 2, 4, 6, 7, 5, 3, 1)
N = len(RING)
AHEAD = [(RING[i], RING[(i + 1) % N]) for i in range(N)]
BACK = [(RING[(i + 1) % N], RING[i]) for i in range(N)]
DEVICES = 4
SWAP_CORE = [(p, p ^ 1) for p in range(DEVICES)]
SWAP_Y = [(p, p ^ 2) for p in range(DEVICES)]


def halves(matrix):
    high = lax.reduce_precision(matrix, 8, 7)
    return jnp.concatenate([high, matrix - high]).astype(BF16)


def after(value, *others):
    return lax.optimization_barrier((value, *others))[0]


def fast(cross_cov, prev_rows, prev_solved, sub_block, inv_first, inv_second):
    p, q = lax.axis_index("prow"), lax.axis_index("pcol")
    rows, block = cross_cov.shape[1], prev_rows.shape[1]
    half = block // 2
    spot = jnp.where(q % 2 == 0, q // 2, N - 1 - q // 2)

    def rows_of(steps, part=0):
        there = (spot + steps) % N
        return jnp.where(there < N // 2, 2 * there, 2 * (N - 1 - there) + 1) * block + part * half

    def starts(*values):
        return jnp.stack([jnp.asarray(v, jnp.int32) for v in values])

    size = N * block

    def ahead(x):
        return lax.ppermute(x, "pcol", AHEAD)

    def back(x):
        return lax.ppermute(x, "pcol", BACK)

    own_a, own_b = prev_rows[0], prev_rows[1]
    fa, ba, fb, bb = [own_a], [own_a], [own_b], [own_b]

    def step(flow, move, *others):
        flow.append(move(after(flow[-1], *others)))

    for f, b in ((fa, ba), (fb, bb), (fa, ba), (fb, bb), (fa, ba)):
        step(f, ahead)
        step(b, back)

    cross = -mult(inv_second, mult(sub_block, inv_first))

    slots = [((d % 2 != p % 2) * 2 + (d // 2 != p // 2)) * rows for d in range(DEVICES)]

    late_starts = starts(rows_of(-3), rows_of(3), rows_of(4, 0), rows_of(4, 1), *slots)
    matrices = [halves(inv_first), halves(cross), halves(inv_second)]
    early_starts = after(starts(*[rows_of(s) for s in (0, -1, 1, -2, 2)], p * rows), late_starts, *matrices)
    rhs_a, held = early(early_starts, [own_a, fa[1], ba[1], fa[2], ba[2]], prev_solved, cross_cov[0], size, True)
    step(fb, ahead, rhs_a)
    step(bb, back, rhs_a)
    fa.append(ahead(fa[3][:half]))
    ba.append(back(ba[3][half:]))
    rhs_b, = early(after(early_starts, fa[3], ba[3]), [own_b, fb[1], bb[1], fb[2], bb[2]], held, cross_cov[1], size, False)
    fb.append(ahead(after(fb[3], rhs_b)[:half]))
    bb.append(back(after(bb[3], rhs_b)[half:]))

    width = cross_cov.shape[2]

    def exchange(keep, sends, *others):
        return pack(after(keep, *others), [lax.ppermute(send, "prow", SWAP_CORE) for send in sends])

    keep, *sends, high_low = late(
        after(late_starts, rhs_b, fb[3], bb[3]), [fa[3], ba[3], fa[4], ba[4]], held, rhs_a, matrices[0], None, 0, width)
    sends = lax.optimization_barrier((*sends, fb[4], bb[4]))[:PIECES]
    base = times(matrices[1], high_low)
    own, coded = exchange(keep, sends, base)
    sums = [(own, lax.ppermute(coded, "prow", SWAP_Y))]
    ready = after(late_starts, coded)
    part = width // SPLITS
    for i in range(SPLITS):
        keep, *sends = late(ready, [fb[3], bb[3], fb[4], bb[4]], held, rhs_b, matrices[2], base, i * part, part)
        own, coded = exchange(keep, sends, *([sums[0][1]] if i == SPLITS - 1 else []))
        sums.append((own, lax.ppermute(coded, "prow", SWAP_Y)))
    return unpack(sums)


def solution(mesh):
    sizes = dict(mesh.shape)
    return jax.shard_map(
        fast if (sizes["prow"], sizes["pcol"]) == (DEVICES, N) else general,
        mesh=mesh,
        in_specs=(
            P(None, "prow", "pcol"),
            P(None, "pcol", "prow"),
            P("prow", "pcol"),
            P(),
            P(),
            P(),
        ),
        out_specs=P(None, "prow", "pcol"),
        check_vma=False,
    )
```

time: 330 us -> 128 us (0.39)
  waiting for transfers between devices: 246 us -> 45.3 us
  matrix products: 63.1 us -> 6.91 us
  Pallas kernels: 0 us -> 39.7 us
  starting transfers between devices: 0.31 us -> 27.6 us
  between operations: 13.2 us -> 0.27 us
    all_gather x3 -> x0, waiting for transfers between devices: 175 us -> none  [the longest x1 130 us: local(): lax.all_gather(prev_rows, 'pcol', axis=1, tiled=True)]
    reduce_scatter x1 -> x0, waiting for transfers between devices: 70.1 us -> none  [local(): update = lax.psum_scatter(terms, 'prow', scatter_dimension=1, tiled=True)]
    dot_general x4 -> x2, matrix products: 63.1 us -> 6.91 us  [mult(): jnp.dot(left, right, preferred_element_type=F32, precision=lax.Precision....]
    ppermute x0 -> x43, waiting for transfers between devices: none -> 45.3 us  [the longest x8 27.5 us: ahead(): return lax.ppermute(x, 'pcol', AHEAD)]
    pallas_call x0 -> x10, Pallas kernels: none -> 39.7 us  [the longest x3 16.5 us: late(): pl.pallas_call(functools.partial(late_kernel, base is not None, first, DE...]
    ppermute x0 -> x43, starting transfers between devices: none -> 27.6 us  [the longest x8 17.4 us: ahead(): return lax.ppermute(x, 'pcol', AHEAD)]
  transfers between devices with their start and end apart: 4 -> 43, of which waited for: 4 -> 14; matrix products, arithmetic and copies ran while one was open for 7% -> 10% of each run, Pallas kernels for 0% -> 29%
where the time goes in v2:
time: 128 us; the launch traced here: 127 us
  waiting for transfers between devices  45.3 us (35%)
  Pallas kernels  39.7 us (31%)
  starting transfers between devices  27.6 us (22%)
  matrix products  6.91 us (5%)
  other arithmetic  5.41 us (4%)
  local copies, waits for them, and re-layouts  2.11 us (2%)
    ppermute x8, waiting for transfers between devices, ahead(): return lax.ppermute(x, 'pcol', AHEAD)  27.5 us
    ppermute x8, starting transfers between devices, ahead(): return lax.ppermute(x, 'pcol', AHEAD)  17.4 us
    pallas_call x3, Pallas kernels, late(): pl.pallas_call(functools.partial(late_kernel, base is not None, first, DE...  16.5 us
    pallas_call x2, Pallas kernels, early(): pl.pallas_call(functools.partial(early_kernel, streams), in_specs=[pl.Blo...  16.5 us
    ppermute x2, waiting for transfers between devices, fast(): sums.append((own, lax.ppermute(coded, 'prow', SWAP_Y)))  11.7 us
    dot_general x2, matrix products, mult(): jnp.dot(left, right, preferred_element_type=F32, precision=lax.Precision....  6.91 us
    ppermute x24, starting transfers between devices, exchange(): lax.ppermute(send, 'prow', SWAP_CORE)  5.76 us
    ppermute x8, waiting for transfers between devices, back(): return lax.ppermute(x, 'pcol', BACK)  4.45 us
  transfers between devices with their start and end apart: 43, of which 14 were waited for; matrix products, arithmetic and copies ran while one was open for 10% of the time, Pallas kernels for 29%

profile of v2, /device:TPU:0, one launch (start us, length us, event | category | flops | bytes accessed | tf_op | source)
XLA Modules:
  0.0 127.3 jit_solution(13353886300745911302)
XLA Ops:
  0.0 1.4 %slice_bitcast_fusion.2 = (bf16[64,4096]{1,0:T(8,128)(2,1)S(1)}, bf16[64,4096]{1,0:T(8,128)(2,1)S(1)}) fusion(bf16[2,64,4096]{2,1,0:T(8,128)(2,1)} %param.7), kind=kLoop, calls=%fused_computation.16 | loop fusion | bytes 2097152 | tf_op jit(solution)/shard_map/squeeze | solution.py:301
  1.4 3.1 %collective-permute-start = (bf16[64,4096]{1,0:T(8,128)(2,1)S(1)}, bf16[64,4096]{1,0:T(8,128)(2,1)}, u32[]{:S(2)}, u32[]{:S(2)}) collective-permute-start(bf16[64,4096]{1,0:T(8,128)(2,1)S(1)} %get-tuple-element.116.refs_0_), channel_id=1, source_target_pairs={{0,2},{2,4},{4,6},{6,7},{7,5},{5,3},{3,1},{1,0},{8,10},{10,12},{12... | collective-permute-start | bytes 1572872 | tf_op jit(solution)/shard_map/ppermute | solution.py:296
  4.4 2.0 %collective-permute-start.6 = (bf16[64,4096]{1,0:T(8,128)(2,1)S(1)}, bf16[64,4096]{1,0:T(8,128)(2,1)S(1)}, u32[]{:S(2)}, u32[]{:S(2)}) collective-permute-start(bf16[64,4096]{1,0:T(8,128)(2,1)S(1)} %get-tuple-element.115.refs_0_), channel_id=1, source_target_pairs={{0,2},{2,4},{4,6},{6,7},{7,5},{5,3},{3,1},{1,0},{8,10},{10,12},{12... | collective-permute-start | bytes 1572872 | tf_op jit(solution)/shard_map/ppermute | solution.py:296
  6.5 2.4 %reduce-precision_convert_fusion.2 = (bf16[512,512]{1,0:T(8,128)(2,1)}, bf16[512,512]{1,0:T(8,128)(2,1)}) fusion(f32[512,512]{1,0:T(8,128)} %param.10), kind=kLoop, calls=%fused_computation.5 | loop fusion | flops 1048576 | bytes 2097152 | tf_op jit(solution)/shard_map/convert.4
  8.9 2.8 %fusion.4 = f32[512,512]{1,0:T(8,128)} fusion(f32[512,512]{1,0:T(8,128)S(1)} %copy-done, f32[512,512]{1,0:T(8,128)S(1)} %copy-done.3), kind=kOutput, calls=%fused_computation.18 | convolution fusion | flops 1610612736 | bytes 3145728 | tf_op jit(solution)/shard_map/dot_general | solution.py:244
  11.7 1.4 %pad_maximum_fusion.refs_6_ = bf16[1024,512]{1,0:T(8,128)(2,1)S(1)} fusion(bf16[512,512]{1,0:T(8,128)(2,1)} %get-tuple-element.122, bf16[512,512]{1,0:T(8,128)(2,1)} %get-tuple-element.121), kind=kLoop, calls=%fused_computation.11 | loop fusion | flops 2097152 | bytes 2097152 | tf_op jit(solution)/shard_map/concatenate | solution.py:273
  13.3 4.1 %reduce-precision_convert_fusion.1 = (bf16[512,512]{1,0:T(8,128)(2,1)}, bf16[512,512]{1,0:T(8,128)(2,1)}) fusion(f32[512,512]{1,0:T(8,128)S(1)} %copy-done.2, f32[512,512]{1,0:T(8,128)} %param.11), kind=kOutput, calls=%fused_computation.3 | convolution fusion | flops 1611923456 | bytes 3145728 | tf_op jit(solution)/shard_map/dot_general | solution.py:244
  17.6 1.4 %pad_maximum_fusion.1.pair_ref = bf16[1024,512]{1,0:T(8,128)(2,1)S(1)} fusion(bf16[512,512]{1,0:T(8,128)(2,1)} %get-tuple-element.120, bf16[512,512]{1,0:T(8,128)(2,1)} %get-tuple-element.119), kind=kLoop, calls=%fused_computation.12 | loop fusion | flops 2097152 | bytes 2097152 | tf_op jit(solution)/shard_map/concatenate | solution.py:273
  19.4 2.1 %collective-permute-start.1 = (bf16[64,4096]{1,0:T(8,128)(2,1)}, bf16[64,4096]{1,0:T(8,128)(2,1)S(1)}, u32[]{:S(2)}, u32[]{:S(2)}) collective-permute-start(bf16[64,4096]{1,0:T(8,128)(2,1)} %collective-permute-done.refs_1_), channel_id=1, source_target_pairs={{0,2},{2,4},{4,6},{6,7},{7,5},{5,3},{3,1},{1,0},{8,10},{10,12},{12... | collective-permute-start | bytes 1572872 | tf_op jit(solution)/shard_map/ppermute | solution.py:296
  21.4 6.9 %collective-permute-done.6.refs_1_ = bf16[64,4096]{1,0:T(8,128)(2,1)S(1)} collective-permute-done((bf16[64,4096]{1,0:T(8,128)(2,1)S(1)}, bf16[64,4096]{1,0:T(8,128)(2,1)S(1)}, u32[]{:S(2)}, u32[]{:S(2)}) %collective-permute-start.6) | collective-permute-done | bytes 524320 | tf_op jit(solution)/shard_map/ppermute | solution.py:296
  28.3 2.1 %collective-permute-start.8 = (bf16[64,4096]{1,0:T(8,128)(2,1)S(1)}, bf16[64,4096]{1,0:T(8,128)(2,1)S(1)}, u32[]{:S(2)}, u32[]{:S(2)}) collective-permute-start(bf16[64,4096]{1,0:T(8,128)(2,1)S(1)} %collective-permute-done.6.refs_1_), channel_id=1, source_target_pairs={{0,2},{2,4},{4,6},{6,7},{7,5},{5,3},{3,1},{1,0},{8,10},{10,12},{12... | collective-permute-start | bytes 1572872 | tf_op jit(solution)/shard_map/ppermute | solution.py:296
  30.7 8.9 %collective-permute-done.1.refs_3_ = bf16[64,4096]{1,0:T(8,128)(2,1)S(1)} collective-permute-done((bf16[64,4096]{1,0:T(8,128)(2,1)}, bf16[64,4096]{1,0:T(8,128)(2,1)S(1)}, u32[]{:S(2)}, u32[]{:S(2)}) %collective-permute-start.1) | collective-permute-done | bytes 524320 | tf_op jit(solution)/shard_map/ppermute | solution.py:296
  39.6 2.1 %collective-permute-start.2 = (bf16[64,4096]{1,0:T(8,128)(2,1)S(1)}, bf16[64,4096]{1,0:T(8,128)(2,1)S(1)}, u32[]{:S(2)}, u32[]{:S(2)}) collective-permute-start(bf16[64,4096]{1,0:T(8,128)(2,1)S(1)} %collective-permute-done.1.refs_3_), channel_id=1, source_target_pairs={{0,2},{2,4},{4,6},{6,7},{7,5},{5,3},{3,1},{1,0},{8,10},{10,12},{12... | collective-permute-start | bytes 1572872 | tf_op jit(solution)/shard_map/ppermute | solution.py:296
  41.8 9.9 %shard_map.64 = (f32[512,2048]{1,0:T(8,128)S(1)}, bf16[4096,2048]{1,0:T(8,128)(2,1)S(1)}) custom-call(s32[6]{0:T(128)S(1)} %stack.63.starts_ref, bf16[64,4096]{1,0:T(8,128)(2,1)S(1)} %get-tuple-element.116.refs_0_, bf16[64,4096]{1,0:T(8,128)(2,1)} %collective-permute-done.refs_1_, bf16[64,4096]{1,0:T(8,128)(2,1)} %collective-permute-done.3.refs_2_, ...), custom_call_target="tpu_custom_call" | custom-call | tf_op jit(solution)/shard_map/pallas_call | solution.py:85
  51.7 2.1 %collective-permute-start.10 = (bf16[64,4096]{1,0:T(8,128)(2,1)S(1)}, bf16[64,4096]{1,0:T(8,128)(2,1)S(1)}, u32[]{:S(2)}, u32[]{:S(2)}) collective-permute-start(bf16[64,4096]{1,0:T(8,128)(2,1)S(1)} %collective-permute-done.8.refs_3_), channel_id=1, source_target_pairs={{0,2},{2,4},{4,6},{6,7},{7,5},{5,3},{3,1},{1,0},{8,10},{10,12},{12... | collective-permute-start | bytes 1572872 | tf_op jit(solution)/shard_map/ppermute | solution.py:296
  53.8 8.2 %collective-permute-done.2.refs_0_ = bf16[64,4096]{1,0:T(8,128)(2,1)S(1)} collective-permute-done((bf16[64,4096]{1,0:T(8,128)(2,1)S(1)}, bf16[64,4096]{1,0:T(8,128)(2,1)S(1)}, u32[]{:S(2)}, u32[]{:S(2)}) %collective-permute-start.2) | collective-permute-done | bytes 524320 | tf_op jit(solution)/shard_map/ppermute | solution.py:296
  62.0 2.2 %collective-permute-done.5.refs_1_ = bf16[64,4096]{1,0:T(8,128)(2,1)S(1)} collective-permute-done((bf16[64,4096]{1,0:T(8,128)(2,1)S(1)}, bf16[64,4096]{1,0:T(8,128)(2,1)S(1)}, u32[]{:S(2)}, u32[]{:S(2)}) %collective-permute-start.5) | collective-permute-done | bytes 524320 | tf_op jit(solution)/shard_map/ppermute | solution.py:299
  64.3 1.6 %collective-permute-start.12 = (bf16[32,4096]{1,0:T(8,128)(2,1)S(1)}, bf16[32,4096]{1,0:T(8,128)(2,1)S(1)}, u32[]{:S(2)}, u32[]{:S(2)}) collective-permute-start(bf16[32,4096]{1,0:T(8,128)(2,1)S(1)} %slice.32), channel_id=1, source_target_pairs={{0,2},{2,4},{4,6},{6,7},{7,5},{5,3},{3,1},{1,0},{8,10},{10,12},{12... | collective-permute-start | bytes 786440 | tf_op jit(solution)/shard_map/ppermute | solution.py:296
  66.6 6.5 %shard_map.65.refs_5_ = f32[512,2048]{1,0:T(8,128)S(1)} custom-call(s32[6]{0:T(128)S(1)} %stack.63.starts_ref, bf16[64,4096]{1,0:T(8,128)(2,1)S(1)} %get-tuple-element.115.refs_0_, bf16[64,4096]{1,0:T(8,128)(2,1)S(1)} %collective-permute-done.6.refs_1_, bf16[64,4096]{1,0:T(8,128)(2,1)S(1)} %collective-permute-done.7.refs_2_, ...), custom_call_target="tpu_custom_call" | custom-call | tf_op jit(solution)/shard_map/pallas_call | solution.py:85
  73.3 2.2 %collective-permute-start.14 = (bf16[32,4096]{1,0:T(8,128)(2,1)S(1)}, bf16[32,4096]{1,0:T(8,128)(2,1)S(1)}, u32[]{:S(2)}, u32[]{:S(2)}) collective-permute-start(bf16[32,4096]{1,0:T(8,128)(2,1)S(1)} %slice.30), channel_id=1, source_target_pairs={{0,2},{2,4},{4,6},{6,7},{7,5},{5,3},{3,1},{1,0},{8,10},{10,12},{12... | collective-permute-start | bytes 786440 | tf_op jit(solution)/shard_map/ppermute | solution.py:296
  75.6 3.3 %collective-permute-done.12.refs_2_ = bf16[32,4096]{1,0:T(8,128)(2,1)S(1)} collective-permute-done((bf16[32,4096]{1,0:T(8,128)(2,1)S(1)}, bf16[32,4096]{1,0:T(8,128)(2,1)S(1)}, u32[]{:S(2)}, u32[]{:S(2)}) %collective-permute-start.12) | collective-permute-done | bytes 262176 | tf_op jit(solution)/shard_map/ppermute | solution.py:296
  78.9 2.2 %collective-permute-done.13.refs_3_ = bf16[32,4096]{1,0:T(8,128)(2,1)S(1)} collective-permute-done((bf16[32,4096]{1,0:T(8,128)(2,1)S(1)}, bf16[32,4096]{1,0:T(8,128)(2,1)S(1)}, u32[]{:S(2)}, u32[]{:S(2)}) %collective-permute-start.13) | collective-permute-done | bytes 262176 | tf_op jit(solution)/shard_map/ppermute | solution.py:299
  81.1 7.9 %shard_map.66 = (f32[256,2048]{1,0:T(8,128)S(1)}, f32[32,2048]{1,0:T(8,128)S(1)}, f32[32,2048]{1,0:T(8,128)S(1)}, f32[32,2048]{1,0:T(8,128)S(1)}, f32[32,2048]{1...) custom-call(s32[8]{0:T(128)S(1)} %stack.56.starts_ref, ...), custom_call_target="tpu_custom_call" | custom-call | tf_op jit(solution)/shard_map/pallas_call | solution.py:147
  91.5 3.4 %shard_map.67.refs_7_ = f32[512,2048]{1,0:T(8,128)S(1)} custom-call(bf16[1024,512]{1,0:T(8,128)(2,1)S(1)} %pad_maximum_fusion.1.pair_ref, bf16[1024,2048]{1,0:T(8,128)(2,1)S(1)} %get-tuple-element.67.whole_ref), custom_call_target="tpu_custom_call" | custom-call | tf_op jit(solution)/shard_map/pallas_call | solution.py:171
  95.6 1.6 %collective-permute-start.24 = (bf16[2064,128]{1,0:T(8,128)(2,1)S(1)}, bf16[2064,128]{1,0:T(8,128)(2,1)S(1)}, u32[]{:S(2)}, u32[]{:S(2)}) collective-permute-start(bf16[2064,128]{1,0:T(8,128)(2,1)S(1)} %get-tuple-element.88), channel_id=1, source_target_pairs={{0,16},{8,24},{16,0},{24,8},{1,17},{9,25},{17,1},{25,9},{2,18},{10... | collective-permute-start | bytes 1585160 | tf_op jit(solution)/shard_map/ppermute | solution.py:337
  97.2 4.4 %shard_map.69 = (f32[256,1024]{1,0:T(8,128)S(1)}, f32[32,1024]{1,0:T(8,128)S(1)}, f32[32,1024]{1,0:T(8,128)S(1)}, f32[32,1024]{1,0:T(8,128)S(1)}, f32[32,1024]{1...) custom-call(s32[8]{0:T(128)S(1)} %stack.56.starts_ref, ...), custom_call_target="tpu_custom_call" | custom-call | tf_op jit(solution)/shard_map/pallas_call | solution.py:147
  103.7 4.2 %shard_map.71 = (f32[256,1024]{1,0:T(8,128)S(1)}, f32[32,1024]{1,0:T(8,128)S(1)}, f32[32,1024]{1,0:T(8,128)S(1)}, f32[32,1024]{1,0:T(8,128)S(1)}, f32[32,1024]{1...) custom-call(s32[8]{0:T(128)S(1)} %stack.56.starts_ref, ...), custom_call_target="tpu_custom_call" | custom-call | tf_op jit(solution)/shard_map/pallas_call | solution.py:147
  111.1 0.8 collective-permute-start.33
  112.2 1.3 %collective-permute-start.42 = (bf16[1040,128]{1,0:T(8,128)(2,1)S(1)}, bf16[1040,128]{1,0:T(8,128)(2,1)S(1)}, u32[]{:S(2)}, u32[]{:S(2)}) collective-permute-start(bf16[1040,128]{1,0:T(8,128)(2,1)S(1)} %get-tuple-element.112), channel_id=1, source_target_pairs={{0,16},{8,24},{16,0},{24,8},{1,17},{9,25},{17,1},{25,9},{2,18},{10... | collective-permute-start | bytes 798728 | tf_op jit(solution)/shard_map/ppermute | solution.py:343
  113.6 6.8 %collective-permute-done.33.refs_3_ = bf16[1040,128]{1,0:T(8,128)(2,1)S(1)} collective-permute-done((bf16[1040,128]{1,0:T(8,128)(2,1)S(1)}, bf16[1040,128]{1,0:T(8,128)(2,1)S(1)}, u32[]{:S(2)}, u32[]{:S(2)}) %collective-permute-start.33) | collective-permute-done | bytes 266272 | tf_op jit(solution)/shard_map/ppermute | solution.py:343
  120.4 5.0 %collective-permute-done.42.refs_5_ = bf16[1040,128]{1,0:T(8,128)(2,1)S(1)} collective-permute-done((bf16[1040,128]{1,0:T(8,128)(2,1)S(1)}, bf16[1040,128]{1,0:T(8,128)(2,1)S(1)}, u32[]{:S(2)}, u32[]{:S(2)}) %collective-permute-start.42) | collective-permute-done | bytes 266272 | tf_op jit(solution)/shard_map/ppermute | solution.py:343
  125.3 2.0 %shard_map.73 = f32[2,128,2048]{2,1,0:T(8,128)} custom-call(f32[128,2048]{1,0:T(8,128)S(1)} %get-tuple-element.87.refs_0_, bf16[2064,128]{1,0:T(8,128)(2,1)S(1)} %collective-permute-done.24.refs_1_, f32[128,1024]{1,0:T(8,128)S(1)} %get-tuple-element.99.refs_2_, bf16[1040,128]{1,0:T(8,128)(2,1)S(1)} %collective-permute-done.33.refs_3_, ...), custom_call_target="tpu_custom_call" | custom-call | tf_op jit(solution)/shard_map/pallas_call | solution.py:233
  (91 shorter events, 10.6 us)
Async XLA Ops:
  1.4 18.0 %collective-permute-start = (bf16[64,4096]{1,0:T(8,128)(2,1)S(1)}, bf16[64,4096]{1,0:T(8,128)(2,1)}, u32[]{:S(2)}, u32[]{:S(2)}) collective-permute-start(bf16[64,4096]{1,0:T(8,128)(2,1)S(1)} %get-tuple-element.116.refs_0_), channel_id=1, source_target_pairs={{0,2},{2,4},{4,6},{6,7},{7,5},{5,3},{3,1},{1,0},{8,10},{10,12},{12... | collective-permute-start | bytes 1572872 | tf_op jit(solution)/shard_map/ppermute | solution.py:296
  4.4 17.0 %collective-permute-start.3 = (bf16[64,4096]{1,0:T(8,128)(2,1)S(1)}, bf16[64,4096]{1,0:T(8,128)(2,1)}, u32[]{:S(2)}, u32[]{:S(2)}) collective-permute-start(bf16[64,4096]{1,0:T(8,128)(2,1)S(1)} %get-tuple-element.116.refs_0_), channel_id=1, source_target_pairs={{2,0},{4,2},{6,4},{7,6},{5,7},{3,5},{1,3},{0,1},{10,8},{12,10},{14... | collective-permute-start | bytes 1572872 | tf_op jit(solution)/shard_map/ppermute | solution.py:299
  4.4 23.9 %collective-permute-start.6 = (bf16[64,4096]{1,0:T(8,128)(2,1)S(1)}, bf16[64,4096]{1,0:T(8,128)(2,1)S(1)}, u32[]{:S(2)}, u32[]{:S(2)}) collective-permute-start(bf16[64,4096]{1,0:T(8,128)(2,1)S(1)} %get-tuple-element.115.refs_0_), channel_id=1, source_target_pairs={{0,2},{2,4},{4,6},{6,7},{7,5},{5,3},{3,1},{1,0},{8,10},{10,12},{12... | collective-permute-start | bytes 1572872 | tf_op jit(solution)/shard_map/ppermute | solution.py:296
  6.5 24.1 %collective-permute-start.7 = (bf16[64,4096]{1,0:T(8,128)(2,1)S(1)}, bf16[64,4096]{1,0:T(8,128)(2,1)S(1)}, u32[]{:S(2)}, u32[]{:S(2)}) collective-permute-start(bf16[64,4096]{1,0:T(8,128)(2,1)S(1)} %get-tuple-element.115.refs_0_), channel_id=1, source_target_pairs={{2,0},{4,2},{6,4},{7,6},{5,7},{3,5},{1,3},{0,1},{10,8},{12,10},{14... | collective-permute-start | bytes 1572872 | tf_op jit(solution)/shard_map/ppermute | solution.py:299
  19.4 20.2 %collective-permute-start.1 = (bf16[64,4096]{1,0:T(8,128)(2,1)}, bf16[64,4096]{1,0:T(8,128)(2,1)S(1)}, u32[]{:S(2)}, u32[]{:S(2)}) collective-permute-start(bf16[64,4096]{1,0:T(8,128)(2,1)} %collective-permute-done.refs_1_), channel_id=1, source_target_pairs={{0,2},{2,4},{4,6},{6,7},{7,5},{5,3},{3,1},{1,0},{8,10},{10,12},{12... | collective-permute-start | bytes 1572872 | tf_op jit(solution)/shard_map/ppermute | solution.py:296
  21.4 20.3 %collective-permute-start.4 = (bf16[64,4096]{1,0:T(8,128)(2,1)}, bf16[64,4096]{1,0:T(8,128)(2,1)S(1)}, u32[]{:S(2)}, u32[]{:S(2)}) collective-permute-start(bf16[64,4096]{1,0:T(8,128)(2,1)} %collective-permute-done.3.refs_2_), channel_id=1, source_target_pairs={{2,0},{4,2},{6,4},{7,6},{5,7},{3,5},{1,3},{0,1},{10,8},{12,10},{14... | collective-permute-start | bytes 1572872 | tf_op jit(solution)/shard_map/ppermute | solution.py:299
  28.3 23.4 %collective-permute-start.8 = (bf16[64,4096]{1,0:T(8,128)(2,1)S(1)}, bf16[64,4096]{1,0:T(8,128)(2,1)S(1)}, u32[]{:S(2)}, u32[]{:S(2)}) collective-permute-start(bf16[64,4096]{1,0:T(8,128)(2,1)S(1)} %collective-permute-done.6.refs_1_), channel_id=1, source_target_pairs={{0,2},{2,4},{4,6},{6,7},{7,5},{5,3},{3,1},{1,0},{8,10},{10,12},{12... | collective-permute-start | bytes 1572872 | tf_op jit(solution)/shard_map/ppermute | solution.py:296
  30.5 23.3 %collective-permute-start.9 = (bf16[64,4096]{1,0:T(8,128)(2,1)S(1)}, bf16[64,4096]{1,0:T(8,128)(2,1)S(1)}, u32[]{:S(2)}, u32[]{:S(2)}) collective-permute-start(bf16[64,4096]{1,0:T(8,128)(2,1)S(1)} %collective-permute-done.7.refs_2_), channel_id=1, source_target_pairs={{2,0},{4,2},{6,4},{7,6},{5,7},{3,5},{1,3},{0,1},{10,8},{12,10},{14... | collective-permute-start | bytes 1572872 | tf_op jit(solution)/shard_map/ppermute | solution.py:299
  39.6 22.5 %collective-permute-start.2 = (bf16[64,4096]{1,0:T(8,128)(2,1)S(1)}, bf16[64,4096]{1,0:T(8,128)(2,1)S(1)}, u32[]{:S(2)}, u32[]{:S(2)}) collective-permute-start(bf16[64,4096]{1,0:T(8,128)(2,1)S(1)} %collective-permute-done.1.refs_3_), channel_id=1, source_target_pairs={{0,2},{2,4},{4,6},{6,7},{7,5},{5,3},{3,1},{1,0},{8,10},{10,12},{12... | collective-permute-start | bytes 1572872 | tf_op jit(solution)/shard_map/ppermute | solution.py:296
  41.8 22.5 %collective-permute-start.5 = (bf16[64,4096]{1,0:T(8,128)(2,1)S(1)}, bf16[64,4096]{1,0:T(8,128)(2,1)S(1)}, u32[]{:S(2)}, u32[]{:S(2)}) collective-permute-start(bf16[64,4096]{1,0:T(8,128)(2,1)S(1)} %collective-permute-done.4.refs_4_), channel_id=1, source_target_pairs={{2,0},{4,2},{6,4},{7,6},{5,7},{3,5},{1,3},{0,1},{10,8},{12,10},{14... | collective-permute-start | bytes 1572872 | tf_op jit(solution)/shard_map/ppermute | solution.py:299
  51.7 21.6 %collective-permute-start.10 = (bf16[64,4096]{1,0:T(8,128)(2,1)S(1)}, bf16[64,4096]{1,0:T(8,128)(2,1)S(1)}, u32[]{:S(2)}, u32[]{:S(2)}) collective-permute-start(bf16[64,4096]{1,0:T(8,128)(2,1)S(1)} %collective-permute-done.8.refs_3_), channel_id=1, source_target_pairs={{0,2},{2,4},{4,6},{6,7},{7,5},{5,3},{3,1},{1,0},{8,10},{10,12},{12... | collective-permute-start | bytes 1572872 | tf_op jit(solution)/shard_map/ppermute | solution.py:296
  53.8 21.7 %collective-permute-start.11 = (bf16[64,4096]{1,0:T(8,128)(2,1)S(1)}, bf16[64,4096]{1,0:T(8,128)(2,1)S(1)}, u32[]{:S(2)}, u32[]{:S(2)}) collective-permute-start(bf16[64,4096]{1,0:T(8,128)(2,1)S(1)} %collective-permute-done.9.refs_4_), channel_id=1, source_target_pairs={{2,0},{4,2},{6,4},{7,6},{5,7},{3,5},{1,3},{0,1},{10,8},{12,10},{14... | collective-permute-start | bytes 1572872 | tf_op jit(solution)/shard_map/ppermute | solution.py:299
  64.3 14.6 %collective-permute-start.12 = (bf16[32,4096]{1,0:T(8,128)(2,1)S(1)}, bf16[32,4096]{1,0:T(8,128)(2,1)S(1)}, u32[]{:S(2)}, u32[]{:S(2)}) collective-permute-start(bf16[32,4096]{1,0:T(8,128)(2,1)S(1)} %slice.32), channel_id=1, source_target_pairs={{0,2},{2,4},{4,6},{6,7},{7,5},{5,3},{3,1},{1,0},{8,10},{10,12},{12... | collective-permute-start | bytes 786440 | tf_op jit(solution)/shard_map/ppermute | solution.py:296
  65.9 15.2 %collective-permute-start.13 = (bf16[32,4096]{1,0:T(8,128)(2,1)S(1)}, bf16[32,4096]{1,0:T(8,128)(2,1)S(1)}, u32[]{:S(2)}, u32[]{:S(2)}) collective-permute-start(bf16[32,4096]{1,0:T(8,128)(2,1)S(1)} %slice.33), channel_id=1, source_target_pairs={{2,0},{4,2},{6,4},{7,6},{5,7},{3,5},{1,3},{0,1},{10,8},{12,10},{14... | collective-permute-start | bytes 786440 | tf_op jit(solution)/shard_map/ppermute | solution.py:299
  73.3 15.7 %collective-permute-start.14 = (bf16[32,4096]{1,0:T(8,128)(2,1)S(1)}, bf16[32,4096]{1,0:T(8,128)(2,1)S(1)}, u32[]{:S(2)}, u32[]{:S(2)}) collective-permute-start(bf16[32,4096]{1,0:T(8,128)(2,1)S(1)} %slice.30), channel_id=1, source_target_pairs={{0,2},{2,4},{4,6},{6,7},{7,5},{5,3},{3,1},{1,0},{8,10},{10,12},{12... | collective-permute-start | bytes 786440 | tf_op jit(solution)/shard_map/ppermute | solution.py:296
  75.5 13.5 %collective-permute-start.15 = (bf16[32,4096]{1,0:T(8,128)(2,1)S(1)}, bf16[32,4096]{1,0:T(8,128)(2,1)S(1)}, u32[]{:S(2)}, u32[]{:S(2)}) collective-permute-start(bf16[32,4096]{1,0:T(8,128)(2,1)S(1)} %slice.31), channel_id=1, source_target_pairs={{2,0},{4,2},{6,4},{7,6},{5,7},{3,5},{1,3},{0,1},{10,8},{12,10},{14... | collective-permute-start | bytes 786440 | tf_op jit(solution)/shard_map/ppermute | solution.py:299
  89.1 1.9 %collective-permute-start.17 = (f32[32,2048]{1,0:T(8,128)S(1)}, f32[32,2048]{1,0:T(8,128)S(1)}, u32[]{:S(2)}, u32[]{:S(2)}) collective-permute-start(f32[32,2048]{1,0:T(8,128)S(1)} %get-tuple-element.80), channel_id=1, source_target_pairs={{0,8},{8,0},{16,24},{24,16},{1,9},{9,1},{17,25},{25,17},{2,10},{10... | collective-permute-start | bytes 786440 | tf_op jit(solution)/shard_map/ppermute | solution.py:330
  89.6 1.8 %collective-permute-start.18 = (f32[32,2048]{1,0:T(8,128)S(1)}, f32[32,2048]{1,0:T(8,128)S(1)}, u32[]{:S(2)}, u32[]{:S(2)}) collective-permute-start(f32[32,2048]{1,0:T(8,128)S(1)} %get-tuple-element.81), channel_id=1, source_target_pairs={{0,8},{8,0},{16,24},{24,16},{1,9},{9,1},{17,25},{25,17},{2,10},{10... | collective-permute-start | bytes 786440 | tf_op jit(solution)/shard_map/ppermute | solution.py:330
  89.7 5.3 %collective-permute-start.19 = (f32[32,2048]{1,0:T(8,128)S(1)}, f32[32,2048]{1,0:T(8,128)S(1)}, u32[]{:S(2)}, u32[]{:S(2)}) collective-permute-start(f32[32,2048]{1,0:T(8,128)S(1)} %get-tuple-element.82), channel_id=1, source_target_pairs={{0,8},{8,0},{16,24},{24,16},{1,9},{9,1},{17,25},{25,17},{2,10},{10... | collective-permute-start | bytes 786440 | tf_op jit(solution)/shard_map/ppermute | solution.py:330
  90.1 4.8 %collective-permute-start.20 = (f32[32,2048]{1,0:T(8,128)S(1)}, f32[32,2048]{1,0:T(8,128)S(1)}, u32[]{:S(2)}, u32[]{:S(2)}) collective-permute-start(f32[32,2048]{1,0:T(8,128)S(1)} %get-tuple-element.83), channel_id=1, source_target_pairs={{0,8},{8,0},{16,24},{24,16},{1,9},{9,1},{17,25},{25,17},{2,10},{10... | collective-permute-start | bytes 786440 | tf_op jit(solution)/shard_map/ppermute | solution.py:330
  90.6 4.3 %collective-permute-start.21 = (f32[32,2048]{1,0:T(8,128)S(1)}, f32[32,2048]{1,0:T(8,128)S(1)}, u32[]{:S(2)}, u32[]{:S(2)}) collective-permute-start(f32[32,2048]{1,0:T(8,128)S(1)} %get-tuple-element.84), channel_id=1, source_target_pairs={{0,8},{8,0},{16,24},{24,16},{1,9},{9,1},{17,25},{25,17},{2,10},{10... | collective-permute-start | bytes 786440 | tf_op jit(solution)/shard_map/ppermute | solution.py:330
  91.0 4.0 %collective-permute-start.22 = (f32[32,2048]{1,0:T(8,128)S(1)}, f32[32,2048]{1,0:T(8,128)S(1)}, u32[]{:S(2)}, u32[]{:S(2)}) collective-permute-start(f32[32,2048]{1,0:T(8,128)S(1)} %get-tuple-element.85), channel_id=1, source_target_pairs={{0,8},{8,0},{16,24},{24,16},{1,9},{9,1},{17,25},{25,17},{2,10},{10... | collective-permute-start | bytes 786440 | tf_op jit(solution)/shard_map/ppermute | solution.py:330
  91.4 3.6 %collective-permute-start.23 = (f32[32,2048]{1,0:T(8,128)S(1)}, f32[32,2048]{1,0:T(8,128)S(1)}, u32[]{:S(2)}, u32[]{:S(2)}) collective-permute-start(f32[32,2048]{1,0:T(8,128)S(1)} %get-tuple-element.86), channel_id=1, source_target_pairs={{0,8},{8,0},{16,24},{24,16},{1,9},{9,1},{17,25},{25,17},{2,10},{10... | collective-permute-start | bytes 786440 | tf_op jit(solution)/shard_map/ppermute | solution.py:330
  95.6 14.8 %collective-permute-start.24 = (bf16[2064,128]{1,0:T(8,128)(2,1)S(1)}, bf16[2064,128]{1,0:T(8,128)(2,1)S(1)}, u32[]{:S(2)}, u32[]{:S(2)}) collective-permute-start(bf16[2064,128]{1,0:T(8,128)(2,1)S(1)} %get-tuple-element.88), channel_id=1, source_target_pairs={{0,16},{8,24},{16,0},{24,8},{1,17},{9,25},{17,1},{25,9},{2,18},{10... | collective-permute-start | bytes 1585160 | tf_op jit(solution)/shard_map/ppermute | solution.py:337
  102.3 5.7 %collective-permute-start.28 = (f32[32,1024]{1,0:T(8,128)S(1)}, f32[32,1024]{1,0:T(8,128)S(1)}, u32[]{:S(2)}, u32[]{:S(2)}) collective-permute-start(f32[32,1024]{1,0:T(8,128)S(1)} %get-tuple-element.94), channel_id=1, source_target_pairs={{0,8},{8,0},{16,24},{24,16},{1,9},{9,1},{17,25},{25,17},{2,10},{10... | collective-permute-start | bytes 393224 | tf_op jit(solution)/shard_map/ppermute | solution.py:330
  103.0 5.3 %collective-permute-start.29 = (f32[32,1024]{1,0:T(8,128)S(1)}, f32[32,1024]{1,0:T(8,128)S(1)}, u32[]{:S(2)}, u32[]{:S(2)}) collective-permute-start(f32[32,1024]{1,0:T(8,128)S(1)} %get-tuple-element.95), channel_id=1, source_target_pairs={{0,8},{8,0},{16,24},{24,16},{1,9},{9,1},{17,25},{25,17},{2,10},{10... | collective-permute-start | bytes 393224 | tf_op jit(solution)/shard_map/ppermute | solution.py:330
  103.2 5.3 %collective-permute-start.30 = (f32[32,1024]{1,0:T(8,128)S(1)}, f32[32,1024]{1,0:T(8,128)S(1)}, u32[]{:S(2)}, u32[]{:S(2)}) collective-permute-start(f32[32,1024]{1,0:T(8,128)S(1)} %get-tuple-element.96), channel_id=1, source_target_pairs={{0,8},{8,0},{16,24},{24,16},{1,9},{9,1},{17,25},{25,17},{2,10},{10... | collective-permute-start | bytes 393224 | tf_op jit(solution)/shard_map/ppermute | solution.py:330
  103.5 5.3 %collective-permute-start.31 = (f32[32,1024]{1,0:T(8,128)S(1)}, f32[32,1024]{1,0:T(8,128)S(1)}, u32[]{:S(2)}, u32[]{:S(2)}) collective-permute-start(f32[32,1024]{1,0:T(8,128)S(1)} %get-tuple-element.97), channel_id=1, source_target_pairs={{0,8},{8,0},{16,24},{24,16},{1,9},{9,1},{17,25},{25,17},{2,10},{10... | collective-permute-start | bytes 393224 | tf_op jit(solution)/shard_map/ppermute | solution.py:330
  109.7 2.2 %collective-permute-start.38 = (f32[32,1024]{1,0:T(8,128)S(1)}, f32[32,1024]{1,0:T(8,128)S(1)}, u32[]{:S(2)}, u32[]{:S(2)}) collective-permute-start(f32[32,1024]{1,0:T(8,128)S(1)} %get-tuple-element.107), channel_id=1, source_target_pairs={{0,8},{8,0},{16,24},{24,16},{1,9},{9,1},{17,25},{25,17},{2,10},{10... | collective-permute-start | bytes 393224 | tf_op jit(solution)/shard_map/ppermute | solution.py:330
  109.9 2.0 %collective-permute-start.39 = (f32[32,1024]{1,0:T(8,128)S(1)}, f32[32,1024]{1,0:T(8,128)S(1)}, u32[]{:S(2)}, u32[]{:S(2)}) collective-permute-start(f32[32,1024]{1,0:T(8,128)S(1)} %get-tuple-element.108), channel_id=1, source_target_pairs={{0,8},{8,0},{16,24},{24,16},{1,9},{9,1},{17,25},{25,17},{2,10},{10... | collective-permute-start | bytes 393224 | tf_op jit(solution)/shard_map/ppermute | solution.py:330
  111.1 9.3 %collective-permute-start.33 = (bf16[1040,128]{1,0:T(8,128)(2,1)S(1)}, bf16[1040,128]{1,0:T(8,128)(2,1)S(1)}, u32[]{:S(2)}, u32[]{:S(2)}) collective-permute-start(bf16[1040,128]{1,0:T(8,128)(2,1)S(1)} %get-tuple-element.100), channel_id=1, source_target_pairs={{0,16},{8,24},{16,0},{24,8},{1,17},{9,25},{17,1},{25,9},{2,18},{10... | collective-permute-start | bytes 798728 | tf_op jit(solution)/shard_map/ppermute | solution.py:343
  112.2 13.1 %collective-permute-start.42 = (bf16[1040,128]{1,0:T(8,128)(2,1)S(1)}, bf16[1040,128]{1,0:T(8,128)(2,1)S(1)}, u32[]{:S(2)}, u32[]{:S(2)}) collective-permute-start(bf16[1040,128]{1,0:T(8,128)(2,1)S(1)} %get-tuple-element.112), channel_id=1, source_target_pairs={{0,16},{8,24},{16,0},{24,8},{1,17},{9,25},{17,1},{25,9},{2,18},{10... | collective-permute-start | bytes 798728 | tf_op jit(solution)/shard_map/ppermute | solution.py:343
  (17 other events, 44.1 us)

commit v3 on v2

--- a/solution.py
+++ b/solution.py
@@ -9,7 +9,7 @@
 
 F32, BF16 = jnp.float32, jnp.bfloat16
 COLS, LANES = 512, 128
-PIECES, SPLITS = 8, 2
+PIECES, SPLITS = 4, 2
 COST = pl.CostEstimate(flops=0, bytes_accessed=0, transcendentals=0)
 KERNEL_BYTES = 12 * 2**20
 OCTAVES, LOWEST = 248.0, -124.0
@@ -155,27 +155,30 @@
     )(starts, *pieces, *given)
 
 
-def times_kernel(pair_ref, whole_ref, out_ref):
+def times_kernel(pair_ref, *refs):
+    *whole_refs, out_ref = refs
     size = out_ref.shape[0]
-    block = size // 2
-    for j in range(out_ref.shape[1] // COLS):
-        columns = slice(j * COLS, (j + 1) * COLS)
-        for top in (0, block):
-            out_ref[top : top + block, columns] = solve(
-                pair_ref, whole_ref[:size, columns], whole_ref[size:, columns], top, block, size
-            )
-
-
-def times(pair, whole):
-    size, width = whole.shape[0] // 2, whole.shape[1]
+    block, at = size // 2, 0
+    for whole_ref in whole_refs:
+        for j in range(whole_ref.shape[1] // COLS):
+            here = slice(j * COLS, (j + 1) * COLS)
+            for top in (0, block):
+                out_ref[top : top + block, at : at + COLS] = solve(
+                    pair_ref, whole_ref[:size, here], whole_ref[size:, here], top, block, size
+                )
+            at += COLS
+
+
+def times(pair, wholes):
+    size, width = wholes[0].shape[0] // 2, sum(whole.shape[1] for whole in wholes)
     return pl.pallas_call(
         times_kernel,
-        in_specs=[VMEM] * 2,
+        in_specs=[VMEM] * (1 + len(wholes)),
         out_specs=VMEM,
         out_shape=pltpu.VMEM((size, width), F32),
         compiler_params=params(),
         cost_estimate=COST,
-    )(pair, whole)
+    )(pair, *wholes)
 
 
 def pack_kernel(keep_ref, *refs):
@@ -316,31 +319,33 @@
     matrices = [halves(inv_first), halves(cross), halves(inv_second)]
     early_starts = after(starts(*[rows_of(s) for s in (0, -1, 1, -2, 2)], p * rows), late_starts, *matrices)
     rhs_a, held = early(early_starts, [own_a, fa[1], ba[1], fa[2], ba[2]], prev_solved, cross_cov[0], size, True)
-    step(fb, ahead, rhs_a)
-    step(bb, back, rhs_a)
-    fa.append(ahead(fa[3][:half]))
-    ba.append(back(ba[3][half:]))
-    rhs_b, = early(after(early_starts, fa[3], ba[3]), [own_b, fb[1], bb[1], fb[2], bb[2]], held, cross_cov[1], size, False)
-    fb.append(ahead(after(fb[3], rhs_b)[:half]))
-    bb.append(back(after(bb[3], rhs_b)[half:]))
+    rhs_b, = early(early_starts, [own_b, fb[1], bb[1], fb[2], bb[2]], held, cross_cov[1], size, False)
+    fa.append(ahead(after(fa[3], rhs_b)[:half]))
+    ba.append(back(after(ba[3], rhs_b)[half:]))
+    step(fb, ahead, fa[4], ba[4])
+    step(bb, back, fa[4], ba[4])
+    fb.append(ahead(fb[3][:half]))
+    bb.append(back(bb[3][half:]))
 
     width = cross_cov.shape[2]
 
     def exchange(keep, sends, *others):
         return pack(after(keep, *others), [lax.ppermute(send, "prow", SWAP_CORE) for send in sends])
 
-    keep, *sends, high_low = late(
-        after(late_starts, rhs_b, fb[3], bb[3]), [fa[3], ba[3], fa[4], ba[4]], held, rhs_a, matrices[0], None, 0, width)
-    sends = lax.optimization_barrier((*sends, fb[4], bb[4]))[:PIECES]
-    base = times(matrices[1], high_low)
-    own, coded = exchange(keep, sends, base)
-    sums = [(own, lax.ppermute(coded, "prow", SWAP_Y))]
-    ready = after(late_starts, coded)
     part = width // SPLITS
+    last_a, last_b = [fa[3], ba[3], fa[4], ba[4]], [fb[3], bb[3], fb[4], bb[4]]
+    sums, parts = [], []
     for i in range(SPLITS):
-        keep, *sends = late(ready, [fb[3], bb[3], fb[4], bb[4]], held, rhs_b, matrices[2], base, i * part, part)
-        own, coded = exchange(keep, sends, *([sums[0][1]] if i == SPLITS - 1 else []))
+        keep, *sends, high_low = late(late_starts, last_a, held, rhs_a, matrices[0], None, i * part, part)
+        own, coded = exchange(keep, sends, *([fb[3], bb[3]] if i else []))
         sums.append((own, lax.ppermute(coded, "prow", SWAP_Y)))
+        parts.append(high_low)
+    base = times(matrices[1], parts)
+    for i in range(SPLITS):
+        ready = after(late_starts, coded, *([sums[0][1]] if i else []))
+        keep, *sends = late(ready, last_b, held, rhs_b, matrices[2], base, i * part, part)
+        own, coded_b = exchange(keep, sends, *([sums[1][1]] if i else []))
+        sums.append((own, lax.ppermute(coded_b, "prow", SWAP_Y)))
     return unpack(sums)
 
 

time: 128 us -> 121 us (0.945)
  waiting for transfers between devices: 45.3 us -> 42.2 us
  other arithmetic: 5.41 us -> 2.47 us
    ppermute x2, waiting for transfers between devices: 11.7 us -> 0.01 us  [fast(): sums.append((own, lax.ppermute(coded, 'prow', SWAP_Y)))]
    ppermute x1 -> x2, waiting for transfers between devices: 0.01 us -> 11 us  [fast(): sums.append((own, lax.ppermute(coded_b, 'prow', SWAP_Y)))]
    ppermute x24 -> x16, starting transfers between devices: 5.76 us -> 3.9 us  [exchange(): lax.ppermute(send, 'prow', SWAP_CORE)]
    ppermute x24 -> x16, waiting for transfers between devices: 1.63 us -> 0.09 us  [exchange(): lax.ppermute(send, 'prow', SWAP_CORE)]
    another operation x2, other arithmetic: 2.62 us -> 1.13 us
    concatenate x3, other arithmetic: 2.79 us -> 1.34 us  [halves(): return jnp.concatenate([high, matrix - high]).astype(BF16)]
    ppermute x1 -> x2, starting transfers between devices: 1.6 us -> 2.84 us  [fast(): sums.append((own, lax.ppermute(coded_b, 'prow', SWAP_Y)))]
    pallas_call x3 -> x4, Pallas kernels: 16.5 us -> 17.1 us  [late(): pl.pallas_call(functools.partial(late_kernel, base is not None, first, DE...]
  transfers between devices with their start and end apart: 43 -> 36, of which waited for: 14 -> 15; matrix products, arithmetic and copies ran while one was open for 10% -> 7% of each run, Pallas kernels for 29% -> 32%
where the time goes in v3:
time: 121 us; the launch traced here: 120 us
  waiting for transfers between devices  42.2 us (35%)
  Pallas kernels  40.7 us (34%)
  starting transfers between devices  26.6 us (22%)
  matrix products  6.04 us (5%)
  other arithmetic  2.47 us (2%)
  local copies, waits for them, and re-layouts  2.09 us (2%)
    ppermute x8, waiting for transfers between devices, ahead(): return lax.ppermute(x, 'pcol', AHEAD)  26.6 us
    pallas_call x4, Pallas kernels, late(): pl.pallas_call(functools.partial(late_kernel, base is not None, first, DE...  17.1 us
    pallas_call x2, Pallas kernels, early(): pl.pallas_call(functools.partial(early_kernel, streams), in_specs=[pl.Blo...  16.9 us
    ppermute x8, starting transfers between devices, ahead(): return lax.ppermute(x, 'pcol', AHEAD)  16.6 us
    ppermute x2, waiting for transfers between devices, fast(): sums.append((own, lax.ppermute(coded_b, 'prow', SWAP_Y)))  11 us
    dot_general x2, matrix products, mult(): jnp.dot(left, right, preferred_element_type=F32, precision=lax.Precision....  6.04 us
    ppermute x8, waiting for transfers between devices, back(): return lax.ppermute(x, 'pcol', BACK)  4.6 us
    ppermute x16, starting transfers between devices, exchange(): lax.ppermute(send, 'prow', SWAP_CORE)  3.9 us
  transfers between devices with their start and end apart: 36, of which 15 were waited for; matrix products, arithmetic and copies ran while one was open for 7% of the time, Pallas kernels for 32%

profile of v3, /device:TPU:0, one launch (start us, length us, event | category | flops | bytes accessed | tf_op | source)
XLA Modules:
  0.0 120.4 jit_solution(16250534749885364377)
XLA Ops:
  0.0 1.4 %slice_bitcast_fusion.2 = (bf16[64,4096]{1,0:T(8,128)(2,1)S(1)}, bf16[64,4096]{1,0:T(8,128)(2,1)S(1)}) fusion(bf16[2,64,4096]{2,1,0:T(8,128)(2,1)} %param.7), kind=kLoop, calls=%fused_computation.16 | loop fusion | bytes 2097152 | tf_op jit(solution)/shard_map/squeeze | solution.py:304
  1.4 3.1 %collective-permute-start = (bf16[64,4096]{1,0:T(8,128)(2,1)S(1)}, bf16[64,4096]{1,0:T(8,128)(2,1)S(1)}, u32[]{:S(2)}, u32[]{:S(2)}) collective-permute-start(bf16[64,4096]{1,0:T(8,128)(2,1)S(1)} %get-tuple-element.90.refs_0_), channel_id=1, source_target_pairs={{0,2},{2,4},{4,6},{6,7},{7,5},{5,3},{3,1},{1,0},{8,10},{10,12},{12... | collective-permute-start | bytes 1572872 | tf_op jit(solution)/shard_map/ppermute | solution.py:299
  4.5 2.0 %collective-permute-start.6 = (bf16[64,4096]{1,0:T(8,128)(2,1)S(1)}, bf16[64,4096]{1,0:T(8,128)(2,1)S(1)}, u32[]{:S(2)}, u32[]{:S(2)}) collective-permute-start(bf16[64,4096]{1,0:T(8,128)(2,1)S(1)} %get-tuple-element.89.refs_0_), channel_id=1, source_target_pairs={{0,2},{2,4},{4,6},{6,7},{7,5},{5,3},{3,1},{1,0},{8,10},{10,12},{12... | collective-permute-start | bytes 1572872 | tf_op jit(solution)/shard_map/ppermute | solution.py:299
  6.6 2.8 %fusion.4 = f32[512,512]{1,0:T(8,128)} fusion(f32[512,512]{1,0:T(8,128)S(1)} %copy-done, f32[512,512]{1,0:T(8,128)S(1)} %copy-done.3), kind=kOutput, calls=%fused_computation.18 | convolution fusion | flops 1610612736 | bytes 3145728 | tf_op jit(solution)/shard_map/dot_general | solution.py:247
  10.5 1.2 pad_maximum_fusion.refs_6_
  11.9 3.2 %reduce-precision_convert_fusion.1 = (bf16[512,512]{1,0:T(8,128)(2,1)S(1)}, bf16[512,512]{1,0:T(8,128)(2,1)S(1)}) fusion(f32[512,512]{1,0:T(8,128)S(1)} %copy-done.2, f32[512,512]{1,0:T(8,128)} %param.11), kind=kOutput, calls=%fused_computation.3 | convolution fusion | flops 1611923456 | bytes 3145728 | tf_op jit(solution)/shard_map/dot_general | solution.py:247
  15.1 2.1 %collective-permute-done.refs_1_ = bf16[64,4096]{1,0:T(8,128)(2,1)S(1)} collective-permute-done((bf16[64,4096]{1,0:T(8,128)(2,1)S(1)}, bf16[64,4096]{1,0:T(8,128)(2,1)S(1)}, u32[]{:S(2)}, u32[]{:S(2)}) %collective-permute-start) | collective-permute-done | bytes 524320 | tf_op jit(solution)/shard_map/ppermute | solution.py:299
  17.2 2.1 %collective-permute-start.1 = (bf16[64,4096]{1,0:T(8,128)(2,1)S(1)}, bf16[64,4096]{1,0:T(8,128)(2,1)S(1)}, u32[]{:S(2)}, u32[]{:S(2)}) collective-permute-start(bf16[64,4096]{1,0:T(8,128)(2,1)S(1)} %collective-permute-done.refs_1_), channel_id=1, source_target_pairs={{0,2},{2,4},{4,6},{6,7},{7,5},{5,3},{3,1},{1,0},{8,10},{10,12},{12... | collective-permute-start | bytes 1572872 | tf_op jit(solution)/shard_map/ppermute | solution.py:299
  19.8 8.6 %collective-permute-done.6.refs_1_ = bf16[64,4096]{1,0:T(8,128)(2,1)S(1)} collective-permute-done((bf16[64,4096]{1,0:T(8,128)(2,1)S(1)}, bf16[64,4096]{1,0:T(8,128)(2,1)S(1)}, u32[]{:S(2)}, u32[]{:S(2)}) %collective-permute-start.6) | collective-permute-done | bytes 524320 | tf_op jit(solution)/shard_map/ppermute | solution.py:299
  28.4 2.1 %collective-permute-start.8 = (bf16[64,4096]{1,0:T(8,128)(2,1)S(1)}, bf16[64,4096]{1,0:T(8,128)(2,1)S(1)}, u32[]{:S(2)}, u32[]{:S(2)}) collective-permute-start(bf16[64,4096]{1,0:T(8,128)(2,1)S(1)} %collective-permute-done.6.refs_1_), channel_id=1, source_target_pairs={{0,2},{2,4},{4,6},{6,7},{7,5},{5,3},{3,1},{1,0},{8,10},{10,12},{12... | collective-permute-start | bytes 1572872 | tf_op jit(solution)/shard_map/ppermute | solution.py:299
  30.7 8.9 %collective-permute-done.1.refs_3_ = bf16[64,4096]{1,0:T(8,128)(2,1)S(1)} collective-permute-done((bf16[64,4096]{1,0:T(8,128)(2,1)S(1)}, bf16[64,4096]{1,0:T(8,128)(2,1)S(1)}, u32[]{:S(2)}, u32[]{:S(2)}) %collective-permute-start.1) | collective-permute-done | bytes 524320 | tf_op jit(solution)/shard_map/ppermute | solution.py:299
  39.7 2.1 %collective-permute-start.2 = (bf16[64,4096]{1,0:T(8,128)(2,1)S(1)}, bf16[64,4096]{1,0:T(8,128)(2,1)S(1)}, u32[]{:S(2)}, u32[]{:S(2)}) collective-permute-start(bf16[64,4096]{1,0:T(8,128)(2,1)S(1)} %collective-permute-done.1.refs_3_), channel_id=1, source_target_pairs={{0,2},{2,4},{4,6},{6,7},{7,5},{5,3},{3,1},{1,0},{8,10},{10,12},{12... | collective-permute-start | bytes 1572872 | tf_op jit(solution)/shard_map/ppermute | solution.py:299
  42.1 9.8 %shard_map.64 = (f32[512,2048]{1,0:T(8,128)S(1)}, bf16[4096,2048]{1,0:T(8,128)(2,1)S(1)}) custom-call(s32[6]{0:T(128)S(1)} %stack.63.starts_ref, bf16[64,4096]{1,0:T(8,128)(2,1)S(1)} %get-tuple-element.90.refs_0_, bf16[64,4096]{1,0:T(8,128)(2,1)S(1)} %collective-permute-done.refs_1_, bf16[64,4096]{1,0:T(8,128)(2,1)} %collective-permute-done.3.refs_2_, ...), custom_call_target="tpu_custom_call" | custom-call | tf_op jit(solution)/shard_map/pallas_call | solution.py:85
  51.9 1.2 %collective-permute-done.9.refs_4_ = bf16[64,4096]{1,0:T(8,128)(2,1)S(1)} collective-permute-done((bf16[64,4096]{1,0:T(8,128)(2,1)}, bf16[64,4096]{1,0:T(8,128)(2,1)S(1)}, u32[]{:S(2)}, u32[]{:S(2)}) %collective-permute-start.9) | collective-permute-done | bytes 524320 | tf_op jit(solution)/shard_map/ppermute | solution.py:302
  53.1 7.1 %shard_map.65.refs_5_ = f32[512,2048]{1,0:T(8,128)S(1)} custom-call(s32[6]{0:T(128)S(1)} %stack.63.starts_ref, bf16[64,4096]{1,0:T(8,128)(2,1)S(1)} %get-tuple-element.89.refs_0_, bf16[64,4096]{1,0:T(8,128)(2,1)S(1)} %collective-permute-done.6.refs_1_, bf16[64,4096]{1,0:T(8,128)(2,1)} %collective-permute-done.7.refs_2_, ...), custom_call_target="tpu_custom_call" | custom-call | tf_op jit(solution)/shard_map/pallas_call | solution.py:85
  61.3 1.9 %collective-permute-start.10 = (bf16[32,4096]{1,0:T(8,128)(2,1)S(1)}, bf16[32,4096]{1,0:T(8,128)(2,1)S(1)}, u32[]{:S(2)}, u32[]{:S(2)}) collective-permute-start(bf16[32,4096]{1,0:T(8,128)(2,1)S(1)} %slice.28), channel_id=1, source_target_pairs={{0,2},{2,4},{4,6},{6,7},{7,5},{5,3},{3,1},{1,0},{8,10},{10,12},{12... | collective-permute-start | bytes 786440 | tf_op jit(solution)/shard_map/ppermute | solution.py:299
  63.5 5.4 %collective-permute-done.10.refs_2_ = bf16[32,4096]{1,0:T(8,128)(2,1)S(1)} collective-permute-done((bf16[32,4096]{1,0:T(8,128)(2,1)S(1)}, bf16[32,4096]{1,0:T(8,128)(2,1)S(1)}, u32[]{:S(2)}, u32[]{:S(2)}) %collective-permute-start.10) | collective-permute-done | bytes 262176 | tf_op jit(solution)/shard_map/ppermute | solution.py:299
  68.9 1.3 %collective-permute-done.11.refs_3_ = bf16[32,4096]{1,0:T(8,128)(2,1)S(1)} collective-permute-done((bf16[32,4096]{1,0:T(8,128)(2,1)S(1)}, bf16[32,4096]{1,0:T(8,128)(2,1)S(1)}, u32[]{:S(2)}, u32[]{:S(2)}) %collective-permute-start.11) | collective-permute-done | bytes 262176 | tf_op jit(solution)/shard_map/ppermute | solution.py:302
  70.2 1.6 %collective-permute-start.17 = (bf16[64,4096]{1,0:T(8,128)(2,1)S(1)}, bf16[64,4096]{1,0:T(8,128)(2,1)S(1)}, u32[]{:S(2)}, u32[]{:S(2)}) collective-permute-start(bf16[64,4096]{1,0:T(8,128)(2,1)S(1)} %collective-permute-done.8.refs_3_), channel_id=1, source_target_pairs={{0,2},{2,4},{4,6},{6,7},{7,5},{5,3},{3,1},{1,0},{8,10},{10,12},{12... | collective-permute-start | bytes 1572872 | tf_op jit(solution)/shard_map/ppermute | solution.py:299
  72.2 4.3 %shard_map.66 = (f32[256,1024]{1,0:T(8,128)S(1)}, f32[64,1024]{1,0:T(8,128)S(1)}, f32[64,1024]{1,0:T(8,128)S(1)}, f32[64,1024]{1,0:T(8,128)S(1)}, f32[64,1024]{1...) custom-call(s32[8]{0:T(128)S(1)} %stack.56.starts_ref, bf16[64,4096]{1,0:T(8,128)(2,1)S(1)} %collective-permute-done.2.refs_0_, ...), custom_call_target="tpu_custom_call" | custom-call | tf_op jit(solution)/shard_map/pallas_call | solution.py:147
  77.2 4.3 %shard_map.68 = (f32[256,1024]{1,0:T(8,128)S(1)}, f32[64,1024]{1,0:T(8,128)S(1)}, f32[64,1024]{1,0:T(8,128)S(1)}, f32[64,1024]{1,0:T(8,128)S(1)}, f32[64,1024]{1...) custom-call(s32[8]{0:T(128)S(1)} %stack.56.starts_ref, bf16[64,4096]{1,0:T(8,128)(2,1)S(1)} %collective-permute-done.2.refs_0_, ...), custom_call_target="tpu_custom_call" | custom-call | tf_op jit(solution)/shard_map/pallas_call | solution.py:147
  83.2 1.6 %collective-permute-start.24 = (bf16[32,4096]{1,0:T(8,128)(2,1)S(1)}, bf16[32,4096]{1,0:T(8,128)(2,1)S(1)}, u32[]{:S(2)}, u32[]{:S(2)}) collective-permute-start(bf16[32,4096]{1,0:T(8,128)(2,1)S(1)} %slice.32), channel_id=1, source_target_pairs={{0,2},{2,4},{4,6},{6,7},{7,5},{5,3},{3,1},{1,0},{8,10},{10,12},{12... | collective-permute-start | bytes 786440 | tf_op jit(solution)/shard_map/ppermute | solution.py:299
  85.5 1.6 %collective-permute-start.16 = (bf16[1040,128]{1,0:T(8,128)(2,1)S(1)}, bf16[1040,128]{1,0:T(8,128)(2,1)S(1)}, u32[]{:S(2)}, u32[]{:S(2)}) collective-permute-start(bf16[1040,128]{1,0:T(8,128)(2,1)S(1)} %get-tuple-element.57), channel_id=1, source_target_pairs={{0,16},{8,24},{16,0},{24,8},{1,17},{9,25},{17,1},{25,9},{2,18},{10... | collective-permute-start | bytes 798728 | tf_op jit(solution)/shard_map/ppermute | solution.py:341
  88.0 3.4 %shard_map.70.refs_7_ = f32[512,2048]{1,0:T(8,128)S(1)} custom-call(bf16[1024,512]{1,0:T(8,128)(2,1)S(1)} %pad_maximum_fusion.1.pair_ref, bf16[1024,1024]{1,0:T(8,128)(2,1)S(1)} %get-tuple-element.69.refs_0_, bf16[1024,1024]{1,0:T(8,128)(2,1)S(1)} %get-tuple-element.70.refs_1_), custom_call_target="tpu_custom_call" | custom-call | tf_op jit(solution)/shard_map/pallas_call | solution.py:174
  91.9 1.3 %collective-permute-done.25.refs_3_ = bf16[32,4096]{1,0:T(8,128)(2,1)S(1)} collective-permute-done((bf16[32,4096]{1,0:T(8,128)(2,1)S(1)}, bf16[32,4096]{1,0:T(8,128)(2,1)S(1)}, u32[]{:S(2)}, u32[]{:S(2)}) %collective-permute-start.25) | collective-permute-done | bytes 262176 | tf_op jit(solution)/shard_map/ppermute | solution.py:302
  93.2 4.2 %shard_map.71 = (f32[256,1024]{1,0:T(8,128)S(1)}, f32[64,1024]{1,0:T(8,128)S(1)}, f32[64,1024]{1,0:T(8,128)S(1)}, f32[64,1024]{1,0:T(8,128)S(1)}, f32[64,1024]{1,0:T(8,128)S(1)}) custom-call(s32[8]{0:T(128)S(1)} %stack.56.starts_ref, bf16[64,4096]{1,0:T(8,128)(2,1)S(1)} %collective-permute-done.17.refs_0_, ...), custom_call_target="tpu_custom_call" | custom-call | tf_op jit(solution)/shard_map/pallas_call | solution.py:147
  98.5 4.2 %shard_map.73 = (f32[256,1024]{1,0:T(8,128)S(1)}, f32[64,1024]{1,0:T(8,128)S(1)}, f32[64,1024]{1,0:T(8,128)S(1)}, f32[64,1024]{1,0:T(8,128)S(1)}, f32[64,1024]{1,0:T(8,128)S(1)}) custom-call(s32[8]{0:T(128)S(1)} %stack.56.starts_ref, bf16[64,4096]{1,0:T(8,128)(2,1)S(1)} %collective-permute-done.17.refs_0_, ...), custom_call_target="tpu_custom_call" | custom-call | tf_op jit(solution)/shard_map/pallas_call | solution.py:147
  104.2 1.6 %collective-permute-start.30 = (bf16[1040,128]{1,0:T(8,128)(2,1)S(1)}, bf16[1040,128]{1,0:T(8,128)(2,1)S(1)}, u32[]{:S(2)}, u32[]{:S(2)}) collective-permute-start(bf16[1040,128]{1,0:T(8,128)(2,1)S(1)} %get-tuple-element.77), channel_id=1, source_target_pairs={{0,16},{8,24},{16,0},{24,8},{1,17},{9,25},{17,1},{25,9},{2,18},{10... | collective-permute-start | bytes 798728 | tf_op jit(solution)/shard_map/ppermute | solution.py:348
  106.2 1.3 %collective-permute-start.35 = (bf16[1040,128]{1,0:T(8,128)(2,1)S(1)}, bf16[1040,128]{1,0:T(8,128)(2,1)S(1)}, u32[]{:S(2)}, u32[]{:S(2)}) collective-permute-start(bf16[1040,128]{1,0:T(8,128)(2,1)S(1)} %get-tuple-element.86), channel_id=1, source_target_pairs={{0,16},{8,24},{16,0},{24,8},{1,17},{9,25},{17,1},{25,9},{2,18},{10... | collective-permute-start | bytes 798728 | tf_op jit(solution)/shard_map/ppermute | solution.py:348
  107.4 6.1 %collective-permute-done.30.refs_5_ = bf16[1040,128]{1,0:T(8,128)(2,1)S(1)} collective-permute-done((bf16[1040,128]{1,0:T(8,128)(2,1)S(1)}, bf16[1040,128]{1,0:T(8,128)(2,1)S(1)}, u32[]{:S(2)}, u32[]{:S(2)}) %collective-permute-start.30) | collective-permute-done | bytes 266272 | tf_op jit(solution)/shard_map/ppermute | solution.py:348
  113.5 4.8 %collective-permute-done.35.refs_7_ = bf16[1040,128]{1,0:T(8,128)(2,1)S(1)} collective-permute-done((bf16[1040,128]{1,0:T(8,128)(2,1)S(1)}, bf16[1040,128]{1,0:T(8,128)(2,1)S(1)}, u32[]{:S(2)}, u32[]{:S(2)}) %collective-permute-start.35) | collective-permute-done | bytes 266272 | tf_op jit(solution)/shard_map/ppermute | solution.py:348
  118.4 2.0 %shard_map.75 = f32[2,128,2048]{2,1,0:T(8,128)} custom-call(f32[128,1024]{1,0:T(8,128)S(1)} %get-tuple-element.56.refs_0_, bf16[1040,128]{1,0:T(8,128)(2,1)S(1)} %collective-permute-done.16.refs_1_, f32[128,1024]{1,0:T(8,128)S(1)} %get-tuple-element.66.refs_2_, bf16[1040,128]{1,0:T(8,128)(2,1)S(1)} %collective-permute-done.23.refs_3_, ...), custom_call_target="tpu_custom_call" | custom-call | tf_op jit(solution)/shard_map/pallas_call | solution.py:236
  (79 shorter events, 11.3 us)
Async XLA Ops:
  1.4 15.7 %collective-permute-start = (bf16[64,4096]{1,0:T(8,128)(2,1)S(1)}, bf16[64,4096]{1,0:T(8,128)(2,1)S(1)}, u32[]{:S(2)}, u32[]{:S(2)}) collective-permute-start(bf16[64,4096]{1,0:T(8,128)(2,1)S(1)} %get-tuple-element.90.refs_0_), channel_id=1, source_target_pairs={{0,2},{2,4},{4,6},{6,7},{7,5},{5,3},{3,1},{1,0},{8,10},{10,12},{12... | collective-permute-start | bytes 1572872 | tf_op jit(solution)/shard_map/ppermute | solution.py:299
  4.5 15.0 %collective-permute-start.3 = (bf16[64,4096]{1,0:T(8,128)(2,1)S(1)}, bf16[64,4096]{1,0:T(8,128)(2,1)}, u32[]{:S(2)}, u32[]{:S(2)}) collective-permute-start(bf16[64,4096]{1,0:T(8,128)(2,1)S(1)} %get-tuple-element.90.refs_0_), channel_id=1, source_target_pairs={{2,0},{4,2},{6,4},{7,6},{5,7},{3,5},{1,3},{0,1},{10,8},{12,10},{14... | collective-permute-start | bytes 1572872 | tf_op jit(solution)/shard_map/ppermute | solution.py:302
  4.5 23.9 %collective-permute-start.6 = (bf16[64,4096]{1,0:T(8,128)(2,1)S(1)}, bf16[64,4096]{1,0:T(8,128)(2,1)S(1)}, u32[]{:S(2)}, u32[]{:S(2)}) collective-permute-start(bf16[64,4096]{1,0:T(8,128)(2,1)S(1)} %get-tuple-element.89.refs_0_), channel_id=1, source_target_pairs={{0,2},{2,4},{4,6},{6,7},{7,5},{5,3},{3,1},{1,0},{8,10},{10,12},{12... | collective-permute-start | bytes 1572872 | tf_op jit(solution)/shard_map/ppermute | solution.py:299
  6.5 24.2 %collective-permute-start.7 = (bf16[64,4096]{1,0:T(8,128)(2,1)S(1)}, bf16[64,4096]{1,0:T(8,128)(2,1)}, u32[]{:S(2)}, u32[]{:S(2)}) collective-permute-start(bf16[64,4096]{1,0:T(8,128)(2,1)S(1)} %get-tuple-element.89.refs_0_), channel_id=1, source_target_pairs={{2,0},{4,2},{6,4},{7,6},{5,7},{3,5},{1,3},{0,1},{10,8},{12,10},{14... | collective-permute-start | bytes 1572872 | tf_op jit(solution)/shard_map/ppermute | solution.py:302
  17.2 22.5 %collective-permute-start.1 = (bf16[64,4096]{1,0:T(8,128)(2,1)S(1)}, bf16[64,4096]{1,0:T(8,128)(2,1)S(1)}, u32[]{:S(2)}, u32[]{:S(2)}) collective-permute-start(bf16[64,4096]{1,0:T(8,128)(2,1)S(1)} %collective-permute-done.refs_1_), channel_id=1, source_target_pairs={{0,2},{2,4},{4,6},{6,7},{7,5},{5,3},{3,1},{1,0},{8,10},{10,12},{12... | collective-permute-start | bytes 1572872 | tf_op jit(solution)/shard_map/ppermute | solution.py:299
  19.5 22.4 %collective-permute-start.4 = (bf16[64,4096]{1,0:T(8,128)(2,1)}, bf16[64,4096]{1,0:T(8,128)(2,1)S(1)}, u32[]{:S(2)}, u32[]{:S(2)}) collective-permute-start(bf16[64,4096]{1,0:T(8,128)(2,1)} %collective-permute-done.3.refs_2_), channel_id=1, source_target_pairs={{2,0},{4,2},{6,4},{7,6},{5,7},{3,5},{1,3},{0,1},{10,8},{12,10},{14... | collective-permute-start | bytes 1572872 | tf_op jit(solution)/shard_map/ppermute | solution.py:302
  28.4 23.4 %collective-permute-start.8 = (bf16[64,4096]{1,0:T(8,128)(2,1)S(1)}, bf16[64,4096]{1,0:T(8,128)(2,1)S(1)}, u32[]{:S(2)}, u32[]{:S(2)}) collective-permute-start(bf16[64,4096]{1,0:T(8,128)(2,1)S(1)} %collective-permute-done.6.refs_1_), channel_id=1, source_target_pairs={{0,2},{2,4},{4,6},{6,7},{7,5},{5,3},{3,1},{1,0},{8,10},{10,12},{12... | collective-permute-start | bytes 1572872 | tf_op jit(solution)/shard_map/ppermute | solution.py:299
  30.7 22.4 %collective-permute-start.9 = (bf16[64,4096]{1,0:T(8,128)(2,1)}, bf16[64,4096]{1,0:T(8,128)(2,1)S(1)}, u32[]{:S(2)}, u32[]{:S(2)}) collective-permute-start(bf16[64,4096]{1,0:T(8,128)(2,1)} %collective-permute-done.7.refs_2_), channel_id=1, source_target_pairs={{2,0},{4,2},{6,4},{7,6},{5,7},{3,5},{1,3},{0,1},{10,8},{12,10},{14... | collective-permute-start | bytes 1572872 | tf_op jit(solution)/shard_map/ppermute | solution.py:302
  39.7 21.6 %collective-permute-start.2 = (bf16[64,4096]{1,0:T(8,128)(2,1)S(1)}, bf16[64,4096]{1,0:T(8,128)(2,1)S(1)}, u32[]{:S(2)}, u32[]{:S(2)}) collective-permute-start(bf16[64,4096]{1,0:T(8,128)(2,1)S(1)} %collective-permute-done.1.refs_3_), channel_id=1, source_target_pairs={{0,2},{2,4},{4,6},{6,7},{7,5},{5,3},{3,1},{1,0},{8,10},{10,12},{12... | collective-permute-start | bytes 1572872 | tf_op jit(solution)/shard_map/ppermute | solution.py:299
  41.8 21.4 %collective-permute-start.5 = (bf16[64,4096]{1,0:T(8,128)(2,1)S(1)}, bf16[64,4096]{1,0:T(8,128)(2,1)S(1)}, u32[]{:S(2)}, u32[]{:S(2)}) collective-permute-start(bf16[64,4096]{1,0:T(8,128)(2,1)S(1)} %collective-permute-done.4.refs_4_), channel_id=1, source_target_pairs={{2,0},{4,2},{6,4},{7,6},{5,7},{3,5},{1,3},{0,1},{10,8},{12,10},{14... | collective-permute-start | bytes 1572872 | tf_op jit(solution)/shard_map/ppermute | solution.py:302
  61.3 7.5 %collective-permute-start.10 = (bf16[32,4096]{1,0:T(8,128)(2,1)S(1)}, bf16[32,4096]{1,0:T(8,128)(2,1)S(1)}, u32[]{:S(2)}, u32[]{:S(2)}) collective-permute-start(bf16[32,4096]{1,0:T(8,128)(2,1)S(1)} %slice.28), channel_id=1, source_target_pairs={{0,2},{2,4},{4,6},{6,7},{7,5},{5,3},{3,1},{1,0},{8,10},{10,12},{12... | collective-permute-start | bytes 786440 | tf_op jit(solution)/shard_map/ppermute | solution.py:299
  63.2 6.9 %collective-permute-start.11 = (bf16[32,4096]{1,0:T(8,128)(2,1)S(1)}, bf16[32,4096]{1,0:T(8,128)(2,1)S(1)}, u32[]{:S(2)}, u32[]{:S(2)}) collective-permute-start(bf16[32,4096]{1,0:T(8,128)(2,1)S(1)} %slice.29), channel_id=1, source_target_pairs={{2,0},{4,2},{6,4},{7,6},{5,7},{3,5},{1,3},{0,1},{10,8},{12,10},{14... | collective-permute-start | bytes 786440 | tf_op jit(solution)/shard_map/ppermute | solution.py:302
  70.2 12.4 %collective-permute-start.17 = (bf16[64,4096]{1,0:T(8,128)(2,1)S(1)}, bf16[64,4096]{1,0:T(8,128)(2,1)S(1)}, u32[]{:S(2)}, u32[]{:S(2)}) collective-permute-start(bf16[64,4096]{1,0:T(8,128)(2,1)S(1)} %collective-permute-done.8.refs_3_), channel_id=1, source_target_pairs={{0,2},{2,4},{4,6},{6,7},{7,5},{5,3},{3,1},{1,0},{8,10},{10,12},{12... | collective-permute-start | bytes 1572872 | tf_op jit(solution)/shard_map/ppermute | solution.py:299
  71.8 11.3 %collective-permute-start.18 = (bf16[64,4096]{1,0:T(8,128)(2,1)S(1)}, bf16[64,4096]{1,0:T(8,128)(2,1)S(1)}, u32[]{:S(2)}, u32[]{:S(2)}) collective-permute-start(bf16[64,4096]{1,0:T(8,128)(2,1)S(1)} %collective-permute-done.9.refs_4_), channel_id=1, source_target_pairs={{2,0},{4,2},{6,4},{7,6},{5,7},{3,5},{1,3},{0,1},{10,8},{12,10},{14... | collective-permute-start | bytes 1572872 | tf_op jit(solution)/shard_map/ppermute | solution.py:302
  76.5 5.0 %collective-permute-start.12 = (f32[64,1024]{1,0:T(8,128)S(1)}, f32[64,1024]{1,0:T(8,128)S(1)}, u32[]{:S(2)}, u32[]{:S(2)}) collective-permute-start(f32[64,1024]{1,0:T(8,128)S(1)} %get-tuple-element.52), channel_id=1, source_target_pairs={{0,8},{8,0},{16,24},{24,16},{1,9},{9,1},{17,25},{25,17},{2,10},{10... | collective-permute-start | bytes 786440 | tf_op jit(solution)/shard_map/ppermute | solution.py:333
  76.6 5.4 %collective-permute-start.13 = (f32[64,1024]{1,0:T(8,128)S(1)}, f32[64,1024]{1,0:T(8,128)S(1)}, u32[]{:S(2)}, u32[]{:S(2)}) collective-permute-start(f32[64,1024]{1,0:T(8,128)S(1)} %get-tuple-element.53), channel_id=1, source_target_pairs={{0,8},{8,0},{16,24},{24,16},{1,9},{9,1},{17,25},{25,17},{2,10},{10... | collective-permute-start | bytes 786440 | tf_op jit(solution)/shard_map/ppermute | solution.py:333
  77.1 5.0 %collective-permute-start.14 = (f32[64,1024]{1,0:T(8,128)S(1)}, f32[64,1024]{1,0:T(8,128)S(1)}, u32[]{:S(2)}, u32[]{:S(2)}) collective-permute-start(f32[64,1024]{1,0:T(8,128)S(1)} %get-tuple-element.54), channel_id=1, source_target_pairs={{0,8},{8,0},{16,24},{24,16},{1,9},{9,1},{17,25},{25,17},{2,10},{10... | collective-permute-start | bytes 786440 | tf_op jit(solution)/shard_map/ppermute | solution.py:333
  82.1 3.4 %collective-permute-start.20 = (f32[64,1024]{1,0:T(8,128)S(1)}, f32[64,1024]{1,0:T(8,128)S(1)}, u32[]{:S(2)}, u32[]{:S(2)}) collective-permute-start(f32[64,1024]{1,0:T(8,128)S(1)} %get-tuple-element.63), channel_id=1, source_target_pairs={{0,8},{8,0},{16,24},{24,16},{1,9},{9,1},{17,25},{25,17},{2,10},{10... | collective-permute-start | bytes 786440 | tf_op jit(solution)/shard_map/ppermute | solution.py:333
  82.5 4.6 %collective-permute-start.21 = (f32[64,1024]{1,0:T(8,128)S(1)}, f32[64,1024]{1,0:T(8,128)S(1)}, u32[]{:S(2)}, u32[]{:S(2)}) collective-permute-start(f32[64,1024]{1,0:T(8,128)S(1)} %get-tuple-element.64), channel_id=1, source_target_pairs={{0,8},{8,0},{16,24},{24,16},{1,9},{9,1},{17,25},{25,17},{2,10},{10... | collective-permute-start | bytes 786440 | tf_op jit(solution)/shard_map/ppermute | solution.py:333
  83.1 4.1 %collective-permute-start.22 = (f32[64,1024]{1,0:T(8,128)S(1)}, f32[64,1024]{1,0:T(8,128)S(1)}, u32[]{:S(2)}, u32[]{:S(2)}) collective-permute-start(f32[64,1024]{1,0:T(8,128)S(1)} %get-tuple-element.65), channel_id=1, source_target_pairs={{0,8},{8,0},{16,24},{24,16},{1,9},{9,1},{17,25},{25,17},{2,10},{10... | collective-permute-start | bytes 786440 | tf_op jit(solution)/shard_map/ppermute | solution.py:333
  83.2 8.7 %collective-permute-start.24 = (bf16[32,4096]{1,0:T(8,128)(2,1)S(1)}, bf16[32,4096]{1,0:T(8,128)(2,1)S(1)}, u32[]{:S(2)}, u32[]{:S(2)}) collective-permute-start(bf16[32,4096]{1,0:T(8,128)(2,1)S(1)} %slice.32), channel_id=1, source_target_pairs={{0,2},{2,4},{4,6},{6,7},{7,5},{5,3},{3,1},{1,0},{8,10},{10,12},{12... | collective-permute-start | bytes 786440 | tf_op jit(solution)/shard_map/ppermute | solution.py:299
  84.8 8.4 %collective-permute-start.25 = (bf16[32,4096]{1,0:T(8,128)(2,1)S(1)}, bf16[32,4096]{1,0:T(8,128)(2,1)S(1)}, u32[]{:S(2)}, u32[]{:S(2)}) collective-permute-start(bf16[32,4096]{1,0:T(8,128)(2,1)S(1)} %slice.33), channel_id=1, source_target_pairs={{2,0},{4,2},{6,4},{7,6},{5,7},{3,5},{1,3},{0,1},{10,8},{12,10},{14... | collective-permute-start | bytes 786440 | tf_op jit(solution)/shard_map/ppermute | solution.py:302
  85.5 12.6 %collective-permute-start.16 = (bf16[1040,128]{1,0:T(8,128)(2,1)S(1)}, bf16[1040,128]{1,0:T(8,128)(2,1)S(1)}, u32[]{:S(2)}, u32[]{:S(2)}) collective-permute-start(bf16[1040,128]{1,0:T(8,128)(2,1)S(1)} %get-tuple-element.57), channel_id=1, source_target_pairs={{0,16},{8,24},{16,0},{24,8},{1,17},{9,25},{17,1},{25,9},{2,18},{10... | collective-permute-start | bytes 798728 | tf_op jit(solution)/shard_map/ppermute | solution.py:341
  87.5 15.3 %collective-permute-start.23 = (bf16[1040,128]{1,0:T(8,128)(2,1)S(1)}, bf16[1040,128]{1,0:T(8,128)(2,1)S(1)}, u32[]{:S(2)}, u32[]{:S(2)}) collective-permute-start(bf16[1040,128]{1,0:T(8,128)(2,1)S(1)} %get-tuple-element.67), channel_id=1, source_target_pairs={{0,16},{8,24},{16,0},{24,8},{1,17},{9,25},{17,1},{25,9},{2,18},{10... | collective-permute-start | bytes 798728 | tf_op jit(solution)/shard_map/ppermute | solution.py:341
  97.4 5.5 %collective-permute-start.26 = (f32[64,1024]{1,0:T(8,128)S(1)}, f32[64,1024]{1,0:T(8,128)S(1)}, u32[]{:S(2)}, u32[]{:S(2)}) collective-permute-start(f32[64,1024]{1,0:T(8,128)S(1)} %get-tuple-element.72), channel_id=1, source_target_pairs={{0,8},{8,0},{16,24},{24,16},{1,9},{9,1},{17,25},{25,17},{2,10},{10... | collective-permute-start | bytes 786440 | tf_op jit(solution)/shard_map/ppermute | solution.py:333
  97.5 5.9 %collective-permute-start.27 = (f32[64,1024]{1,0:T(8,128)S(1)}, f32[64,1024]{1,0:T(8,128)S(1)}, u32[]{:S(2)}, u32[]{:S(2)}) collective-permute-start(f32[64,1024]{1,0:T(8,128)S(1)} %get-tuple-element.73), channel_id=1, source_target_pairs={{0,8},{8,0},{16,24},{24,16},{1,9},{9,1},{17,25},{25,17},{2,10},{10... | collective-permute-start | bytes 786440 | tf_op jit(solution)/shard_map/ppermute | solution.py:333
  98.0 5.4 %collective-permute-start.28 = (f32[64,1024]{1,0:T(8,128)S(1)}, f32[64,1024]{1,0:T(8,128)S(1)}, u32[]{:S(2)}, u32[]{:S(2)}) collective-permute-start(f32[64,1024]{1,0:T(8,128)S(1)} %get-tuple-element.74), channel_id=1, source_target_pairs={{0,8},{8,0},{16,24},{24,16},{1,9},{9,1},{17,25},{25,17},{2,10},{10... | collective-permute-start | bytes 786440 | tf_op jit(solution)/shard_map/ppermute | solution.py:333
  98.1 5.8 %collective-permute-start.29 = (f32[64,1024]{1,0:T(8,128)S(1)}, f32[64,1024]{1,0:T(8,128)S(1)}, u32[]{:S(2)}, u32[]{:S(2)}) collective-permute-start(f32[64,1024]{1,0:T(8,128)S(1)} %get-tuple-element.75), channel_id=1, source_target_pairs={{0,8},{8,0},{16,24},{24,16},{1,9},{9,1},{17,25},{25,17},{2,10},{10... | collective-permute-start | bytes 786440 | tf_op jit(solution)/shard_map/ppermute | solution.py:333
  102.8 3.0 %collective-permute-start.31 = (f32[64,1024]{1,0:T(8,128)S(1)}, f32[64,1024]{1,0:T(8,128)S(1)}, u32[]{:S(2)}, u32[]{:S(2)}) collective-permute-start(f32[64,1024]{1,0:T(8,128)S(1)} %get-tuple-element.81), channel_id=1, source_target_pairs={{0,8},{8,0},{16,24},{24,16},{1,9},{9,1},{17,25},{25,17},{2,10},{10... | collective-permute-start | bytes 786440 | tf_op jit(solution)/shard_map/ppermute | solution.py:333
  102.9 2.9 %collective-permute-start.32 = (f32[64,1024]{1,0:T(8,128)S(1)}, f32[64,1024]{1,0:T(8,128)S(1)}, u32[]{:S(2)}, u32[]{:S(2)}) collective-permute-start(f32[64,1024]{1,0:T(8,128)S(1)} %get-tuple-element.82), channel_id=1, source_target_pairs={{0,8},{8,0},{16,24},{24,16},{1,9},{9,1},{17,25},{25,17},{2,10},{10... | collective-permute-start | bytes 786440 | tf_op jit(solution)/shard_map/ppermute | solution.py:333
  104.2 9.3 %collective-permute-start.30 = (bf16[1040,128]{1,0:T(8,128)(2,1)S(1)}, bf16[1040,128]{1,0:T(8,128)(2,1)S(1)}, u32[]{:S(2)}, u32[]{:S(2)}) collective-permute-start(bf16[1040,128]{1,0:T(8,128)(2,1)S(1)} %get-tuple-element.77), channel_id=1, source_target_pairs={{0,16},{8,24},{16,0},{24,8},{1,17},{9,25},{17,1},{25,9},{2,18},{10... | collective-permute-start | bytes 798728 | tf_op jit(solution)/shard_map/ppermute | solution.py:348
  106.2 12.2 %collective-permute-start.35 = (bf16[1040,128]{1,0:T(8,128)(2,1)S(1)}, bf16[1040,128]{1,0:T(8,128)(2,1)S(1)}, u32[]{:S(2)}, u32[]{:S(2)}) collective-permute-start(bf16[1040,128]{1,0:T(8,128)(2,1)S(1)} %get-tuple-element.86), channel_id=1, source_target_pairs={{0,16},{8,24},{16,0},{24,8},{1,17},{9,25},{17,1},{25,9},{2,18},{10... | collective-permute-start | bytes 798728 | tf_op jit(solution)/shard_map/ppermute | solution.py:348
  (10 other events, 55.7 us)

commit v4 on v3

v4 whole, which is shorter than its diff:
```python
import functools

import jax
import jax.numpy as jnp
from jax import lax
from jax.experimental import pallas as pl
from jax.experimental.pallas import tpu as pltpu
from jax.sharding import PartitionSpec as P

F32, BF16 = jnp.float32, jnp.bfloat16
COLS, LANES = 512, 128
PIECES, SPLITS = 4, 2
COST = pl.CostEstimate(flops=0, bytes_accessed=0, transcendentals=0)
KERNEL_BYTES = 10 * 2**20
OCTAVES, LOWEST = 248.0, -124.0


VMEM = pl.BlockSpec(memory_space=pltpu.VMEM)


def params():
    return pltpu.CompilerParams(vmem_limit_bytes=KERNEL_BYTES)


def split(value):
    high = value.astype(BF16)
    return high, (value - high.astype(F32)).astype(BF16)


def dot(left, right):
    return jnp.dot(left, right, preferred_element_type=F32)


def gather_rows(piece_refs, rows_ref):
    top = 0
    for ref in piece_refs:
        rows_ref[top : top + ref.shape[0]] = ref[...]
        top += ref.shape[0]


def by_spans(ref, body, unrolled=False):
    if unrolled:
        for start in range(0, ref.shape[1], COLS):
            body(start)
        return

    def step(j, carry):
        body(pl.multiple_of(j * COLS, COLS))
        return carry

    lax.fori_loop(0, ref.shape[1] // COLS, step, 0)


def take_off(starts_ref, piece_refs, rows_ref, held_ref, columns, rhs_ref):
    terms = dot(rows_ref[...], held_ref[:, columns])
    top = 0
    for i, ref in enumerate(piece_refs):
        count = ref.shape[0]
        place = pl.ds(pl.multiple_of(starts_ref[i], 16), count)
        rhs_ref[place, columns] = rhs_ref[place, columns] - terms[top : top + count]
        top += count


def first_kernel(n, starts_ref, *refs):
    pieces, (solved_ref, *refs) = refs[: 2 * n], refs[2 * n :]
    cov_refs, rhs_refs, (held_ref, rows_ref, sems) = refs[:2], refs[2:4], refs[4:]
    steps = held_ref.shape[1] // COLS

    def copy(j):
        columns = pl.ds(pl.multiple_of(j * COLS, COLS), COLS)
        return pltpu.make_async_copy(solved_ref.at[:, columns], held_ref.at[:, columns], sems.at[j])

    copy(0).start()
    copy(1).start()
    gather_rows(pieces, rows_ref)
    count, rows = pieces[0].shape[0], cov_refs[0].shape[0]

    def body(j, carry):
        columns = pl.ds(pl.multiple_of(j * COLS, COLS), COLS)
        for cov_ref, rhs_ref in zip(cov_refs, rhs_refs):
            rhs_ref[:, columns] = jnp.zeros((rhs_ref.shape[0], COLS), F32)
            rhs_ref[pl.ds(pl.multiple_of(starts_ref[n], 16), rows), columns] = cov_ref[:, columns]
        copy(j).wait()

        @pl.when(j + 2 < steps)
        def _():
            copy(j + 2).start()

        terms = dot(rows_ref[...], held_ref[:, columns])
        for i in range(2 * n):
            place = pl.ds(pl.multiple_of(starts_ref[i % n], 16), count)
            rhs_ref = rhs_refs[i // n]
            rhs_ref[place, columns] = rhs_ref[place, columns] - terms[i * count : (i + 1) * count]
        return carry

    lax.fori_loop(0, steps, body, 0)


def first(starts, pieces, solved, cov_a, cov_b, size):
    depth, width = solved.shape
    rows = sum(piece.shape[0] for piece in pieces)
    hbm = pl.BlockSpec(memory_space=pltpu.HBM)
    return pl.pallas_call(
        functools.partial(first_kernel, len(pieces) // 2),
        in_specs=[pl.BlockSpec(memory_space=pltpu.SMEM)] + [VMEM] * len(pieces) + [hbm, VMEM, VMEM],
        out_specs=[VMEM] * 3,
        out_shape=[pltpu.VMEM((size, width), F32)] * 2 + [pltpu.VMEM((depth, width), BF16)],
        scratch_shapes=[pltpu.VMEM((rows, depth), BF16), pltpu.SemaphoreType.DMA((width // COLS,))],
        compiler_params=params(),
        cost_estimate=COST,
    )(starts, *pieces, pltpu.with_memory_space_constraint(solved, pltpu.HBM), cov_a, cov_b)


def more_kernel(starts_ref, *refs):
    *piece_refs, held_ref, given_ref, rhs_ref, rows_ref = refs
    del given_ref
    gather_rows(piece_refs, rows_ref)

    def body(start):
        take_off(starts_ref, piece_refs, rows_ref, held_ref, pl.ds(start, COLS), rhs_ref)

    by_spans(held_ref, body)


def more(starts, pieces, held, rhs):
    rows = sum(piece.shape[0] for piece in pieces)
    return pl.pallas_call(
        more_kernel,
        in_specs=[pl.BlockSpec(memory_space=pltpu.SMEM)] + [VMEM] * (len(pieces) + 2),
        out_specs=VMEM,
        out_shape=pltpu.VMEM(rhs.shape, F32),
        input_output_aliases={len(pieces) + 2: 0},
        scratch_shapes=[pltpu.VMEM((rows, held.shape[0]), BF16)],
        compiler_params=params(),
        cost_estimate=COST,
    )(starts, *pieces, held, rhs)


def product(pair_ref, high, low, top, count, end):
    size = high.shape[0]
    wide, fine = pair_ref[top : top + count, :end], pair_ref[size + top : size + top + count, :end]
    return dot(wide, high[:end]) + dot(wide, low[:end]) + dot(fine, high[:end])


def solve_kernel(full, rhs_ref, pair_ref, *refs):
    *base_refs, out_ref = refs
    size, width = rhs_ref.shape
    block = size // 2

    def body(start):
        columns = pl.ds(start, COLS)
        high, low = split(rhs_ref[:, columns])
        for top in (0, block):
            place = slice(top, top + block)
            value = product(pair_ref, high, low, top, block, size if full else top + block)
            for base_ref in base_refs:
                value = value + base_ref[place, columns]
            out_ref[place, columns] = value

    by_spans(rhs_ref, body)


def solve(rhs, base, pair, full):
    given = [rhs, pair] + ([] if base is None else [base])
    return pl.pallas_call(
        functools.partial(solve_kernel, full),
        in_specs=[VMEM] * len(given),
        out_specs=[VMEM],
        out_shape=[pltpu.VMEM(rhs.shape, F32)],
        input_output_aliases={} if base is None else {2: 0},
        compiler_params=params(),
        cost_estimate=COST,
    )(*given)


def last_kernel(n, sends, at, starts_ref, *refs):
    refs = list(refs)
    piece_refs, refs = refs[:n], refs[n:]
    held_ref, sum_ref, matrix_ref, *refs = refs
    *refs, rows_ref, stack_ref, out_ref = refs
    keep_ref, *send_refs = refs[: sends + 1]
    parts_refs = refs[sends + 1 :]
    size = sum_ref.shape[0]
    block, count = size // 2, size // DEVICES
    few = block // sends
    gather_rows(piece_refs, rows_ref)
    rows = rows_ref.shape[0]

    def body(start):
        here, columns = pl.ds(start, COLS), pl.ds(at + start, COLS)
        high, low = split(dot(rows_ref[...], held_ref[:, columns]))
        for k, part in enumerate((high, low, high)):
            stack_ref[k * rows : (k + 1) * rows] = part
        for parts_ref in parts_refs:
            parts_ref[:, here] = stack_ref[...]
        value = sum_ref[:, columns] - dot(matrix_ref[...], stack_ref[...])
        for d in range(DEVICES):
            out_ref[pl.ds(pl.multiple_of(starts_ref[d], 16), count)] = value[d * count : (d + 1) * count]
        keep_ref[:, here] = out_ref[:block]
        for i, send_ref in enumerate(send_refs):
            send_ref[:, here] = out_ref[block + i * few : block + (i + 1) * few]

    by_spans(keep_ref, body, True)


def last(starts, pieces, held, total, matrix, at, width, sends, gives_parts):
    depth = held.shape[0]
    rows, size = sum(piece.shape[0] for piece in pieces), total.shape[0]
    given = [held, total, matrix]
    outs = [pltpu.VMEM((size // 2, width), F32)] + [pltpu.VMEM((size // 2 // sends, width), F32)] * sends
    if gives_parts:
        outs.append(pltpu.VMEM((3 * rows, width), BF16))
    return pl.pallas_call(
        functools.partial(last_kernel, len(pieces), sends, at),
        in_specs=[pl.BlockSpec(memory_space=pltpu.SMEM)] + [VMEM] * (len(pieces) + len(given)),
        out_specs=[VMEM] * len(outs),
        out_shape=outs,
        scratch_shapes=[
            pltpu.VMEM((rows, depth), BF16),
            pltpu.VMEM((matrix.shape[1], COLS), BF16),
            pltpu.VMEM((size, COLS), F32),
        ],
        compiler_params=params(),
        cost_estimate=COST,
    )(starts, *pieces, *given)


def less_kernel(sum_ref, matrix_ref, *refs):
    *part_refs, out_ref = refs
    at = 0
    for part_ref in part_refs:

        def body(start, part_ref=part_ref, at=at):
            columns = pl.ds(at + start, COLS)
            out_ref[:, columns] = sum_ref[:, columns] - dot(matrix_ref[...], part_ref[:, pl.ds(start, COLS)])

        by_spans(part_ref, body, True)
        at += part_ref.shape[1]


def less(total, matrix, parts):
    return pl.pallas_call(
        less_kernel,
        in_specs=[VMEM] * (2 + len(parts)),
        out_specs=VMEM,
        out_shape=pltpu.VMEM(total.shape, F32),
        input_output_aliases={0: 0},
        compiler_params=params(),
        cost_estimate=COST,
    )(total, matrix, *parts)


def pack_kernel(parts, *refs):
    *refs, own_ref, coded_ref = refs
    count = own_ref.shape[0]
    blocks = own_ref.shape[1] // LANES
    tops, block = [], 0
    for i in range(parts):
        keep_ref, *got_refs = refs[i * len(refs) // parts : (i + 1) * len(refs) // parts]
        near, far = got_refs[: len(got_refs) // 2], got_refs[len(got_refs) // 2 :]
        few, width = near[0].shape
        for k, ref in enumerate(near):
            rows = slice(k * few, (k + 1) * few)
            own_ref[rows, block * LANES : block * LANES + width] = keep_ref[rows] + ref[...]
        for start in range(0, width, LANES):
            columns = slice(start, start + LANES)
            value = keep_ref[count:, columns] + jnp.concatenate([ref[:, columns] for ref in far])
            size = jnp.abs(value)
            top = jnp.maximum(jnp.max(size, axis=0, keepdims=True) * 1.01, 1e-30).astype(BF16)
            level = jnp.minimum(size / top.astype(F32), 1.0) * OCTAVES + LOWEST
            coded = jnp.exp2(level)
            coded_ref[block * count : (block + 1) * count] = jnp.where(value < 0, -coded, coded).astype(BF16)
            tops.append(top)
            block += 1
    spare = coded_ref.shape[0] - blocks * (count + 1)
    if spare:
        tops.append(jnp.ones((spare, LANES), BF16))
    coded_ref[blocks * count :] = jnp.concatenate(tops)


def pack(parts):
    count, width = parts[0][0].shape[0] // 2, sum(keep.shape[1] for keep, _ in parts)
    blocks = width // LANES
    given = [array for keep, got in parts for array in (keep, *got)]
    return pl.pallas_call(
        functools.partial(pack_kernel, len(parts)),
        in_specs=[VMEM] * len(given),
        out_specs=[VMEM] * 2,
        out_shape=[pltpu.VMEM((count, width), F32), pltpu.VMEM((blocks * count + -(-blocks // 16) * 16, LANES), BF16)],
        compiler_params=params(),
        cost_estimate=COST,
    )(*given)


def unpack_kernel(*refs):
    *refs, out_ref = refs
    count = out_ref.shape[1]
    at = 0
    for own_ref, got_ref in zip(refs[::2], refs[1::2]):
        blocks = own_ref.shape[1] // LANES
        tops = got_ref[blocks * count :].astype(F32) * (1.0 / OCTAVES)
        for i in range(blocks):
            coded = got_ref[i * count : (i + 1) * count].astype(F32)
            size = jnp.maximum(jnp.log2(jnp.abs(coded)) - LOWEST, 0.0) * tops[i : i + 1]
            value = own_ref[:, i * LANES : (i + 1) * LANES] + jnp.where(coded < 0, -size, size)
            out_ref[at // out_ref.shape[2], :, at % out_ref.shape[2] : at % out_ref.shape[2] + LANES] = value
            at += LANES


def unpack(sums):
    count, width = sums[0][0].shape[0], sum(own.shape[1] for own, _ in sums) // 2
    return pl.pallas_call(
        unpack_kernel,
        in_specs=[VMEM] * (2 * len(sums)),
        out_specs=VMEM,
        out_shape=jax.ShapeDtypeStruct((2, count, width), F32),
        compiler_params=params(),
        cost_estimate=COST,
    )(*[array for pair in sums for array in pair])


def mult(left, right):
    return jnp.dot(left, right, preferred_element_type=F32, precision=lax.Precision.HIGHEST)


def general(cross_cov, prev_rows, prev_solved, sub_block, inv_first, inv_second):
    terms = jnp.einsum(
        "kra,ac->krc",
        lax.all_gather(prev_rows, "pcol", axis=1, tiled=True),
        prev_solved,
        preferred_element_type=F32,
    )
    update = lax.psum_scatter(terms, "prow", scatter_dimension=1, tiled=True)
    reduced = lax.all_gather(cross_cov - update, "prow", axis=1, tiled=True)
    first = mult(inv_first, reduced[0])
    second = mult(inv_second, reduced[1] - mult(sub_block, first))
    rows = cross_cov.shape[1]
    return lax.dynamic_slice_in_dim(jnp.stack([first, second]), lax.axis_index("prow") * rows, rows, 1)


RING = (0, 2, 4, 6, 7, 5, 3, 1)
N = len(RING)
AHEAD = [(RING[i], RING[(i + 1) % N]) for i in range(N)]
BACK = [(RING[(i + 1) % N], RING[i]) for i in range(N)]
DEVICES = 4
SWAP_CORE = [(p, p ^ 1) for p in range(DEVICES)]
SWAP_Y = [(p, p ^ 2) for p in range(DEVICES)]


def halves(matrix):
    high = lax.reduce_precision(matrix, 8, 7)
    return jnp.concatenate([high, matrix - high]).astype(BF16)


def after(value, *others):
    return lax.optimization_barrier((value, *others))[0]


def fast(cross_cov, prev_rows, prev_solved, sub_block, inv_first, inv_second):
    p, q = lax.axis_index("prow"), lax.axis_index("pcol")
    rows, block = cross_cov.shape[1], prev_rows.shape[1]
    half = block // 2
    spot = jnp.where(q % 2 == 0, q // 2, N - 1 - q // 2)

    def rows_of(steps, part=0):
        there = (spot + steps) % N
        return jnp.where(there < N // 2, 2 * there, 2 * (N - 1 - there) + 1) * block + part * half

    def starts(*values):
        return jnp.stack([jnp.asarray(v, jnp.int32) for v in values])

    size = N * block

    def ahead(x):
        return lax.ppermute(x, "pcol", AHEAD)

    def back(x):
        return lax.ppermute(x, "pcol", BACK)

    own_a, own_b = prev_rows[0], prev_rows[1]
    fa, ba, fb, bb = [own_a], [own_a], [own_b], [own_b]

    def step(flow, move, *others):
        flow.append(move(after(flow[-1], *others)))

    for f, b in ((fa, ba), (fb, bb)):
        step(f, ahead)
        step(b, back)

    cross = -mult(inv_second, mult(sub_block, inv_first))
    matrices = [halves(inv_first), halves(cross), halves(inv_second)]
    rest = jnp.concatenate([rows_of(steps) + jnp.arange(block) for steps in (-3, 3, 4)])
    chosen = jnp.arange(size)[:, None] == rest[None]
    columns = [dot(matrix, chosen.astype(BF16)).astype(BF16) for matrix in matrices]
    columns = [jnp.concatenate([c[:size], c[:size], c[size:]], 1) for c in columns]
    slots = starts(*[((d % 2 != p % 2) * 2 + (d // 2 != p // 2)) * rows for d in range(DEVICES)])
    place = starts(rows_of(-2), rows_of(2))
    first_place = after(starts(rows_of(0), rows_of(-1), rows_of(1), p * rows), slots, place, *columns, *matrices)

    step(fa, ahead)
    step(ba, back)
    step(fb, ahead)
    step(bb, back)
    known = [own_a, fa[1], ba[1], own_b, fb[1], bb[1]]
    rhs_a, rhs_b, held = first(first_place, known, prev_solved, cross_cov[0], cross_cov[1], size)
    step(fa, ahead, held)
    step(ba, back, held)
    rhs_a = more(place, [fa[2], ba[2]], held, rhs_a)
    sum_a, = solve(rhs_a, None, matrices[0], False)
    base, = solve(rhs_a, None, matrices[1], True)
    rhs_b = more(after(place, sum_a, base), [fb[2], bb[2]], held, rhs_b)
    fa.append(ahead(after(fa[3], rhs_b)[:half]))
    ba.append(back(after(ba[3], rhs_b)[half:]))
    sum_b, = solve(after(rhs_b, fa[3], ba[3]), base, matrices[2], False)
    step(fb, ahead, fa[4], ba[4], sum_b)
    step(bb, back, fa[4], ba[4], sum_b)
    fb.append(ahead(fb[3][:half]))
    bb.append(back(bb[3][half:]))
    last_b = [fb[3], bb[3], fb[4], bb[4]]

    width = cross_cov.shape[2]

    def across(sends):
        return [lax.ppermute(send, "prow", SWAP_CORE) for send in sends]

    part = width // SPLITS
    halves_a, parts = [], []
    for i in range(SPLITS):
        ready = after(slots, sum_b)
        keep, *sends, given = last(ready, [fa[3], ba[3], fa[4], ba[4]], held, sum_a, columns[0], i * part, part, PIECES, True)
        halves_a.append((keep, across(sends)))
        parts.append(given)
    sum_b = less(sum_b, columns[1], parts)
    keep, got = halves_a[0]
    halves_a[0] = after(keep, fb[3], bb[3]), got
    own, coded = pack(halves_a)
    sums = [(own, lax.ppermute(coded, "prow", SWAP_Y))]
    for i in range(SPLITS):
        keep, *sends = last(after(slots, coded), last_b, held, sum_b, columns[2], i * part, part, PIECES, False)
        own, coded = pack([(after(keep, *([got for _, got in sums] if i else [])), across(sends))])
        sums.append((own, lax.ppermute(coded, "prow", SWAP_Y)))
    return unpack(sums)


def solution(mesh):
    sizes = dict(mesh.shape)
    return jax.shard_map(
        fast if (sizes["prow"], sizes["pcol"]) == (DEVICES, N) else general,
        mesh=mesh,
        in_specs=(
            P(None, "prow", "pcol"),
            P(None, "pcol", "prow"),
            P("prow", "pcol"),
            P(),
            P(),
            P(),
        ),
        out_specs=P(None, "prow", "pcol"),
        check_vma=False,
    )
```

time: 121 us -> 118 us (0.975)
  waiting for transfers between devices: 42.2 us -> 32 us
  Pallas kernels: 40.7 us -> 48.7 us
    ppermute x8, waiting for transfers between devices: 26.6 us -> 5.04 us  [ahead(): return lax.ppermute(x, 'pcol', AHEAD)]
    ppermute x8, starting transfers between devices: 1.17 us -> 15.3 us  [back(): return lax.ppermute(x, 'pcol', BACK)]
    ppermute x8, starting transfers between devices: 16.6 us -> 2.55 us  [ahead(): return lax.ppermute(x, 'pcol', AHEAD)]
    ppermute x8, waiting for transfers between devices: 4.6 us -> 16.7 us  [back(): return lax.ppermute(x, 'pcol', BACK)]
    ppermute x18 -> x17, waiting for transfers between devices: 11 us -> 1.67 us  [the longest x16 1.67 us: across(): return [lax.ppermute(send, 'prow', SWAP_CORE) for send in sends]]
    ppermute x2, waiting for transfers between devices: 0.01 us -> 8.63 us  [fast(): sums.append((own, lax.ppermute(coded, 'prow', SWAP_Y)))]
    pallas_call x11 -> x14, Pallas kernels: 38.7 us -> 46.7 us  [the longest x4 14.6 us: last(): pl.pallas_call(functools.partial(last_kernel, len(pieces), sends, at), in...]
    dot_general x2, matrix products: 6.04 us -> 3.77 us  [mult(): jnp.dot(left, right, preferred_element_type=F32, precision=lax.Precision....]
  transfers between devices with their start and end apart: 36 -> 35, of which waited for: 15 -> 16; matrix products, arithmetic and copies ran while one was open for 7% -> 7% of each run, Pallas kernels for 32% -> 39%
where the time goes in v4:
time: 118 us; the launch traced here: 117 us
  Pallas kernels  48.7 us (41%)
  waiting for transfers between devices  32 us (27%)
  starting transfers between devices  26.5 us (22%)
  matrix products  5.23 us (4%)
  other arithmetic  2.75 us (2%)
  local copies, waits for them, and re-layouts  1.85 us (2%)
    ppermute x8, waiting for transfers between devices, back(): return lax.ppermute(x, 'pcol', BACK)  16.7 us
    ppermute x8, starting transfers between devices, back(): return lax.ppermute(x, 'pcol', BACK)  15.3 us
    pallas_call x4, Pallas kernels, last(): pl.pallas_call(functools.partial(last_kernel, len(pieces), sends, at), in...  14.6 us
    pallas_call x1, Pallas kernels, first(): pl.pallas_call(functools.partial(first_kernel, len(pieces) // 2), in_spec...  11.2 us
    pallas_call x3, Pallas kernels, solve(): pl.pallas_call(functools.partial(solve_kernel, full), in_specs=[VMEM] * l...  10.5 us
    ppermute x2, waiting for transfers between devices, fast(): sums.append((own, lax.ppermute(coded, 'prow', SWAP_Y)))  8.63 us
    pallas_call x2, Pallas kernels, more(): pl.pallas_call(more_kernel, in_specs=[pl.BlockSpec(memory_space=pltpu.SME...  7.08 us
    ppermute x8, waiting for transfers between devices, ahead(): return lax.ppermute(x, 'pcol', AHEAD)  5.04 us
  transfers between devices with their start and end apart: 35, of which 16 were waited for; matrix products, arithmetic and copies ran while one was open for 7% of the time, Pallas kernels for 39%

profile of v4, /device:TPU:0, one launch (start us, length us, event | category | flops | bytes accessed | tf_op | source)
XLA Modules:
  0.0 117.4 jit_solution(12845094193173968755)
XLA Ops:
  1.4 3.0 %collective-permute-start.2 = (bf16[64,4096]{1,0:T(8,128)(2,1)S(1)}, bf16[64,4096]{1,0:T(8,128)(2,1)}, u32[]{:S(2)}, u32[]{:S(2)}) collective-permute-start(bf16[64,4096]{1,0:T(8,128)(2,1)S(1)} %get-tuple-element.98.refs_0_), channel_id=1, source_target_pairs={{2,0},{4,2},{6,4},{7,6},{5,7},{3,5},{1,3},{0,1},{10,8},{12,10},{14... | collective-permute-start | bytes 1572872 | tf_op jit(solution)/shard_map/ppermute | solution.py:378
  4.5 1.9 %collective-permute-start.5 = (bf16[64,4096]{1,0:T(8,128)(2,1)S(1)}, bf16[64,4096]{1,0:T(8,128)(2,1)S(1)}, u32[]{:S(2)}, u32[]{:S(2)}) collective-permute-start(bf16[64,4096]{1,0:T(8,128)(2,1)S(1)} %get-tuple-element.97.refs_3_), channel_id=1, source_target_pairs={{2,0},{4,2},{6,4},{7,6},{5,7},{3,5},{1,3},{0,1},{10,8},{12,10},{14... | collective-permute-start | bytes 1572872 | tf_op jit(solution)/shard_map/ppermute | solution.py:378
  6.6 1.5 %reduce-precision_convert_fusion.2 = (bf16[512,512]{1,0:T(8,128)(2,1)S(1)}, bf16[512,512]{1,0:T(8,128)(2,1)S(1)}) fusion(f32[512,512]{1,0:T(8,128)} %param.10), kind=kLoop, calls=%fused_computation.5 | loop fusion | flops 1048576 | bytes 2097152 | tf_op jit(solution)/shard_map/convert.4
  8.1 1.8 %fusion.10 = f32[512,512]{1,0:T(8,128)S(1)} fusion(f32[512,512]{1,0:T(8,128)S(1)} %copy-done, f32[512,512]{1,0:T(8,128)S(1)} %copy-done.2), kind=kOutput, calls=%fused_computation.38 | convolution fusion | flops 1610612736 | bytes 3145728 | tf_op jit(solution)/shard_map/dot_general | solution.py:323
  10.1 1.9 %reduce-precision_convert_fusion.1 = (bf16[512,512]{1,0:T(8,128)(2,1)S(1)}, bf16[512,512]{1,0:T(8,128)(2,1)S(1)}) fusion(f32[512,512]{1,0:T(8,128)S(1)} %fusion.10, f32[512,512]{1,0:T(8,128)S(1)} %copy-done.3), kind=kOutput, calls=%fused_computation.3 | convolution fusion | flops 1611923456 | bytes 3145728 | tf_op jit(solution)/shard_map/dot_general | solution.py:323
  14.8 2.5 %collective-permute-done.2.refs_2_ = bf16[64,4096]{1,0:T(8,128)(2,1)} collective-permute-done((bf16[64,4096]{1,0:T(8,128)(2,1)S(1)}, bf16[64,4096]{1,0:T(8,128)(2,1)}, u32[]{:S(2)}, u32[]{:S(2)}) %collective-permute-start.2) | collective-permute-done | bytes 524320 | tf_op jit(solution)/shard_map/ppermute | solution.py:378
  17.3 2.0 %collective-permute-start.3 = (bf16[64,4096]{1,0:T(8,128)(2,1)}, bf16[64,4096]{1,0:T(8,128)(2,1)S(1)}, u32[]{:S(2)}, u32[]{:S(2)}) collective-permute-start(bf16[64,4096]{1,0:T(8,128)(2,1)} %collective-permute-done.2.refs_2_), channel_id=1, source_target_pairs={{2,0},{4,2},{6,4},{7,6},{5,7},{3,5},{1,3},{0,1},{10,8},{12,10},{14... | collective-permute-start | bytes 1572872 | tf_op jit(solution)/shard_map/ppermute | solution.py:378
  19.7 8.8 %collective-permute-done.5.refs_5_ = bf16[64,4096]{1,0:T(8,128)(2,1)S(1)} collective-permute-done((bf16[64,4096]{1,0:T(8,128)(2,1)S(1)}, bf16[64,4096]{1,0:T(8,128)(2,1)S(1)}, u32[]{:S(2)}, u32[]{:S(2)}) %collective-permute-start.5) | collective-permute-done | bytes 524320 | tf_op jit(solution)/shard_map/ppermute | solution.py:378
  28.4 2.0 %collective-permute-start.7 = (bf16[64,4096]{1,0:T(8,128)(2,1)S(1)}, bf16[64,4096]{1,0:T(8,128)(2,1)S(1)}, u32[]{:S(2)}, u32[]{:S(2)}) collective-permute-start(bf16[64,4096]{1,0:T(8,128)(2,1)S(1)} %collective-permute-done.5.refs_5_), channel_id=1, source_target_pairs={{2,0},{4,2},{6,4},{7,6},{5,7},{3,5},{1,3},{0,1},{10,8},{12,10},{14... | collective-permute-start | bytes 1572872 | tf_op jit(solution)/shard_map/ppermute | solution.py:378
  30.6 11.2 %shard_map.64 = (f32[512,2048]{1,0:T(8,128)S(1)}, f32[512,2048]{1,0:T(8,128)S(1)}, bf16[4096,2048]{1,0:T(8,128)(2,1)S(1)}) custom-call(s32[4]{0:T(128)S(1)} %get-tuple-element.50.starts_ref, bf16[64,4096]{1,0:T(8,128)(2,1)S(1)} %get-tuple-element.98.refs_0_, bf16[64,4096]{1,0:T(8,128)(2,1)} %collective-permute-done.refs_1_, ...), custom_call_target="tpu_custom_call" | custom-call | tf_op jit(solution)/shard_map/pallas_call | solution.py:103
  41.8 2.0 %collective-permute-start.9 = (bf16[64,4096]{1,0:T(8,128)(2,1)S(1)}, bf16[64,4096]{1,0:T(8,128)(2,1)S(1)}, u32[]{:S(2)}, u32[]{:S(2)}) collective-permute-start(bf16[64,4096]{1,0:T(8,128)(2,1)S(1)} %collective-permute-done.3.refs_1_), channel_id=1, source_target_pairs={{2,0},{4,2},{6,4},{7,6},{5,7},{3,5},{1,3},{0,1},{10,8},{12,10},{14... | collective-permute-start | bytes 1572872 | tf_op jit(solution)/shard_map/ppermute | solution.py:378
  44.1 3.5 %shard_map.65.rhs_ref = f32[512,2048]{1,0:T(8,128)S(1)} custom-call(s32[2]{0:T(128)S(1)} %pad_add_fusion.2.starts_ref, bf16[64,4096]{1,0:T(8,128)(2,1)S(1)} %collective-permute-done.1.refs_0_, bf16[64,4096]{1,0:T(8,128)(2,1)S(1)} %collective-permute-done.3.refs_1_, ...), custom_call_target="tpu_custom_call", output_to_operand_aliasing={{}: (4, {})} | custom-call | tf_op jit(solution)/shard_map/pallas_call | solution.py:127
  47.6 3.2 %shard_map.66.refs_5_ = f32[512,2048]{1,0:T(8,128)S(1)} custom-call(f32[512,2048]{1,0:T(8,128)S(1)} %shard_map.65.rhs_ref, bf16[1024,512]{1,0:T(8,128)(2,1)S(1)} %get-tuple-element.113.pair_ref), custom_call_target="tpu_custom_call" | custom-call | tf_op jit(solution)/shard_map/pallas_call | solution.py:165
  50.8 4.0 %shard_map.67.refs_0_ = f32[512,2048]{1,0:T(8,128)S(1)} custom-call(f32[512,2048]{1,0:T(8,128)S(1)} %shard_map.65.rhs_ref, bf16[1024,512]{1,0:T(8,128)(2,1)S(1)} %get-tuple-element.114.pair_ref), custom_call_target="tpu_custom_call" | custom-call | tf_op jit(solution)/shard_map/pallas_call | solution.py:165
  54.9 3.5 %shard_map.68.rhs_ref = f32[512,2048]{1,0:T(8,128)S(1)} custom-call(s32[2]{0:T(128)S(1)} %pad_add_fusion.2.starts_ref, bf16[64,4096]{1,0:T(8,128)(2,1)S(1)} %collective-permute-done.6.refs_0_, bf16[64,4096]{1,0:T(8,128)(2,1)S(1)} %collective-permute-done.7.refs_1_, ...), custom_call_target="tpu_custom_call", output_to_operand_aliasing={{}: (4, {})} | custom-call | tf_op jit(solution)/shard_map/pallas_call | solution.py:127
  58.4 2.9 %collective-permute-done.9.refs_1_ = bf16[64,4096]{1,0:T(8,128)(2,1)S(1)} collective-permute-done((bf16[64,4096]{1,0:T(8,128)(2,1)S(1)}, bf16[64,4096]{1,0:T(8,128)(2,1)S(1)}, u32[]{:S(2)}, u32[]{:S(2)}) %collective-permute-start.9) | collective-permute-done | bytes 524320 | tf_op jit(solution)/shard_map/ppermute | solution.py:378
  62.8 1.6 %collective-permute-start.11 = (bf16[32,4096]{1,0:T(8,128)(2,1)S(1)}, bf16[32,4096]{1,0:T(8,128)(2,1)S(1)}, u32[]{:S(2)}, u32[]{:S(2)}) collective-permute-start(bf16[32,4096]{1,0:T(8,128)(2,1)S(1)} %slice.56), channel_id=1, source_target_pairs={{2,0},{4,2},{6,4},{7,6},{5,7},{3,5},{1,3},{0,1},{10,8},{12,10},{14... | collective-permute-start | bytes 786440 | tf_op jit(solution)/shard_map/ppermute | solution.py:378
  64.8 3.3 %shard_map.69.sum_ref = f32[512,2048]{1,0:T(8,128)S(1)} custom-call(f32[512,2048]{1,0:T(8,128)S(1)} %shard_map.68.rhs_ref, bf16[1024,512]{1,0:T(8,128)(2,1)S(1)} %pad_maximum_fusion.2.pair_ref, f32[512,2048]{1,0:T(8,128)S(1)} %shard_map.67.refs_0_), custom_call_target="tpu_custom_call", output_to_operand_aliasing={{}: (2, {})} | custom-call | tf_op jit(solution)/shard_map/pallas_call | solution.py:165
  68.1 1.6 %collective-permute-done.11.refs_3_ = bf16[32,4096]{1,0:T(8,128)(2,1)S(1)} collective-permute-done((bf16[32,4096]{1,0:T(8,128)(2,1)S(1)}, bf16[32,4096]{1,0:T(8,128)(2,1)S(1)}, u32[]{:S(2)}, u32[]{:S(2)}) %collective-permute-start.11) | collective-permute-done | bytes 262176 | tf_op jit(solution)/shard_map/ppermute | solution.py:378
  71.4 1.6 %collective-permute-start.13 = (bf16[64,4096]{1,0:T(8,128)(2,1)S(1)}, bf16[64,4096]{1,0:T(8,128)(2,1)S(1)}, u32[]{:S(2)}, u32[]{:S(2)}) collective-permute-start(bf16[64,4096]{1,0:T(8,128)(2,1)S(1)} %collective-permute-done.7.refs_1_), channel_id=1, source_target_pairs={{2,0},{4,2},{6,4},{7,6},{5,7},{3,5},{1,3},{0,1},{10,8},{12,10},{14... | collective-permute-start | bytes 1572872 | tf_op jit(solution)/shard_map/ppermute | solution.py:378
  73.0 3.7 %shard_map.71 = (f32[256,1024]{1,0:T(8,128)S(1)}, f32[64,1024]{1,0:T(8,128)S(1)}, f32[64,1024]{1,0:T(8,128)S(1)}, f32[64,1024]{1,0:T(8,128)S(1)}, f32[64,1024]{1,0:T(8,128)S(1)}, /*index=5*/bf16[576,1024]{1,0:T(8,128)(2,1)S(1)}) custom-call(s32[4]{0:T(128)S(1)} %get-tuple-element.86.starts_ref, bf16[64,4096]{1,0:T(8,128)(2,1)S(1)} %collective-permute-done.8.refs_0_, ...), custom_call_target="tpu_custom_call" | custom-call | tf_op jit(solution)/shard_map/pallas_call | solution.py:213
  77.3 3.7 %shard_map.70 = (f32[256,1024]{1,0:T(8,128)S(1)}, f32[64,1024]{1,0:T(8,128)S(1)}, f32[64,1024]{1,0:T(8,128)S(1)}, f32[64,1024]{1,0:T(8,128)S(1)}, f32[64,1024]{1,0:T(8,128)S(1)}, /*index=5*/bf16[576,1024]{1,0:T(8,128)(2,1)S(1)}) custom-call(s32[4]{0:T(128)S(1)} %get-tuple-element.86.starts_ref, bf16[64,4096]{1,0:T(8,128)(2,1)S(1)} %collective-permute-done.8.refs_0_, ...), custom_call_target="tpu_custom_call" | custom-call | tf_op jit(solution)/shard_map/pallas_call | solution.py:213
  85.5 1.6 %collective-permute-start.22 = (bf16[2064,128]{1,0:T(8,128)(2,1)S(1)}, bf16[2064,128]{1,0:T(8,128)(2,1)S(1)}, u32[]{:S(2)}, u32[]{:S(2)}) collective-permute-start(bf16[2064,128]{1,0:T(8,128)(2,1)S(1)} %get-tuple-element.75), channel_id=1, source_target_pairs={{0,16},{8,24},{16,0},{24,8},{1,17},{9,25},{17,1},{25,9},{2,18},{10... | collective-permute-start | bytes 1585160 | tf_op jit(solution)/shard_map/ppermute | solution.py:437
  87.1 2.1 %shard_map.73.refs_5_ = f32[512,2048]{1,0:T(8,128)S(1)} custom-call(f32[512,2048]{1,0:T(8,128)S(1)} %shard_map.69.sum_ref, bf16[512,576]{1,0:T(8,128)(2,1)S(1)} %pad_maximum_fusion.4.matrix_ref, bf16[576,1024]{1,0:T(8,128)(2,1)S(1)} %get-tuple-element.77.refs_0_, bf16[576,1024]{1,0:T(8,128)(2,1)S(1)} %get-tuple-element.78.refs_1_), custom_call_target="tpu_custom_call", output_to_operand_aliasing={{}: (0, {})} | custom-call | tf_op jit(solution)/shard_map/pallas_call | solution.py:242
  89.2 2.0 %collective-permute-done.23.refs_2_ = bf16[32,4096]{1,0:T(8,128)(2,1)S(1)} collective-permute-done((bf16[32,4096]{1,0:T(8,128)(2,1)S(1)}, bf16[32,4096]{1,0:T(8,128)(2,1)S(1)}, u32[]{:S(2)}, u32[]{:S(2)}) %collective-permute-start.23) | collective-permute-done | bytes 262176 | tf_op jit(solution)/shard_map/ppermute | solution.py:375
  92.0 3.6 %shard_map.74 = (f32[256,1024]{1,0:T(8,128)S(1)}, f32[64,1024]{1,0:T(8,128)S(1)}, f32[64,1024]{1,0:T(8,128)S(1)}, f32[64,1024]{1,0:T(8,128)S(1)}, f32[64,1024]{1,0:T(8,128)S(1)}) custom-call(s32[4]{0:T(128)S(1)} %get-tuple-element.86.starts_ref, bf16[64,4096]{1,0:T(8,128)(2,1)S(1)} %collective-permute-done.12.refs_0_, ...), custom_call_target="tpu_custom_call" | custom-call | tf_op jit(solution)/shard_map/pallas_call | solution.py:213
  98.7 1.5 %collective-permute-start.29 = (bf16[1040,128]{1,0:T(8,128)(2,1)S(1)}, bf16[1040,128]{1,0:T(8,128)(2,1)S(1)}, u32[]{:S(2)}, u32[]{:S(2)}) collective-permute-start(bf16[1040,128]{1,0:T(8,128)(2,1)S(1)} %get-tuple-element.85), channel_id=1, source_target_pairs={{0,16},{8,24},{16,0},{24,8},{1,17},{9,25},{17,1},{25,9},{2,18},{10... | collective-permute-start | bytes 798728 | tf_op jit(solution)/shard_map/ppermute | solution.py:441
  100.2 3.6 %shard_map.76 = (f32[256,1024]{1,0:T(8,128)S(1)}, f32[64,1024]{1,0:T(8,128)S(1)}, f32[64,1024]{1,0:T(8,128)S(1)}, f32[64,1024]{1,0:T(8,128)S(1)}, f32[64,1024]{1,0:T(8,128)S(1)}) custom-call(s32[4]{0:T(128)S(1)} %get-tuple-element.86.starts_ref, bf16[64,4096]{1,0:T(8,128)(2,1)S(1)} %collective-permute-done.12.refs_0_, ...), custom_call_target="tpu_custom_call" | custom-call | tf_op jit(solution)/shard_map/pallas_call | solution.py:213
  104.9 2.3 %collective-permute-done.29.refs_3_ = bf16[1040,128]{1,0:T(8,128)(2,1)S(1)} collective-permute-done((bf16[1040,128]{1,0:T(8,128)(2,1)S(1)}, bf16[1040,128]{1,0:T(8,128)(2,1)S(1)}, u32[]{:S(2)}, u32[]{:S(2)}) %collective-permute-start.29) | collective-permute-done | bytes 266272 | tf_op jit(solution)/shard_map/ppermute | solution.py:441
  107.6 1.5 %collective-permute-start.34 = (bf16[1040,128]{1,0:T(8,128)(2,1)S(1)}, bf16[1040,128]{1,0:T(8,128)(2,1)S(1)}, u32[]{:S(2)}, u32[]{:S(2)}) collective-permute-start(bf16[1040,128]{1,0:T(8,128)(2,1)S(1)} %get-tuple-element.94), channel_id=1, source_target_pairs={{0,16},{8,24},{16,0},{24,8},{1,17},{9,25},{17,1},{25,9},{2,18},{10... | collective-permute-start | bytes 798728 | tf_op jit(solution)/shard_map/ppermute | solution.py:441
  109.1 6.4 %collective-permute-done.34.refs_5_ = bf16[1040,128]{1,0:T(8,128)(2,1)S(1)} collective-permute-done((bf16[1040,128]{1,0:T(8,128)(2,1)S(1)}, bf16[1040,128]{1,0:T(8,128)(2,1)S(1)}, u32[]{:S(2)}, u32[]{:S(2)}) %collective-permute-start.34) | collective-permute-done | bytes 266272 | tf_op jit(solution)/shard_map/ppermute | solution.py:441
  115.4 2.0 %shard_map.78 = f32[2,128,2048]{2,1,0:T(8,128)} custom-call(f32[128,2048]{1,0:T(8,128)S(1)} %get-tuple-element.74.refs_0_, bf16[2064,128]{1,0:T(8,128)(2,1)S(1)} %collective-permute-done.22.refs_1_, f32[128,1024]{1,0:T(8,128)S(1)} %get-tuple-element.84.refs_2_, bf16[1040,128]{1,0:T(8,128)(2,1)S(1)} %collective-permute-done.29.refs_3_, ...), custom_call_target="tpu_custom_call" | custom-call | tf_op jit(solution)/shard_map/pallas_call | solution.py:312
  (89 shorter events, 19.5 us)
Async XLA Ops:
  1.4 15.9 %collective-permute-start.2 = (bf16[64,4096]{1,0:T(8,128)(2,1)S(1)}, bf16[64,4096]{1,0:T(8,128)(2,1)}, u32[]{:S(2)}, u32[]{:S(2)}) collective-permute-start(bf16[64,4096]{1,0:T(8,128)(2,1)S(1)} %get-tuple-element.98.refs_0_), channel_id=1, source_target_pairs={{2,0},{4,2},{6,4},{7,6},{5,7},{3,5},{1,3},{0,1},{10,8},{12,10},{14... | collective-permute-start | bytes 1572872 | tf_op jit(solution)/shard_map/ppermute | solution.py:378
  4.4 15.0 %collective-permute-start = (bf16[64,4096]{1,0:T(8,128)(2,1)S(1)}, bf16[64,4096]{1,0:T(8,128)(2,1)}, u32[]{:S(2)}, u32[]{:S(2)}) collective-permute-start(bf16[64,4096]{1,0:T(8,128)(2,1)S(1)} %get-tuple-element.98.refs_0_), channel_id=1, source_target_pairs={{0,2},{2,4},{4,6},{6,7},{7,5},{5,3},{3,1},{1,0},{8,10},{10,12},{12... | collective-permute-start | bytes 1572872 | tf_op jit(solution)/shard_map/ppermute | solution.py:375
  4.5 23.9 %collective-permute-start.5 = (bf16[64,4096]{1,0:T(8,128)(2,1)S(1)}, bf16[64,4096]{1,0:T(8,128)(2,1)S(1)}, u32[]{:S(2)}, u32[]{:S(2)}) collective-permute-start(bf16[64,4096]{1,0:T(8,128)(2,1)S(1)} %get-tuple-element.97.refs_3_), channel_id=1, source_target_pairs={{2,0},{4,2},{6,4},{7,6},{5,7},{3,5},{1,3},{0,1},{10,8},{12,10},{14... | collective-permute-start | bytes 1572872 | tf_op jit(solution)/shard_map/ppermute | solution.py:378
  6.4 24.1 %collective-permute-start.4 = (bf16[64,4096]{1,0:T(8,128)(2,1)S(1)}, bf16[64,4096]{1,0:T(8,128)(2,1)S(1)}, u32[]{:S(2)}, u32[]{:S(2)}) collective-permute-start(bf16[64,4096]{1,0:T(8,128)(2,1)S(1)} %get-tuple-element.97.refs_3_), channel_id=1, source_target_pairs={{0,2},{2,4},{4,6},{6,7},{7,5},{5,3},{3,1},{1,0},{8,10},{10,12},{12... | collective-permute-start | bytes 1572872 | tf_op jit(solution)/shard_map/ppermute | solution.py:375
  17.3 24.4 %collective-permute-start.3 = (bf16[64,4096]{1,0:T(8,128)(2,1)}, bf16[64,4096]{1,0:T(8,128)(2,1)S(1)}, u32[]{:S(2)}, u32[]{:S(2)}) collective-permute-start(bf16[64,4096]{1,0:T(8,128)(2,1)} %collective-permute-done.2.refs_2_), channel_id=1, source_target_pairs={{2,0},{4,2},{6,4},{7,6},{5,7},{3,5},{1,3},{0,1},{10,8},{12,10},{14... | collective-permute-start | bytes 1572872 | tf_op jit(solution)/shard_map/ppermute | solution.py:378
  19.3 24.4 %collective-permute-start.1 = (bf16[64,4096]{1,0:T(8,128)(2,1)}, bf16[64,4096]{1,0:T(8,128)(2,1)S(1)}, u32[]{:S(2)}, u32[]{:S(2)}) collective-permute-start(bf16[64,4096]{1,0:T(8,128)(2,1)} %collective-permute-done.refs_1_), channel_id=1, source_target_pairs={{0,2},{2,4},{4,6},{6,7},{7,5},{5,3},{3,1},{1,0},{8,10},{10,12},{12... | collective-permute-start | bytes 1572872 | tf_op jit(solution)/shard_map/ppermute | solution.py:375
  28.4 26.4 %collective-permute-start.7 = (bf16[64,4096]{1,0:T(8,128)(2,1)S(1)}, bf16[64,4096]{1,0:T(8,128)(2,1)S(1)}, u32[]{:S(2)}, u32[]{:S(2)}) collective-permute-start(bf16[64,4096]{1,0:T(8,128)(2,1)S(1)} %collective-permute-done.5.refs_5_), channel_id=1, source_target_pairs={{2,0},{4,2},{6,4},{7,6},{5,7},{3,5},{1,3},{0,1},{10,8},{12,10},{14... | collective-permute-start | bytes 1572872 | tf_op jit(solution)/shard_map/ppermute | solution.py:378
  30.5 24.4 %collective-permute-start.6 = (bf16[64,4096]{1,0:T(8,128)(2,1)S(1)}, bf16[64,4096]{1,0:T(8,128)(2,1)S(1)}, u32[]{:S(2)}, u32[]{:S(2)}) collective-permute-start(bf16[64,4096]{1,0:T(8,128)(2,1)S(1)} %collective-permute-done.4.refs_4_), channel_id=1, source_target_pairs={{0,2},{2,4},{4,6},{6,7},{7,5},{5,3},{3,1},{1,0},{8,10},{10,12},{12... | collective-permute-start | bytes 1572872 | tf_op jit(solution)/shard_map/ppermute | solution.py:375
  41.8 19.6 %collective-permute-start.9 = (bf16[64,4096]{1,0:T(8,128)(2,1)S(1)}, bf16[64,4096]{1,0:T(8,128)(2,1)S(1)}, u32[]{:S(2)}, u32[]{:S(2)}) collective-permute-start(bf16[64,4096]{1,0:T(8,128)(2,1)S(1)} %collective-permute-done.3.refs_1_), channel_id=1, source_target_pairs={{2,0},{4,2},{6,4},{7,6},{5,7},{3,5},{1,3},{0,1},{10,8},{12,10},{14... | collective-permute-start | bytes 1572872 | tf_op jit(solution)/shard_map/ppermute | solution.py:378
  43.7 19.0 %collective-permute-start.8 = (bf16[64,4096]{1,0:T(8,128)(2,1)S(1)}, bf16[64,4096]{1,0:T(8,128)(2,1)S(1)}, u32[]{:S(2)}, u32[]{:S(2)}) collective-permute-start(bf16[64,4096]{1,0:T(8,128)(2,1)S(1)} %collective-permute-done.1.refs_0_), channel_id=1, source_target_pairs={{0,2},{2,4},{4,6},{6,7},{7,5},{5,3},{3,1},{1,0},{8,10},{10,12},{12... | collective-permute-start | bytes 1572872 | tf_op jit(solution)/shard_map/ppermute | solution.py:375
  62.8 6.9 %collective-permute-start.11 = (bf16[32,4096]{1,0:T(8,128)(2,1)S(1)}, bf16[32,4096]{1,0:T(8,128)(2,1)S(1)}, u32[]{:S(2)}, u32[]{:S(2)}) collective-permute-start(bf16[32,4096]{1,0:T(8,128)(2,1)S(1)} %slice.56), channel_id=1, source_target_pairs={{2,0},{4,2},{6,4},{7,6},{5,7},{3,5},{1,3},{0,1},{10,8},{12,10},{14... | collective-permute-start | bytes 786440 | tf_op jit(solution)/shard_map/ppermute | solution.py:378
  64.4 6.6 %collective-permute-start.10 = (bf16[32,4096]{1,0:T(8,128)(2,1)S(1)}, bf16[32,4096]{1,0:T(8,128)(2,1)S(1)}, u32[]{:S(2)}, u32[]{:S(2)}) collective-permute-start(bf16[32,4096]{1,0:T(8,128)(2,1)S(1)} %slice.55), channel_id=1, source_target_pairs={{0,2},{2,4},{4,6},{6,7},{7,5},{5,3},{3,1},{1,0},{8,10},{10,12},{12... | collective-permute-start | bytes 786440 | tf_op jit(solution)/shard_map/ppermute | solution.py:375
  71.0 11.3 %collective-permute-start.12 = (bf16[64,4096]{1,0:T(8,128)(2,1)S(1)}, bf16[64,4096]{1,0:T(8,128)(2,1)S(1)}, u32[]{:S(2)}, u32[]{:S(2)}) collective-permute-start(bf16[64,4096]{1,0:T(8,128)(2,1)S(1)} %collective-permute-done.6.refs_0_), channel_id=1, source_target_pairs={{0,2},{2,4},{4,6},{6,7},{7,5},{5,3},{3,1},{1,0},{8,10},{10,12},{12... | collective-permute-start | bytes 1572872 | tf_op jit(solution)/shard_map/ppermute | solution.py:375
  71.4 11.0 %collective-permute-start.13 = (bf16[64,4096]{1,0:T(8,128)(2,1)S(1)}, bf16[64,4096]{1,0:T(8,128)(2,1)S(1)}, u32[]{:S(2)}, u32[]{:S(2)}) collective-permute-start(bf16[64,4096]{1,0:T(8,128)(2,1)S(1)} %collective-permute-done.7.refs_1_), channel_id=1, source_target_pairs={{2,0},{4,2},{6,4},{7,6},{5,7},{3,5},{1,3},{0,1},{10,8},{12,10},{14... | collective-permute-start | bytes 1572872 | tf_op jit(solution)/shard_map/ppermute | solution.py:378
  76.6 4.3 %collective-permute-start.18 = (f32[64,1024]{1,0:T(8,128)S(1)}, f32[64,1024]{1,0:T(8,128)S(1)}, u32[]{:S(2)}, u32[]{:S(2)}) collective-permute-start(f32[64,1024]{1,0:T(8,128)S(1)} %get-tuple-element.70), channel_id=1, source_target_pairs={{0,8},{8,0},{16,24},{24,16},{1,9},{9,1},{17,25},{25,17},{2,10},{10... | collective-permute-start | bytes 786440 | tf_op jit(solution)/shard_map/ppermute | solution.py:424
  76.7 4.7 %collective-permute-start.19 = (f32[64,1024]{1,0:T(8,128)S(1)}, f32[64,1024]{1,0:T(8,128)S(1)}, u32[]{:S(2)}, u32[]{:S(2)}) collective-permute-start(f32[64,1024]{1,0:T(8,128)S(1)} %get-tuple-element.71), channel_id=1, source_target_pairs={{0,8},{8,0},{16,24},{24,16},{1,9},{9,1},{17,25},{25,17},{2,10},{10... | collective-permute-start | bytes 786440 | tf_op jit(solution)/shard_map/ppermute | solution.py:424
  77.2 4.3 %collective-permute-start.20 = (f32[64,1024]{1,0:T(8,128)S(1)}, f32[64,1024]{1,0:T(8,128)S(1)}, u32[]{:S(2)}, u32[]{:S(2)}) collective-permute-start(f32[64,1024]{1,0:T(8,128)S(1)} %get-tuple-element.72), channel_id=1, source_target_pairs={{0,8},{8,0},{16,24},{24,16},{1,9},{9,1},{17,25},{25,17},{2,10},{10... | collective-permute-start | bytes 786440 | tf_op jit(solution)/shard_map/ppermute | solution.py:424
  81.5 2.1 %collective-permute-start.14 = (f32[64,1024]{1,0:T(8,128)S(1)}, f32[64,1024]{1,0:T(8,128)S(1)}, u32[]{:S(2)}, u32[]{:S(2)}) collective-permute-start(f32[64,1024]{1,0:T(8,128)S(1)} %get-tuple-element.65), channel_id=1, source_target_pairs={{0,8},{8,0},{16,24},{24,16},{1,9},{9,1},{17,25},{25,17},{2,10},{10... | collective-permute-start | bytes 786440 | tf_op jit(solution)/shard_map/ppermute | solution.py:424
  81.6 3.3 %collective-permute-start.15 = (f32[64,1024]{1,0:T(8,128)S(1)}, f32[64,1024]{1,0:T(8,128)S(1)}, u32[]{:S(2)}, u32[]{:S(2)}) collective-permute-start(f32[64,1024]{1,0:T(8,128)S(1)} %get-tuple-element.66), channel_id=1, source_target_pairs={{0,8},{8,0},{16,24},{24,16},{1,9},{9,1},{17,25},{25,17},{2,10},{10... | collective-permute-start | bytes 786440 | tf_op jit(solution)/shard_map/ppermute | solution.py:424
  82.2 2.7 %collective-permute-start.16 = (f32[64,1024]{1,0:T(8,128)S(1)}, f32[64,1024]{1,0:T(8,128)S(1)}, u32[]{:S(2)}, u32[]{:S(2)}) collective-permute-start(f32[64,1024]{1,0:T(8,128)S(1)} %get-tuple-element.67), channel_id=1, source_target_pairs={{0,8},{8,0},{16,24},{24,16},{1,9},{9,1},{17,25},{25,17},{2,10},{10... | collective-permute-start | bytes 786440 | tf_op jit(solution)/shard_map/ppermute | solution.py:424
  82.4 2.5 %collective-permute-start.17 = (f32[64,1024]{1,0:T(8,128)S(1)}, f32[64,1024]{1,0:T(8,128)S(1)}, u32[]{:S(2)}, u32[]{:S(2)}) collective-permute-start(f32[64,1024]{1,0:T(8,128)S(1)} %get-tuple-element.68), channel_id=1, source_target_pairs={{0,8},{8,0},{16,24},{24,16},{1,9},{9,1},{17,25},{25,17},{2,10},{10... | collective-permute-start | bytes 786440 | tf_op jit(solution)/shard_map/ppermute | solution.py:424
  82.8 8.4 %collective-permute-start.23 = (bf16[32,4096]{1,0:T(8,128)(2,1)S(1)}, bf16[32,4096]{1,0:T(8,128)(2,1)S(1)}, u32[]{:S(2)}, u32[]{:S(2)}) collective-permute-start(bf16[32,4096]{1,0:T(8,128)(2,1)S(1)} %slice.65), channel_id=1, source_target_pairs={{0,2},{2,4},{4,6},{6,7},{7,5},{5,3},{3,1},{1,0},{8,10},{10,12},{12... | collective-permute-start | bytes 786440 | tf_op jit(solution)/shard_map/ppermute | solution.py:375
  83.6 8.4 %collective-permute-start.24 = (bf16[32,4096]{1,0:T(8,128)(2,1)S(1)}, bf16[32,4096]{1,0:T(8,128)(2,1)S(1)}, u32[]{:S(2)}, u32[]{:S(2)}) collective-permute-start(bf16[32,4096]{1,0:T(8,128)(2,1)S(1)} %slice.66), channel_id=1, source_target_pairs={{2,0},{4,2},{6,4},{7,6},{5,7},{3,5},{1,3},{0,1},{10,8},{12,10},{14... | collective-permute-start | bytes 786440 | tf_op jit(solution)/shard_map/ppermute | solution.py:378
  85.5 19.0 %collective-permute-start.22 = (bf16[2064,128]{1,0:T(8,128)(2,1)S(1)}, bf16[2064,128]{1,0:T(8,128)(2,1)S(1)}, u32[]{:S(2)}, u32[]{:S(2)}) collective-permute-start(bf16[2064,128]{1,0:T(8,128)(2,1)S(1)} %get-tuple-element.75), channel_id=1, source_target_pairs={{0,16},{8,24},{16,0},{24,8},{1,17},{9,25},{17,1},{25,9},{2,18},{10... | collective-permute-start | bytes 1585160 | tf_op jit(solution)/shard_map/ppermute | solution.py:437
  95.8 1.9 %collective-permute-start.26 = (f32[64,1024]{1,0:T(8,128)S(1)}, f32[64,1024]{1,0:T(8,128)S(1)}, u32[]{:S(2)}, u32[]{:S(2)}) collective-permute-start(f32[64,1024]{1,0:T(8,128)S(1)} %get-tuple-element.81), channel_id=1, source_target_pairs={{0,8},{8,0},{16,24},{24,16},{1,9},{9,1},{17,25},{25,17},{2,10},{10... | collective-permute-start | bytes 786440 | tf_op jit(solution)/shard_map/ppermute | solution.py:424
  96.3 2.1 %collective-permute-start.28 = (f32[64,1024]{1,0:T(8,128)S(1)}, f32[64,1024]{1,0:T(8,128)S(1)}, u32[]{:S(2)}, u32[]{:S(2)}) collective-permute-start(f32[64,1024]{1,0:T(8,128)S(1)} %get-tuple-element.83), channel_id=1, source_target_pairs={{0,8},{8,0},{16,24},{24,16},{1,9},{9,1},{17,25},{25,17},{2,10},{10... | collective-permute-start | bytes 786440 | tf_op jit(solution)/shard_map/ppermute | solution.py:424
  98.7 8.5 %collective-permute-start.29 = (bf16[1040,128]{1,0:T(8,128)(2,1)S(1)}, bf16[1040,128]{1,0:T(8,128)(2,1)S(1)}, u32[]{:S(2)}, u32[]{:S(2)}) collective-permute-start(bf16[1040,128]{1,0:T(8,128)(2,1)S(1)} %get-tuple-element.85), channel_id=1, source_target_pairs={{0,16},{8,24},{16,0},{24,8},{1,17},{9,25},{17,1},{25,9},{2,18},{10... | collective-permute-start | bytes 798728 | tf_op jit(solution)/shard_map/ppermute | solution.py:441
  103.9 3.4 %collective-permute-start.30 = (f32[64,1024]{1,0:T(8,128)S(1)}, f32[64,1024]{1,0:T(8,128)S(1)}, u32[]{:S(2)}, u32[]{:S(2)}) collective-permute-start(f32[64,1024]{1,0:T(8,128)S(1)} %get-tuple-element.89), channel_id=1, source_target_pairs={{0,8},{8,0},{16,24},{24,16},{1,9},{9,1},{17,25},{25,17},{2,10},{10... | collective-permute-start | bytes 786440 | tf_op jit(solution)/shard_map/ppermute | solution.py:424
  103.9 3.3 %collective-permute-start.31 = (f32[64,1024]{1,0:T(8,128)S(1)}, f32[64,1024]{1,0:T(8,128)S(1)}, u32[]{:S(2)}, u32[]{:S(2)}) collective-permute-start(f32[64,1024]{1,0:T(8,128)S(1)} %get-tuple-element.90), channel_id=1, source_target_pairs={{0,8},{8,0},{16,24},{24,16},{1,9},{9,1},{17,25},{25,17},{2,10},{10... | collective-permute-start | bytes 786440 | tf_op jit(solution)/shard_map/ppermute | solution.py:424
  104.4 2.8 %collective-permute-start.32 = (f32[64,1024]{1,0:T(8,128)S(1)}, f32[64,1024]{1,0:T(8,128)S(1)}, u32[]{:S(2)}, u32[]{:S(2)}) collective-permute-start(f32[64,1024]{1,0:T(8,128)S(1)} %get-tuple-element.91), channel_id=1, source_target_pairs={{0,8},{8,0},{16,24},{24,16},{1,9},{9,1},{17,25},{25,17},{2,10},{10... | collective-permute-start | bytes 786440 | tf_op jit(solution)/shard_map/ppermute | solution.py:424
  104.5 2.7 %collective-permute-start.33 = (f32[64,1024]{1,0:T(8,128)S(1)}, f32[64,1024]{1,0:T(8,128)S(1)}, u32[]{:S(2)}, u32[]{:S(2)}) collective-permute-start(f32[64,1024]{1,0:T(8,128)S(1)} %get-tuple-element.92), channel_id=1, source_target_pairs={{0,8},{8,0},{16,24},{24,16},{1,9},{9,1},{17,25},{25,17},{2,10},{10... | collective-permute-start | bytes 786440 | tf_op jit(solution)/shard_map/ppermute | solution.py:424
  107.6 7.8 %collective-permute-start.34 = (bf16[1040,128]{1,0:T(8,128)(2,1)S(1)}, bf16[1040,128]{1,0:T(8,128)(2,1)S(1)}, u32[]{:S(2)}, u32[]{:S(2)}) collective-permute-start(bf16[1040,128]{1,0:T(8,128)(2,1)S(1)} %get-tuple-element.94), channel_id=1, source_target_pairs={{0,16},{8,24},{16,0},{24,8},{1,17},{9,25},{17,1},{25,9},{2,18},{10... | collective-permute-start | bytes 798728 | tf_op jit(solution)/shard_map/ppermute | solution.py:441
  (8 other events, 23.4 us)

commit v5 on v4

--- a/solution.py
+++ b/solution.py
@@ -292,31 +292,45 @@
     )(*given)
 
 
-def unpack_kernel(*refs):
-    *refs, out_ref = refs
-    count = out_ref.shape[1]
-    at = 0
-    for own_ref, got_ref in zip(refs[::2], refs[1::2]):
-        blocks = own_ref.shape[1] // LANES
-        tops = got_ref[blocks * count :].astype(F32) * (1.0 / OCTAVES)
-        for i in range(blocks):
-            coded = got_ref[i * count : (i + 1) * count].astype(F32)
-            size = jnp.maximum(jnp.log2(jnp.abs(coded)) - LOWEST, 0.0) * tops[i : i + 1]
-            value = own_ref[:, i * LANES : (i + 1) * LANES] + jnp.where(coded < 0, -size, size)
-            out_ref[at // out_ref.shape[2], :, at % out_ref.shape[2] : at % out_ref.shape[2] + LANES] = value
-            at += LANES
+def unpack_kernel(panel, first, own_ref, got_ref, *refs):
+    *_, out_ref, value_ref, sems = refs
+    count, width = own_ref.shape
+    blocks = width // LANES
+    tops = got_ref[blocks * count :].astype(F32) * (1.0 / OCTAVES)
+    copies = []
+    for i in range(blocks):
+        coded = got_ref[i * count : (i + 1) * count].astype(F32)
+        size = jnp.maximum(jnp.log2(jnp.abs(coded)) - LOWEST, 0.0) * tops[i : i + 1]
+        columns = slice(i * LANES, (i + 1) * LANES)
+        value_ref[:, columns] = own_ref[:, columns] + jnp.where(coded < 0, -size, size)
+        if (i + 1) * LANES % COLS == 0:
+            done = slice((i + 1) * LANES - COLS, (i + 1) * LANES)
+            there = out_ref.at[panel, :, first + done.start : first + done.stop]
+            copies.append(pltpu.make_async_copy(value_ref.at[:, done], there, sems.at[len(copies)]))
+            copies[-1].start()
+    for copy in copies:
+        copy.wait()
 
 
 def unpack(sums):
     count, width = sums[0][0].shape[0], sum(own.shape[1] for own, _ in sums) // 2
-    return pl.pallas_call(
-        unpack_kernel,
-        in_specs=[VMEM] * (2 * len(sums)),
-        out_specs=VMEM,
-        out_shape=jax.ShapeDtypeStruct((2, count, width), F32),
-        compiler_params=params(),
-        cost_estimate=COST,
-    )(*[array for pair in sums for array in pair])
+    hbm = pl.BlockSpec(memory_space=pltpu.HBM)
+    out, at = [], 0
+    for own, got in sums:
+        out = [
+            pl.pallas_call(
+                functools.partial(unpack_kernel, at // width, at % width),
+                in_specs=[VMEM] * 2 + [hbm] * len(out),
+                out_specs=hbm,
+                out_shape=jax.ShapeDtypeStruct((2, count, width), F32),
+                input_output_aliases={2: 0} if out else {},
+                scratch_shapes=[pltpu.VMEM(own.shape, F32), pltpu.SemaphoreType.DMA((own.shape[1] // COLS,))],
+                compiler_params=params(),
+                cost_estimate=COST,
+            )(own, got, *out)
+        ]
+        at += own.shape[1]
+    return out[0]
 
 
 def mult(left, right):
@@ -435,10 +449,12 @@
     halves_a[0] = after(keep, fb[3], bb[3]), got
     own, coded = pack(halves_a)
     sums = [(own, lax.ppermute(coded, "prow", SWAP_Y))]
-    for i in range(SPLITS):
-        keep, *sends = last(after(slots, coded), last_b, held, sum_b, columns[2], i * part, part, PIECES, False)
-        own, coded = pack([(after(keep, *([got for _, got in sums] if i else [])), across(sends))])
+    at = 0
+    for i, (wide, sends) in enumerate(((3 * width // 4, 2 * PIECES), (width // 4, PIECES))):
+        keep, *sends = last(after(slots, coded), last_b, held, sum_b, columns[2], at, wide, sends, False)
+        own, coded = pack([(after(keep, *([sums[0][1]] if i else [])), across(sends))])
         sums.append((own, lax.ppermute(coded, "prow", SWAP_Y)))
+        at += wide
     return unpack(sums)
 
 

time: 118 us -> 117 us (level)
  waiting for transfers between devices: 32 us -> 30.2 us
    ppermute x2, waiting for transfers between devices: 8.63 us -> 5.57 us  [fast(): sums.append((own, lax.ppermute(coded, 'prow', SWAP_Y)))]
    ppermute x16 -> x20, waiting for transfers between devices: 1.67 us -> 2.9 us  [across(): return [lax.ppermute(send, 'prow', SWAP_CORE) for send in sends]]
    pallas_call x1 -> x3, Pallas kernels: 2.01 us -> 2.88 us  [unpack(): pl.pallas_call(functools.partial(unpack_kernel, at // width, at % width),...]
    ppermute x16 -> x20, starting transfers between devices: 4.15 us -> 4.99 us  [across(): return [lax.ppermute(send, 'prow', SWAP_CORE) for send in sends]]
  transfers between devices with their start and end apart: 35 -> 39, of which waited for: 16 -> 22; matrix products, arithmetic and copies ran while one was open for 7% -> 7% of each run, Pallas kernels for 39% -> 42%
where the time goes in v5:
time: 117 us
  Pallas kernels  49.6 us (42%)
  waiting for transfers between devices  30.2 us (26%)
  starting transfers between devices  26.6 us (23%)
  matrix products  5.23 us (4%)
  other arithmetic  2.75 us (2%)
  local copies, waits for them, and re-layouts  2.36 us (2%)
    ppermute x8, waiting for transfers between devices, back(): return lax.ppermute(x, 'pcol', BACK)  16.7 us
    ppermute x8, starting transfers between devices, back(): return lax.ppermute(x, 'pcol', BACK)  15.3 us
    pallas_call x4, Pallas kernels, last(): pl.pallas_call(functools.partial(last_kernel, len(pieces), sends, at), in...  14.6 us
    pallas_call x1, Pallas kernels, first(): pl.pallas_call(functools.partial(first_kernel, len(pieces) // 2), in_spec...  11.2 us
    pallas_call x3, Pallas kernels, solve(): pl.pallas_call(functools.partial(solve_kernel, full), in_specs=[VMEM] * l...  10.5 us
    pallas_call x2, Pallas kernels, more(): pl.pallas_call(more_kernel, in_specs=[pl.BlockSpec(memory_space=pltpu.SME...  7.08 us
    ppermute x2, waiting for transfers between devices, fast(): sums.append((own, lax.ppermute(coded, 'prow', SWAP_Y)))  5.57 us
    ppermute x8, waiting for transfers between devices, ahead(): return lax.ppermute(x, 'pcol', AHEAD)  5.04 us
  transfers between devices with their start and end apart: 39, of which 22 were waited for; matrix products, arithmetic and copies ran while one was open for 7% of the time, Pallas kernels for 42%

profile of v5, /device:TPU:0, one launch (start us, length us, event | category | flops | bytes accessed | tf_op | source)
XLA Modules:
  0.0 117.1 jit_solution(6391435654197864999)
XLA Ops:
  0.0 1.4 %slice_bitcast_fusion.2 = (bf16[64,4096]{1,0:T(8,128)(2,1)S(1)}, bf16[64,4096]{1,0:T(8,128)(2,1)S(1)}) fusion(bf16[2,64,4096]{2,1,0:T(8,128)(2,1)} %param.7), kind=kLoop, calls=%fused_computation.22 | loop fusion | bytes 2097152 | tf_op jit(solution)/shard_map/squeeze | solution.py:394
  1.4 3.0 %collective-permute-start.2 = (bf16[64,4096]{1,0:T(8,128)(2,1)S(1)}, bf16[64,4096]{1,0:T(8,128)(2,1)}, u32[]{:S(2)}, u32[]{:S(2)}) collective-permute-start(bf16[64,4096]{1,0:T(8,128)(2,1)S(1)} %get-tuple-element.106.refs_0_), channel_id=1, source_target_pairs={{2,0},{4,2},{6,4},{7,6},{5,7},{3,5},{1,3},{0,1},{10,8},{12,10},{14... | collective-permute-start | bytes 1572872 | tf_op jit(solution)/shard_map/ppermute | solution.py:392
  4.5 1.9 %collective-permute-start.5 = (bf16[64,4096]{1,0:T(8,128)(2,1)S(1)}, bf16[64,4096]{1,0:T(8,128)(2,1)S(1)}, u32[]{:S(2)}, u32[]{:S(2)}) collective-permute-start(bf16[64,4096]{1,0:T(8,128)(2,1)S(1)} %get-tuple-element.105.refs_3_), channel_id=1, source_target_pairs={{2,0},{4,2},{6,4},{7,6},{5,7},{3,5},{1,3},{0,1},{10,8},{12,10},{14... | collective-permute-start | bytes 1572872 | tf_op jit(solution)/shard_map/ppermute | solution.py:392
  6.6 1.5 %reduce-precision_convert_fusion.2 = (bf16[512,512]{1,0:T(8,128)(2,1)S(1)}, bf16[512,512]{1,0:T(8,128)(2,1)S(1)}) fusion(f32[512,512]{1,0:T(8,128)} %param.10), kind=kLoop, calls=%fused_computation.5 | loop fusion | flops 1048576 | bytes 2097152 | tf_op jit(solution)/shard_map/convert.4
  8.1 1.8 %fusion.10 = f32[512,512]{1,0:T(8,128)S(1)} fusion(f32[512,512]{1,0:T(8,128)S(1)} %copy-done, f32[512,512]{1,0:T(8,128)S(1)} %copy-done.2), kind=kOutput, calls=%fused_computation.38 | convolution fusion | flops 1610612736 | bytes 3145728 | tf_op jit(solution)/shard_map/dot_general | solution.py:337
  10.1 1.9 %reduce-precision_convert_fusion.1 = (bf16[512,512]{1,0:T(8,128)(2,1)S(1)}, bf16[512,512]{1,0:T(8,128)(2,1)S(1)}) fusion(f32[512,512]{1,0:T(8,128)S(1)} %fusion.10, f32[512,512]{1,0:T(8,128)S(1)} %copy-done.3), kind=kOutput, calls=%fused_computation.3 | convolution fusion | flops 1611923456 | bytes 3145728 | tf_op jit(solution)/shard_map/dot_general | solution.py:337
  14.8 2.5 %collective-permute-done.2.refs_2_ = bf16[64,4096]{1,0:T(8,128)(2,1)} collective-permute-done((bf16[64,4096]{1,0:T(8,128)(2,1)S(1)}, bf16[64,4096]{1,0:T(8,128)(2,1)}, u32[]{:S(2)}, u32[]{:S(2)}) %collective-permute-start.2) | collective-permute-done | bytes 524320 | tf_op jit(solution)/shard_map/ppermute | solution.py:392
  17.3 2.0 %collective-permute-start.3 = (bf16[64,4096]{1,0:T(8,128)(2,1)}, bf16[64,4096]{1,0:T(8,128)(2,1)S(1)}, u32[]{:S(2)}, u32[]{:S(2)}) collective-permute-start(bf16[64,4096]{1,0:T(8,128)(2,1)} %collective-permute-done.2.refs_2_), channel_id=1, source_target_pairs={{2,0},{4,2},{6,4},{7,6},{5,7},{3,5},{1,3},{0,1},{10,8},{12,10},{14... | collective-permute-start | bytes 1572872 | tf_op jit(solution)/shard_map/ppermute | solution.py:392
  19.7 8.8 %collective-permute-done.5.refs_5_ = bf16[64,4096]{1,0:T(8,128)(2,1)S(1)} collective-permute-done((bf16[64,4096]{1,0:T(8,128)(2,1)S(1)}, bf16[64,4096]{1,0:T(8,128)(2,1)S(1)}, u32[]{:S(2)}, u32[]{:S(2)}) %collective-permute-start.5) | collective-permute-done | bytes 524320 | tf_op jit(solution)/shard_map/ppermute | solution.py:392
  28.4 2.0 %collective-permute-start.7 = (bf16[64,4096]{1,0:T(8,128)(2,1)S(1)}, bf16[64,4096]{1,0:T(8,128)(2,1)S(1)}, u32[]{:S(2)}, u32[]{:S(2)}) collective-permute-start(bf16[64,4096]{1,0:T(8,128)(2,1)S(1)} %collective-permute-done.5.refs_5_), channel_id=1, source_target_pairs={{2,0},{4,2},{6,4},{7,6},{5,7},{3,5},{1,3},{0,1},{10,8},{12,10},{14... | collective-permute-start | bytes 1572872 | tf_op jit(solution)/shard_map/ppermute | solution.py:392
  30.6 11.2 %shard_map.64 = (f32[512,2048]{1,0:T(8,128)S(1)}, f32[512,2048]{1,0:T(8,128)S(1)}, bf16[4096,2048]{1,0:T(8,128)(2,1)S(1)}) custom-call(s32[4]{0:T(128)S(1)} %get-tuple-element.54.starts_ref, bf16[64,4096]{1,0:T(8,128)(2,1)S(1)} %get-tuple-element.106.refs_0_, bf16[64,4096]{1,0:T(8,128)(2,1)} %collective-permute-done.refs_1_, ...), custom_call_target="tpu_custom_call" | custom-call | tf_op jit(solution)/shard_map/pallas_call | solution.py:103
  41.8 2.0 %collective-permute-start.9 = (bf16[64,4096]{1,0:T(8,128)(2,1)S(1)}, bf16[64,4096]{1,0:T(8,128)(2,1)S(1)}, u32[]{:S(2)}, u32[]{:S(2)}) collective-permute-start(bf16[64,4096]{1,0:T(8,128)(2,1)S(1)} %collective-permute-done.3.refs_1_), channel_id=1, source_target_pairs={{2,0},{4,2},{6,4},{7,6},{5,7},{3,5},{1,3},{0,1},{10,8},{12,10},{14... | collective-permute-start | bytes 1572872 | tf_op jit(solution)/shard_map/ppermute | solution.py:392
  44.1 3.5 %shard_map.65.rhs_ref = f32[512,2048]{1,0:T(8,128)S(1)} custom-call(s32[2]{0:T(128)S(1)} %pad_add_fusion.2.starts_ref, bf16[64,4096]{1,0:T(8,128)(2,1)S(1)} %collective-permute-done.1.refs_0_, bf16[64,4096]{1,0:T(8,128)(2,1)S(1)} %collective-permute-done.3.refs_1_, ...), custom_call_target="tpu_custom_call", output_to_operand_aliasing={{}: (4, {})} | custom-call | tf_op jit(solution)/shard_map/pallas_call | solution.py:127
  47.6 3.2 %shard_map.66.refs_5_ = f32[512,2048]{1,0:T(8,128)S(1)} custom-call(f32[512,2048]{1,0:T(8,128)S(1)} %shard_map.65.rhs_ref, bf16[1024,512]{1,0:T(8,128)(2,1)S(1)} %get-tuple-element.121.pair_ref), custom_call_target="tpu_custom_call" | custom-call | tf_op jit(solution)/shard_map/pallas_call | solution.py:165
  50.8 4.0 %shard_map.67.refs_0_ = f32[512,2048]{1,0:T(8,128)S(1)} custom-call(f32[512,2048]{1,0:T(8,128)S(1)} %shard_map.65.rhs_ref, bf16[1024,512]{1,0:T(8,128)(2,1)S(1)} %get-tuple-element.122.pair_ref), custom_call_target="tpu_custom_call" | custom-call | tf_op jit(solution)/shard_map/pallas_call | solution.py:165
  54.9 3.5 %shard_map.68.rhs_ref = f32[512,2048]{1,0:T(8,128)S(1)} custom-call(s32[2]{0:T(128)S(1)} %pad_add_fusion.2.starts_ref, bf16[64,4096]{1,0:T(8,128)(2,1)S(1)} %collective-permute-done.6.refs_0_, bf16[64,4096]{1,0:T(8,128)(2,1)S(1)} %collective-permute-done.7.refs_1_, ...), custom_call_target="tpu_custom_call", output_to_operand_aliasing={{}: (4, {})} | custom-call | tf_op jit(solution)/shard_map/pallas_call | solution.py:127
  58.4 2.9 %collective-permute-done.9.refs_1_ = bf16[64,4096]{1,0:T(8,128)(2,1)S(1)} collective-permute-done((bf16[64,4096]{1,0:T(8,128)(2,1)S(1)}, bf16[64,4096]{1,0:T(8,128)(2,1)S(1)}, u32[]{:S(2)}, u32[]{:S(2)}) %collective-permute-start.9) | collective-permute-done | bytes 524320 | tf_op jit(solution)/shard_map/ppermute | solution.py:392
  61.3 1.4 %collective-permute-done.8.refs_0_ = bf16[64,4096]{1,0:T(8,128)(2,1)S(1)} collective-permute-done((bf16[64,4096]{1,0:T(8,128)(2,1)S(1)}, bf16[64,4096]{1,0:T(8,128)(2,1)S(1)}, u32[]{:S(2)}, u32[]{:S(2)}) %collective-permute-start.8) | collective-permute-done | bytes 524320 | tf_op jit(solution)/shard_map/ppermute | solution.py:389
  62.8 1.6 %collective-permute-start.11 = (bf16[32,4096]{1,0:T(8,128)(2,1)S(1)}, bf16[32,4096]{1,0:T(8,128)(2,1)S(1)}, u32[]{:S(2)}, u32[]{:S(2)}) collective-permute-start(bf16[32,4096]{1,0:T(8,128)(2,1)S(1)} %slice.56), channel_id=1, source_target_pairs={{2,0},{4,2},{6,4},{7,6},{5,7},{3,5},{1,3},{0,1},{10,8},{12,10},{14... | collective-permute-start | bytes 786440 | tf_op jit(solution)/shard_map/ppermute | solution.py:392
  64.8 3.3 %shard_map.69.sum_ref = f32[512,2048]{1,0:T(8,128)S(1)} custom-call(f32[512,2048]{1,0:T(8,128)S(1)} %shard_map.68.rhs_ref, bf16[1024,512]{1,0:T(8,128)(2,1)S(1)} %pad_maximum_fusion.2.pair_ref, f32[512,2048]{1,0:T(8,128)S(1)} %shard_map.67.refs_0_), custom_call_target="tpu_custom_call", output_to_operand_aliasing={{}: (2, {})} | custom-call | tf_op jit(solution)/shard_map/pallas_call | solution.py:165
  68.1 1.6 %collective-permute-done.11.refs_3_ = bf16[32,4096]{1,0:T(8,128)(2,1)S(1)} collective-permute-done((bf16[32,4096]{1,0:T(8,128)(2,1)S(1)}, bf16[32,4096]{1,0:T(8,128)(2,1)S(1)}, u32[]{:S(2)}, u32[]{:S(2)}) %collective-permute-start.11) | collective-permute-done | bytes 262176 | tf_op jit(solution)/shard_map/ppermute | solution.py:392
  71.4 1.6 %collective-permute-start.13 = (bf16[64,4096]{1,0:T(8,128)(2,1)S(1)}, bf16[64,4096]{1,0:T(8,128)(2,1)S(1)}, u32[]{:S(2)}, u32[]{:S(2)}) collective-permute-start(bf16[64,4096]{1,0:T(8,128)(2,1)S(1)} %collective-permute-done.7.refs_1_), channel_id=1, source_target_pairs={{2,0},{4,2},{6,4},{7,6},{5,7},{3,5},{1,3},{0,1},{10,8},{12,10},{14... | collective-permute-start | bytes 1572872 | tf_op jit(solution)/shard_map/ppermute | solution.py:392
  73.0 3.7 %shard_map.71 = (f32[256,1024]{1,0:T(8,128)S(1)}, f32[64,1024]{1,0:T(8,128)S(1)}, f32[64,1024]{1,0:T(8,128)S(1)}, f32[64,1024]{1,0:T(8,128)S(1)}, f32[64,1024]{1,0:T(8,128)S(1)}, /*index=5*/bf16[576,1024]{1,0:T(8,128)(2,1)S(1)}) custom-call(s32[4]{0:T(128)S(1)} %get-tuple-element.92.starts_ref, bf16[64,4096]{1,0:T(8,128)(2,1)S(1)} %collective-permute-done.8.refs_0_, ...), custom_call_target="tpu_custom_call" | custom-call | tf_op jit(solution)/shard_map/pallas_call | solution.py:213
  77.3 3.7 %shard_map.70 = (f32[256,1024]{1,0:T(8,128)S(1)}, f32[64,1024]{1,0:T(8,128)S(1)}, f32[64,1024]{1,0:T(8,128)S(1)}, f32[64,1024]{1,0:T(8,128)S(1)}, f32[64,1024]{1,0:T(8,128)S(1)}, /*index=5*/bf16[576,1024]{1,0:T(8,128)(2,1)S(1)}) custom-call(s32[4]{0:T(128)S(1)} %get-tuple-element.92.starts_ref, bf16[64,4096]{1,0:T(8,128)(2,1)S(1)} %collective-permute-done.8.refs_0_, ...), custom_call_target="tpu_custom_call" | custom-call | tf_op jit(solution)/shard_map/pallas_call | solution.py:213
  83.6 1.3 %collective-permute-start.23 = (bf16[32,4096]{1,0:T(8,128)(2,1)S(1)}, bf16[32,4096]{1,0:T(8,128)(2,1)S(1)}, u32[]{:S(2)}, u32[]{:S(2)}) collective-permute-start(bf16[32,4096]{1,0:T(8,128)(2,1)S(1)} %slice.66), channel_id=1, source_target_pairs={{2,0},{4,2},{6,4},{7,6},{5,7},{3,5},{1,3},{0,1},{10,8},{12,10},{14... | collective-permute-start | bytes 786440 | tf_op jit(solution)/shard_map/ppermute | solution.py:392
  85.5 1.6 %collective-permute-start.32 = (bf16[2064,128]{1,0:T(8,128)(2,1)S(1)}, bf16[2064,128]{1,0:T(8,128)(2,1)S(1)}, u32[]{:S(2)}, u32[]{:S(2)}) collective-permute-start(bf16[2064,128]{1,0:T(8,128)(2,1)S(1)} %get-tuple-element.78), channel_id=1, source_target_pairs={{0,16},{8,24},{16,0},{24,8},{1,17},{9,25},{17,1},{25,9},{2,18},{10... | collective-permute-start | bytes 1585160 | tf_op jit(solution)/shard_map/ppermute | solution.py:451
  87.1 2.1 %shard_map.73.refs_5_ = f32[512,2048]{1,0:T(8,128)S(1)} custom-call(f32[512,2048]{1,0:T(8,128)S(1)} %shard_map.69.sum_ref, bf16[512,576]{1,0:T(8,128)(2,1)S(1)} %pad_maximum_fusion.4.matrix_ref, bf16[576,1024]{1,0:T(8,128)(2,1)S(1)} %get-tuple-element.80.refs_0_, bf16[576,1024]{1,0:T(8,128)(2,1)S(1)} %get-tuple-element.81.refs_1_), custom_call_target="tpu_custom_call", output_to_operand_aliasing={{}: (0, {})} | custom-call | tf_op jit(solution)/shard_map/pallas_call | solution.py:242
  89.2 2.0 %collective-permute-done.22.refs_2_ = bf16[32,4096]{1,0:T(8,128)(2,1)S(1)} collective-permute-done((bf16[32,4096]{1,0:T(8,128)(2,1)S(1)}, bf16[32,4096]{1,0:T(8,128)(2,1)S(1)}, u32[]{:S(2)}, u32[]{:S(2)}) %collective-permute-start.22) | collective-permute-done | bytes 262176 | tf_op jit(solution)/shard_map/ppermute | solution.py:389
  92.0 5.1 %shard_map.74 = (f32[256,1536]{1,0:T(8,128)S(1)}, f32[32,1536]{1,0:T(8,128)S(1)}, f32[32,1536]{1,0:T(8,128)S(1)}, f32[32,1536]{1,0:T(8,128)S(1)}, f32[32,1536]{1...) custom-call(s32[4]{0:T(128)S(1)} %get-tuple-element.92.starts_ref, ...), custom_call_target="tpu_custom_call" | custom-call | tf_op jit(solution)/shard_map/pallas_call | solution.py:213
  101.4 1.4 %collective-permute-start.38 = (bf16[1552,128]{1,0:T(8,128)(2,1)S(1)}, bf16[1552,128]{1,0:T(8,128)(2,1)S(1)}, u32[]{:S(2)}, u32[]{:S(2)}) collective-permute-start(bf16[1552,128]{1,0:T(8,128)(2,1)S(1)} %get-tuple-element.91), channel_id=1, source_target_pairs={{0,16},{8,24},{16,0},{24,8},{1,17},{9,25},{17,1},{25,9},{2,18},{10... | collective-permute-start | bytes 1191944 | tf_op jit(solution)/shard_map/ppermute | solution.py:456
  102.9 2.2 %shard_map.76 = (f32[256,512]{1,0:T(8,128)S(1)}, f32[64,512]{1,0:T(8,128)S(1)}, f32[64,512]{1,0:T(8,128)S(1)}, f32[64,512]{1,0:T(8,128)S(1)}, f32[64,512]{1,0:T(8,128)S(1)}) custom-call(s32[4]{0:T(128)S(1)} %get-tuple-element.92.starts_ref, bf16[64,4096]{1,0:T(8,128)(2,1)S(1)} %collective-permute-done.12.refs_0_, ...), custom_call_target="tpu_custom_call" | custom-call | tf_op jit(solution)/shard_map/pallas_call | solution.py:213
  109.2 4.4 %collective-permute-done.38.got_ref = bf16[1552,128]{1,0:T(8,128)(2,1)S(1)} collective-permute-done((bf16[1552,128]{1,0:T(8,128)(2,1)S(1)}, bf16[1552,128]{1,0:T(8,128)(2,1)S(1)}, u32[]{:S(2)}, u32[]{:S(2)}) %collective-permute-start.38) | collective-permute-done | bytes 397344 | tf_op jit(solution)/shard_map/ppermute | solution.py:456
  (99 shorter events, 22.9 us)
Async XLA Ops:
  1.4 15.9 %collective-permute-start.2 = (bf16[64,4096]{1,0:T(8,128)(2,1)S(1)}, bf16[64,4096]{1,0:T(8,128)(2,1)}, u32[]{:S(2)}, u32[]{:S(2)}) collective-permute-start(bf16[64,4096]{1,0:T(8,128)(2,1)S(1)} %get-tuple-element.106.refs_0_), channel_id=1, source_target_pairs={{2,0},{4,2},{6,4},{7,6},{5,7},{3,5},{1,3},{0,1},{10,8},{12,10},{14... | collective-permute-start | bytes 1572872 | tf_op jit(solution)/shard_map/ppermute | solution.py:392
  4.4 15.0 %collective-permute-start = (bf16[64,4096]{1,0:T(8,128)(2,1)S(1)}, bf16[64,4096]{1,0:T(8,128)(2,1)}, u32[]{:S(2)}, u32[]{:S(2)}) collective-permute-start(bf16[64,4096]{1,0:T(8,128)(2,1)S(1)} %get-tuple-element.106.refs_0_), channel_id=1, source_target_pairs={{0,2},{2,4},{4,6},{6,7},{7,5},{5,3},{3,1},{1,0},{8,10},{10,12},{12... | collective-permute-start | bytes 1572872 | tf_op jit(solution)/shard_map/ppermute | solution.py:389
  4.5 23.9 %collective-permute-start.5 = (bf16[64,4096]{1,0:T(8,128)(2,1)S(1)}, bf16[64,4096]{1,0:T(8,128)(2,1)S(1)}, u32[]{:S(2)}, u32[]{:S(2)}) collective-permute-start(bf16[64,4096]{1,0:T(8,128)(2,1)S(1)} %get-tuple-element.105.refs_3_), channel_id=1, source_target_pairs={{2,0},{4,2},{6,4},{7,6},{5,7},{3,5},{1,3},{0,1},{10,8},{12,10},{14... | collective-permute-start | bytes 1572872 | tf_op jit(solution)/shard_map/ppermute | solution.py:392
  6.4 24.1 %collective-permute-start.4 = (bf16[64,4096]{1,0:T(8,128)(2,1)S(1)}, bf16[64,4096]{1,0:T(8,128)(2,1)S(1)}, u32[]{:S(2)}, u32[]{:S(2)}) collective-permute-start(bf16[64,4096]{1,0:T(8,128)(2,1)S(1)} %get-tuple-element.105.refs_3_), channel_id=1, source_target_pairs={{0,2},{2,4},{4,6},{6,7},{7,5},{5,3},{3,1},{1,0},{8,10},{10,12},{12... | collective-permute-start | bytes 1572872 | tf_op jit(solution)/shard_map/ppermute | solution.py:389
  17.3 24.4 %collective-permute-start.3 = (bf16[64,4096]{1,0:T(8,128)(2,1)}, bf16[64,4096]{1,0:T(8,128)(2,1)S(1)}, u32[]{:S(2)}, u32[]{:S(2)}) collective-permute-start(bf16[64,4096]{1,0:T(8,128)(2,1)} %collective-permute-done.2.refs_2_), channel_id=1, source_target_pairs={{2,0},{4,2},{6,4},{7,6},{5,7},{3,5},{1,3},{0,1},{10,8},{12,10},{14... | collective-permute-start | bytes 1572872 | tf_op jit(solution)/shard_map/ppermute | solution.py:392
  19.3 24.4 %collective-permute-start.1 = (bf16[64,4096]{1,0:T(8,128)(2,1)}, bf16[64,4096]{1,0:T(8,128)(2,1)S(1)}, u32[]{:S(2)}, u32[]{:S(2)}) collective-permute-start(bf16[64,4096]{1,0:T(8,128)(2,1)} %collective-permute-done.refs_1_), channel_id=1, source_target_pairs={{0,2},{2,4},{4,6},{6,7},{7,5},{5,3},{3,1},{1,0},{8,10},{10,12},{12... | collective-permute-start | bytes 1572872 | tf_op jit(solution)/shard_map/ppermute | solution.py:389
  28.4 26.4 %collective-permute-start.7 = (bf16[64,4096]{1,0:T(8,128)(2,1)S(1)}, bf16[64,4096]{1,0:T(8,128)(2,1)S(1)}, u32[]{:S(2)}, u32[]{:S(2)}) collective-permute-start(bf16[64,4096]{1,0:T(8,128)(2,1)S(1)} %collective-permute-done.5.refs_5_), channel_id=1, source_target_pairs={{2,0},{4,2},{6,4},{7,6},{5,7},{3,5},{1,3},{0,1},{10,8},{12,10},{14... | collective-permute-start | bytes 1572872 | tf_op jit(solution)/shard_map/ppermute | solution.py:392
  30.5 24.4 %collective-permute-start.6 = (bf16[64,4096]{1,0:T(8,128)(2,1)S(1)}, bf16[64,4096]{1,0:T(8,128)(2,1)S(1)}, u32[]{:S(2)}, u32[]{:S(2)}) collective-permute-start(bf16[64,4096]{1,0:T(8,128)(2,1)S(1)} %collective-permute-done.4.refs_4_), channel_id=1, source_target_pairs={{0,2},{2,4},{4,6},{6,7},{7,5},{5,3},{3,1},{1,0},{8,10},{10,12},{12... | collective-permute-start | bytes 1572872 | tf_op jit(solution)/shard_map/ppermute | solution.py:389
  41.8 19.6 %collective-permute-start.9 = (bf16[64,4096]{1,0:T(8,128)(2,1)S(1)}, bf16[64,4096]{1,0:T(8,128)(2,1)S(1)}, u32[]{:S(2)}, u32[]{:S(2)}) collective-permute-start(bf16[64,4096]{1,0:T(8,128)(2,1)S(1)} %collective-permute-done.3.refs_1_), channel_id=1, source_target_pairs={{2,0},{4,2},{6,4},{7,6},{5,7},{3,5},{1,3},{0,1},{10,8},{12,10},{14... | collective-permute-start | bytes 1572872 | tf_op jit(solution)/shard_map/ppermute | solution.py:392
  43.7 19.0 %collective-permute-start.8 = (bf16[64,4096]{1,0:T(8,128)(2,1)S(1)}, bf16[64,4096]{1,0:T(8,128)(2,1)S(1)}, u32[]{:S(2)}, u32[]{:S(2)}) collective-permute-start(bf16[64,4096]{1,0:T(8,128)(2,1)S(1)} %collective-permute-done.1.refs_0_), channel_id=1, source_target_pairs={{0,2},{2,4},{4,6},{6,7},{7,5},{5,3},{3,1},{1,0},{8,10},{10,12},{12... | collective-permute-start | bytes 1572872 | tf_op jit(solution)/shard_map/ppermute | solution.py:389
  62.8 6.9 %collective-permute-start.11 = (bf16[32,4096]{1,0:T(8,128)(2,1)S(1)}, bf16[32,4096]{1,0:T(8,128)(2,1)S(1)}, u32[]{:S(2)}, u32[]{:S(2)}) collective-permute-start(bf16[32,4096]{1,0:T(8,128)(2,1)S(1)} %slice.56), channel_id=1, source_target_pairs={{2,0},{4,2},{6,4},{7,6},{5,7},{3,5},{1,3},{0,1},{10,8},{12,10},{14... | collective-permute-start | bytes 786440 | tf_op jit(solution)/shard_map/ppermute | solution.py:392
  64.4 6.6 %collective-permute-start.10 = (bf16[32,4096]{1,0:T(8,128)(2,1)S(1)}, bf16[32,4096]{1,0:T(8,128)(2,1)S(1)}, u32[]{:S(2)}, u32[]{:S(2)}) collective-permute-start(bf16[32,4096]{1,0:T(8,128)(2,1)S(1)} %slice.55), channel_id=1, source_target_pairs={{0,2},{2,4},{4,6},{6,7},{7,5},{5,3},{3,1},{1,0},{8,10},{10,12},{12... | collective-permute-start | bytes 786440 | tf_op jit(solution)/shard_map/ppermute | solution.py:389
  71.0 11.3 %collective-permute-start.12 = (bf16[64,4096]{1,0:T(8,128)(2,1)S(1)}, bf16[64,4096]{1,0:T(8,128)(2,1)S(1)}, u32[]{:S(2)}, u32[]{:S(2)}) collective-permute-start(bf16[64,4096]{1,0:T(8,128)(2,1)S(1)} %collective-permute-done.6.refs_0_), channel_id=1, source_target_pairs={{0,2},{2,4},{4,6},{6,7},{7,5},{5,3},{3,1},{1,0},{8,10},{10,12},{12... | collective-permute-start | bytes 1572872 | tf_op jit(solution)/shard_map/ppermute | solution.py:389
  71.4 11.0 %collective-permute-start.13 = (bf16[64,4096]{1,0:T(8,128)(2,1)S(1)}, bf16[64,4096]{1,0:T(8,128)(2,1)S(1)}, u32[]{:S(2)}, u32[]{:S(2)}) collective-permute-start(bf16[64,4096]{1,0:T(8,128)(2,1)S(1)} %collective-permute-done.7.refs_1_), channel_id=1, source_target_pairs={{2,0},{4,2},{6,4},{7,6},{5,7},{3,5},{1,3},{0,1},{10,8},{12,10},{14... | collective-permute-start | bytes 1572872 | tf_op jit(solution)/shard_map/ppermute | solution.py:392
  76.6 4.3 %collective-permute-start.18 = (f32[64,1024]{1,0:T(8,128)S(1)}, f32[64,1024]{1,0:T(8,128)S(1)}, u32[]{:S(2)}, u32[]{:S(2)}) collective-permute-start(f32[64,1024]{1,0:T(8,128)S(1)} %get-tuple-element.74), channel_id=1, source_target_pairs={{0,8},{8,0},{16,24},{24,16},{1,9},{9,1},{17,25},{25,17},{2,10},{10... | collective-permute-start | bytes 786440 | tf_op jit(solution)/shard_map/ppermute | solution.py:438
  76.7 4.7 %collective-permute-start.19 = (f32[64,1024]{1,0:T(8,128)S(1)}, f32[64,1024]{1,0:T(8,128)S(1)}, u32[]{:S(2)}, u32[]{:S(2)}) collective-permute-start(f32[64,1024]{1,0:T(8,128)S(1)} %get-tuple-element.75), channel_id=1, source_target_pairs={{0,8},{8,0},{16,24},{24,16},{1,9},{9,1},{17,25},{25,17},{2,10},{10... | collective-permute-start | bytes 786440 | tf_op jit(solution)/shard_map/ppermute | solution.py:438
  77.2 4.3 %collective-permute-start.20 = (f32[64,1024]{1,0:T(8,128)S(1)}, f32[64,1024]{1,0:T(8,128)S(1)}, u32[]{:S(2)}, u32[]{:S(2)}) collective-permute-start(f32[64,1024]{1,0:T(8,128)S(1)} %get-tuple-element.76), channel_id=1, source_target_pairs={{0,8},{8,0},{16,24},{24,16},{1,9},{9,1},{17,25},{25,17},{2,10},{10... | collective-permute-start | bytes 786440 | tf_op jit(solution)/shard_map/ppermute | solution.py:438
  81.0 1.8 %collective-permute-start.21 = (f32[64,1024]{1,0:T(8,128)S(1)}, f32[64,1024]{1,0:T(8,128)S(1)}, u32[]{:S(2)}, u32[]{:S(2)}) collective-permute-start(f32[64,1024]{1,0:T(8,128)S(1)} %get-tuple-element.77), channel_id=1, source_target_pairs={{0,8},{8,0},{16,24},{24,16},{1,9},{9,1},{17,25},{25,17},{2,10},{10... | collective-permute-start | bytes 786440 | tf_op jit(solution)/shard_map/ppermute | solution.py:438
  81.5 2.1 %collective-permute-start.14 = (f32[64,1024]{1,0:T(8,128)S(1)}, f32[64,1024]{1,0:T(8,128)S(1)}, u32[]{:S(2)}, u32[]{:S(2)}) collective-permute-start(f32[64,1024]{1,0:T(8,128)S(1)} %get-tuple-element.69), channel_id=1, source_target_pairs={{0,8},{8,0},{16,24},{24,16},{1,9},{9,1},{17,25},{25,17},{2,10},{10... | collective-permute-start | bytes 786440 | tf_op jit(solution)/shard_map/ppermute | solution.py:438
  81.6 3.3 %collective-permute-start.15 = (f32[64,1024]{1,0:T(8,128)S(1)}, f32[64,1024]{1,0:T(8,128)S(1)}, u32[]{:S(2)}, u32[]{:S(2)}) collective-permute-start(f32[64,1024]{1,0:T(8,128)S(1)} %get-tuple-element.70), channel_id=1, source_target_pairs={{0,8},{8,0},{16,24},{24,16},{1,9},{9,1},{17,25},{25,17},{2,10},{10... | collective-permute-start | bytes 786440 | tf_op jit(solution)/shard_map/ppermute | solution.py:438
  82.2 2.7 %collective-permute-start.16 = (f32[64,1024]{1,0:T(8,128)S(1)}, f32[64,1024]{1,0:T(8,128)S(1)}, u32[]{:S(2)}, u32[]{:S(2)}) collective-permute-start(f32[64,1024]{1,0:T(8,128)S(1)} %get-tuple-element.71), channel_id=1, source_target_pairs={{0,8},{8,0},{16,24},{24,16},{1,9},{9,1},{17,25},{25,17},{2,10},{10... | collective-permute-start | bytes 786440 | tf_op jit(solution)/shard_map/ppermute | solution.py:438
  82.4 2.5 %collective-permute-start.17 = (f32[64,1024]{1,0:T(8,128)S(1)}, f32[64,1024]{1,0:T(8,128)S(1)}, u32[]{:S(2)}, u32[]{:S(2)}) collective-permute-start(f32[64,1024]{1,0:T(8,128)S(1)} %get-tuple-element.72), channel_id=1, source_target_pairs={{0,8},{8,0},{16,24},{24,16},{1,9},{9,1},{17,25},{25,17},{2,10},{10... | collective-permute-start | bytes 786440 | tf_op jit(solution)/shard_map/ppermute | solution.py:438
  82.8 8.4 %collective-permute-start.22 = (bf16[32,4096]{1,0:T(8,128)(2,1)S(1)}, bf16[32,4096]{1,0:T(8,128)(2,1)S(1)}, u32[]{:S(2)}, u32[]{:S(2)}) collective-permute-start(bf16[32,4096]{1,0:T(8,128)(2,1)S(1)} %slice.65), channel_id=1, source_target_pairs={{0,2},{2,4},{4,6},{6,7},{7,5},{5,3},{3,1},{1,0},{8,10},{10,12},{12... | collective-permute-start | bytes 786440 | tf_op jit(solution)/shard_map/ppermute | solution.py:389
  83.6 8.4 %collective-permute-start.23 = (bf16[32,4096]{1,0:T(8,128)(2,1)S(1)}, bf16[32,4096]{1,0:T(8,128)(2,1)S(1)}, u32[]{:S(2)}, u32[]{:S(2)}) collective-permute-start(bf16[32,4096]{1,0:T(8,128)(2,1)S(1)} %slice.66), channel_id=1, source_target_pairs={{2,0},{4,2},{6,4},{7,6},{5,7},{3,5},{1,3},{0,1},{10,8},{12,10},{14... | collective-permute-start | bytes 786440 | tf_op jit(solution)/shard_map/ppermute | solution.py:392
  85.5 20.2 %collective-permute-start.32 = (bf16[2064,128]{1,0:T(8,128)(2,1)S(1)}, bf16[2064,128]{1,0:T(8,128)(2,1)S(1)}, u32[]{:S(2)}, u32[]{:S(2)}) collective-permute-start(bf16[2064,128]{1,0:T(8,128)(2,1)S(1)} %get-tuple-element.78), channel_id=1, source_target_pairs={{0,16},{8,24},{16,0},{24,8},{1,17},{9,25},{17,1},{25,9},{2,18},{10... | collective-permute-start | bytes 1585160 | tf_op jit(solution)/shard_map/ppermute | solution.py:451
  97.2 1.5 %collective-permute-start.24 = (f32[32,1536]{1,0:T(8,128)S(1)}, f32[32,1536]{1,0:T(8,128)S(1)}, u32[]{:S(2)}, u32[]{:S(2)}) collective-permute-start(f32[32,1536]{1,0:T(8,128)S(1)} %get-tuple-element.83), channel_id=1, source_target_pairs={{0,8},{8,0},{16,24},{24,16},{1,9},{9,1},{17,25},{25,17},{2,10},{10... | collective-permute-start | bytes 589832 | tf_op jit(solution)/shard_map/ppermute | solution.py:438
  97.2 1.7 %collective-permute-start.25 = (f32[32,1536]{1,0:T(8,128)S(1)}, f32[32,1536]{1,0:T(8,128)S(1)}, u32[]{:S(2)}, u32[]{:S(2)}) collective-permute-start(f32[32,1536]{1,0:T(8,128)S(1)} %get-tuple-element.84), channel_id=1, source_target_pairs={{0,8},{8,0},{16,24},{24,16},{1,9},{9,1},{17,25},{25,17},{2,10},{10... | collective-permute-start | bytes 589832 | tf_op jit(solution)/shard_map/ppermute | solution.py:438
  97.7 1.5 %collective-permute-start.26 = (f32[32,1536]{1,0:T(8,128)S(1)}, f32[32,1536]{1,0:T(8,128)S(1)}, u32[]{:S(2)}, u32[]{:S(2)}) collective-permute-start(f32[32,1536]{1,0:T(8,128)S(1)} %get-tuple-element.85), channel_id=1, source_target_pairs={{0,8},{8,0},{16,24},{24,16},{1,9},{9,1},{17,25},{25,17},{2,10},{10... | collective-permute-start | bytes 589832 | tf_op jit(solution)/shard_map/ppermute | solution.py:438
  97.8 1.7 %collective-permute-start.27 = (f32[32,1536]{1,0:T(8,128)S(1)}, f32[32,1536]{1,0:T(8,128)S(1)}, u32[]{:S(2)}, u32[]{:S(2)}) collective-permute-start(f32[32,1536]{1,0:T(8,128)S(1)} %get-tuple-element.86), channel_id=1, source_target_pairs={{0,8},{8,0},{16,24},{24,16},{1,9},{9,1},{17,25},{25,17},{2,10},{10... | collective-permute-start | bytes 589832 | tf_op jit(solution)/shard_map/ppermute | solution.py:438
  101.4 12.1 %collective-permute-start.38 = (bf16[1552,128]{1,0:T(8,128)(2,1)S(1)}, bf16[1552,128]{1,0:T(8,128)(2,1)S(1)}, u32[]{:S(2)}, u32[]{:S(2)}) collective-permute-start(bf16[1552,128]{1,0:T(8,128)(2,1)S(1)} %get-tuple-element.91), channel_id=1, source_target_pairs={{0,16},{8,24},{16,0},{24,8},{1,17},{9,25},{17,1},{25,9},{2,18},{10... | collective-permute-start | bytes 1191944 | tf_op jit(solution)/shard_map/ppermute | solution.py:456
  105.2 1.5 %collective-permute-start.34 = (f32[64,512]{1,0:T(8,128)S(1)}, f32[64,512]{1,0:T(8,128)S(1)}, u32[]{:S(2)}, u32[]{:S(2)}) collective-permute-start(f32[64,512]{1,0:T(8,128)S(1)} %get-tuple-element.96), channel_id=1, source_target_pairs={{0,8},{8,0},{16,24},{24,16},{1,9},{9,1},{17,25},{25,17},{2,10},{10... | collective-permute-start | bytes 393224 | tf_op jit(solution)/shard_map/ppermute | solution.py:438
  107.4 8.4 %collective-permute-start.37 = (bf16[528,128]{1,0:T(8,128)(2,1)S(1)}, bf16[528,128]{1,0:T(8,128)(2,1)S(1)}, u32[]{:S(2)}, u32[]{:S(2)}) collective-permute-start(bf16[528,128]{1,0:T(8,128)(2,1)S(1)} %get-tuple-element.100), channel_id=1, source_target_pairs={{0,16},{8,24},{16,0},{24,8},{1,17},{9,25},{17,1},{25,9},{2,18},{10... | collective-permute-start | bytes 405512 | tf_op jit(solution)/shard_map/ppermute | solution.py:456
  (12 other events, 27.5 us)
